TPU v7x, 32 devices: a whole 2x2x4 slice. The times are simulated.
32 devices in a mesh: tile: 8 (over z, x), ens: 4 (over y, core).
Axes of the slice: x: 2, y: 2, z: 4, core: 2. Of those that a mesh axis runs over, the one named last changes fastest.
Arguments:
- initial_sample_set: float32 [80, 2, 32, 2048], P('ens', None, 'tile'), may hold values from -6 to 6
- flow_velocity: float32 [2, 2, 32, 2048], P(None, None, 'tile'), may hold values from -0.4 to 0.4
- obs_loc: int32 [3, 2, 8192], P(None, None, 'tile'), may hold values from 0 to 2047, as said below
- obs_count: int32 [2, 8], P(None, 'tile'), may hold values from 256 to 1024, as said below
- obs_value: float32 [2, 8192], P(None, 'tile'), may hold values from -6 to 6
- obs_error: float32 [2, 8192], P(None, 'tile'), may hold values from 0.25 to 2
Outputs:
- analysis: float32 [80, 2, 32, 2048], P('ens', None, 'tile')
Inputs may be any that keep to these rules, and one draw needn't show every extreme that they name: `obs_loc`: slots 1024 * t to 1024 * (t + 1) - 1 of a batch belong to tile t: their row lies in rows 4 * t to 4 * (t + 1) - 1; columns lie in 0 to 2047 and levels in 0 to 1. `obs_count`: in every batch some tile has exactly 1024 live observations; a tile's live observations are its first slots.
All inputs are finite; a program needn't handle non-finite values.
Results may differ from a plain program's by a relative error of at most 0.0003.
Values sent between devices are 32-bit elements; how exact they have to be, the bound alone decides.
No kernel may reach another device: no remote copies, remote signals or barrier semaphores. Data moves between devices by JAX's collectives and lax.ppermute only.
A program may use at most 128 MiB of HBM per device.

v0:
```python
import functools

import jax
import jax.numpy as jnp
from jax import lax
from jax.experimental import pallas as pl
from jax.experimental.pallas import tpu as pltpu
from jax.sharding import PartitionSpec as P

BATCHES = 2
REACH = 2
SPARE = 4
SPREAD_RATE = 0.05
EPSILON = 1e-06
LANE = 128
DEEP = 256
BLOCK = 512
F32 = jnp.float32
BF16 = jnp.bfloat16
VMEM = pl.BlockSpec(memory_space=pltpu.VMEM)
SMEM = pl.BlockSpec(memory_space=pltpu.SMEM)
PARAMS = pltpu.CompilerParams(vmem_limit_bytes=48 << 20)


def split(value):
    high = value.astype(BF16)
    return high, (value - high.astype(F32)).astype(BF16)


def order_kernel(rows, id_ref, loc_ref, value_ref, error_ref, count_ref, att_ref):
    batches, slots = value_ref.shape
    earlier = (
        lax.broadcasted_iota(jnp.int32, (slots, slots), 0)
        < lax.broadcasted_iota(jnp.int32, (slots, slots), 1)
    ).astype(BF16)
    slot = lax.broadcasted_iota(jnp.int32, (1, slots), 1)
    key_of = lax.broadcasted_iota(jnp.int32, (8, slots), 0)
    for b in range(batches):
        count = count_ref[b, 0]
        local_row = loc_ref[0, b : b + 1, :] - id_ref[0] * rows
        key = jnp.where(slot < count, local_row, rows)
        mine = key_of == jnp.broadcast_to(key, (8, slots))
        ones = mine.astype(F32)
        before = jnp.dot(ones.astype(BF16), earlier, preferred_element_type=F32)
        totals = jnp.sum(ones, axis=1, keepdims=True)
        start = jnp.zeros((1, slots), F32)
        place = jnp.zeros((1, slots), F32)
        cumulative = jnp.where(slot == 0, count.astype(F32), 0.0)
        for r in range(rows + 1):
            place = place + ones[r : r + 1] * (before[r : r + 1] + start)
            start = start + totals[r : r + 1]
            cumulative = jnp.where(slot == r + 1, start, cumulative)
        level = loc_ref[2, b : b + 1, :]
        fields = [
            loc_ref[0, b : b + 1, :].astype(F32),
            loc_ref[1, b : b + 1, :].astype(F32),
            level.astype(F32),
            value_ref[b : b + 1, :],
            error_ref[b : b + 1, :],
            (level * rows + local_row).astype(F32),
        ]
        table = jnp.concatenate(fields + [jnp.zeros((2, slots), F32)], axis=0)
        high, low = split(table)
        rest = (table - high.astype(F32) - low.astype(F32)).astype(BF16)
        target = lax.broadcasted_iota(jnp.int32, (slots, slots), 0)
        moved = (target == jnp.broadcast_to(place.astype(jnp.int32), (slots, slots))).astype(BF16)
        out = lax.dot_general(
            jnp.concatenate([high.astype(F32), low.astype(F32), rest.astype(F32)], axis=0).astype(BF16),
            moved,
            (((1,), (1,)), ((), ())),
            preferred_element_type=F32,
        )
        out = (out[0:8] + out[8:16]) + out[16:24]
        att_ref[b] = jnp.concatenate([out[0:5], cumulative, out[5:6], jnp.zeros((1, slots), F32)], axis=0)


def order(ids, obs_loc, obs_value, obs_error, obs_count, rows):
    batches, slots = obs_value.shape
    return pl.pallas_call(
        functools.partial(order_kernel, rows),
        out_shape=jax.ShapeDtypeStruct((batches, 8, slots), F32),
        in_specs=[SMEM, VMEM, VMEM, VMEM, SMEM],
        out_specs=VMEM,
        compiler_params=PARAMS,
        name="order",
    )(ids, obs_loc, obs_value, obs_error, obs_count)


def forecast_kernel(id_ref, x_ref, top_ref, bottom_ref, flow_ref, *refs):
    outs, row_ref = refs[:-1], refs[-1]
    members, levels, rows, cols = x_ref.shape
    height = levels * rows
    parts, bands = len(outs), outs[0].shape[0]
    row = lax.broadcasted_iota(jnp.int32, (height, cols), 0)
    col = lax.broadcasted_iota(jnp.int32, (height, cols), 1)
    winds = [
        jnp.concatenate([flow_ref[d, l] for l in range(levels)], axis=0) for d in range(2)
    ]

    def body(m, _):
        x = jnp.concatenate([x_ref[m, l] for l in range(levels)], axis=0)
        above = pltpu.roll(x, 1, 0)
        below = pltpu.roll(x, height - 1, 0)
        for l in range(levels):
            above = jnp.where(row == l * rows, top_ref[m, l : l + 1, :], above)
            below = jnp.where(row == (l + 1) * rows - 1, bottom_ref[m, l : l + 1, :], below)
        left = jnp.where(col == 0, 0.0, pltpu.roll(x, 1, 1))
        right = jnp.where(col == cols - 1, 0.0, pltpu.roll(x, cols - 1, 1))
        tendency = (
            jnp.maximum(winds[0], 0.0) * (x - above)
            + jnp.minimum(winds[0], 0.0) * (below - x)
            + jnp.maximum(winds[1], 0.0) * (x - left)
            + jnp.minimum(winds[1], 0.0) * (right - x)
        )
        row_ref[...] = x - tendency + SPREAD_RATE * (above + below + left + right - 4.0 * x)
        at = pl.multiple_of(m * height, height)
        for k in range(parts):
            first = (id_ref[1] ^ k) * (bands * LANE)
            for band in range(bands):
                source = pl.multiple_of(first + band * LANE, LANE)
                outs[k][band, pl.ds(at, height), :] = row_ref[:, pl.ds(source, LANE)]
        return 0

    lax.fori_loop(0, members, body, 0)


def forecast(ids, x, top, bottom, flow, parts):
    members, levels, rows, cols = x.shape
    out = jax.ShapeDtypeStruct((cols // parts // LANE, members * levels * rows, LANE), F32)
    return pl.pallas_call(
        forecast_kernel,
        out_shape=[out] * parts,
        in_specs=[SMEM] + [VMEM] * 4,
        out_specs=[VMEM] * parts,
        scratch_shapes=[pltpu.VMEM((levels * rows, cols), F32)],
        compiler_params=PARAMS,
        name="forecast",
    )(ids, x, top, bottom, flow)


def fill_spare(put, att, odd):
    even_rows = jnp.concatenate([att[0:3], att[5:6]], axis=0)
    odd_rows = jnp.concatenate([att[3:5], att[3:5]], axis=0)
    put(jnp.where(odd, odd_rows, even_rows))


def observe_kernel(height, share, id_ref, att_ref, *refs):
    parts, out_ref = refs[:-1], refs[-1]
    bands = parts[0].shape[0]
    batches, _, slots = att_ref.shape
    row = lax.broadcasted_iota(jnp.int32, (height, LANE), 0)
    for b in range(batches):
        att = att_ref[b]
        odd = (id_ref[1] & 1) == 1

        def put(rows, b=b):
            out_ref[b, share : share + SPARE, :] = rows

        fill_spare(put, att, odd)

        def body(n, _, b=b):
            at = pl.multiple_of(n * LANE, LANE)
            column = att_ref[b, 1:2, pl.ds(at, LANE)].astype(jnp.int32)
            flat_row = att_ref[b, 6:7, pl.ds(at, LANE)].astype(jnp.int32)
            band_of = jnp.broadcast_to(column // LANE, (height, LANE))
            lane_of = jnp.broadcast_to(column % LANE, (height, LANE))
            mine = jnp.broadcast_to(flat_row, (height, LANE)) == row
            here = [
                band_of == (id_ref[1] ^ k) * bands + band
                for k in range(len(parts))
                for band in range(bands)
            ]
            for m in range(share):
                found = jnp.zeros((height, LANE), F32)
                for i in range(len(parts) * bands):
                    block = parts[i // bands][i % bands, m * height : (m + 1) * height, :]
                    picked = jnp.take_along_axis(block, lane_of, axis=1)
                    found = jnp.where(here[i], picked, found)
                value = jnp.sum(jnp.where(mine, found, 0.0), axis=0, keepdims=True)
                out_ref[b, m : m + 1, pl.ds(at, LANE)] = value
            return 0

        lax.fori_loop(0, slots // LANE, body, 0)


def observe(ids, att, parts, height, share):
    batches, _, slots = att.shape
    padded = (share + SPARE + 7) // 8 * 8
    return pl.pallas_call(
        functools.partial(observe_kernel, height, share),
        out_shape=jax.ShapeDtypeStruct((batches, padded, slots), F32),
        in_specs=[SMEM] + [VMEM] * (1 + len(parts)),
        out_specs=VMEM,
        compiler_params=PARAMS,
        name="observe",
    )(ids, att, *parts)


def weigh(prior, value, error, live):
    members = prior.shape[0]
    average = jnp.sum(prior, axis=0, keepdims=True) / members
    deviation = prior - average
    var_prior = jnp.sum(deviation * deviation, axis=0, keepdims=True) / (members - 1) + EPSILON
    combined = var_prior + error
    shrink = jnp.sqrt(error / combined)
    post = (error * average + var_prior * value) / combined
    shift = live * ((shrink - 1.0) * deviation + (post - average))
    weight = (live / ((members - 1) * var_prior)) * deviation
    return weight, shift


def pack(geometry, id_ref, flip, priors, w_ref, s_ref, rc_ref):
    levels, rows, share, row_scale, col_scale = geometry
    halves, groups, _, width = priors[0].shape
    chunk = min(2 * LANE, width)
    lane = lax.broadcasted_iota(jnp.int32, (1, LANE), 1)
    counts = [ref[0, 0, share + 3 : share + 4, 0:LANE] for ref in priors]

    def number(t, at):
        return jnp.sum(jnp.where(lane == at, counts[t], 0.0)).astype(jnp.int32)

    off = jnp.int32(0)
    starts = []
    for t, ref in enumerate(priors):
        count = number(t, 0)
        starts.append(off)

        def body(k, _, ref=ref, off=off, count=count):
            src = k * chunk
            half = (src // width) ^ (id_ref[1] & (halves - 1))
            at = pl.multiple_of(src % width, chunk)
            dst = pl.multiple_of(off + src, LANE)
            slot = lax.broadcasted_iota(jnp.int32, (1, chunk), 1) + src
            live = (slot < count).astype(F32)
            prior = jnp.concatenate(
                [ref[half, flip ^ g, 0:share, pl.ds(at, chunk)] for g in range(groups)], axis=0
            )
            place = ref[half, 0, share : share + SPARE, pl.ds(at, chunk)]
            seen = ref[half, 1, share : share + SPARE, pl.ds(at, chunk)]
            members = prior.shape[0]
            weight, shift = weigh(prior, seen[0:1], seen[1:2], live)
            pad = jnp.zeros((DEEP - 3 * members, chunk), BF16)
            for l in range(levels):
                high, low = split(weight / (1.0 + jnp.abs(place[2:3] - float(l))))
                w_ref[l, :, pl.ds(dst, chunk)] = jnp.concatenate([high, low, high, pad], axis=0)
            turned = jnp.concatenate([shift, jnp.zeros((LANE - members, chunk), F32)], axis=0).T
            high, low = split(turned)
            s_ref[pl.ds(dst, chunk), 0:LANE] = high
            s_ref[pl.ds(dst, chunk), LANE : 2 * LANE] = low
            rc_ref[0:1, pl.ds(dst, chunk)] = place[0:1] * row_scale
            rc_ref[1:2, pl.ds(dst, chunk)] = place[1:2] * col_scale
            return 0

        lax.fori_loop(0, (count + chunk - 1) // chunk, body, 0)
        off = off + (count + LANE - 1) // LANE * LANE
    dst = pl.multiple_of(off, LANE)
    for l in range(levels):
        w_ref[l, :, pl.ds(dst, BLOCK)] = jnp.zeros((DEEP, BLOCK), BF16)
    s_ref[pl.ds(dst, BLOCK), :] = jnp.zeros((BLOCK, 2 * LANE), BF16)
    rc_ref[:, pl.ds(dst, BLOCK)] = jnp.zeros((8, BLOCK), F32)
    first = [number(0, p + 1) // LANE * LANE for p in range(rows)]
    last = [starts[-1] + number(len(priors) - 1, p) if p else starts[-1] for p in range(rows)]
    return off, first, last


def scratch(levels, window, slots):
    room = window * slots + BLOCK + 2 * LANE
    return [
        pltpu.VMEM((levels, DEEP, room), BF16),
        pltpu.VMEM((room, 2 * LANE), BF16),
        pltpu.VMEM((8, room), F32),
    ]


def triple(x):
    high, low = split(x)
    members, width = x.shape
    pad = jnp.zeros((DEEP - 3 * members, width), BF16)
    return jnp.concatenate([high, high, low, pad], axis=0).T


def points_kernel(geometry, window, id_ref, att_ref, seen_ref, *refs):
    levels, _, share, row_scale, col_scale = geometry
    priors, (out_ref, w_ref, s_ref, rc_ref, acc_ref) = refs[:window], refs[window:]
    groups, _, width = out_ref.shape
    off, _, _ = pack(geometry, id_ref, 0, priors, w_ref, s_ref, rc_ref)
    at = pl.multiple_of((id_ref[1] & 1) * width, width)
    x = jnp.concatenate([seen_ref[g, 0:share, pl.ds(at, width)] for g in range(groups)], axis=0)
    att = att_ref[:, pl.ds(at, width)]
    cells = triple(x)
    place = jnp.concatenate([att, jnp.zeros((LANE - 8, width), F32)], axis=0).T
    cell_row = place[:, 0:1] * row_scale
    cell_col = place[:, 1:2] * col_scale
    cell_lev = place[:, 2:3]
    acc_ref[...] = jnp.zeros(acc_ref.shape, F32)

    def body(b, _):
        at = pl.multiple_of(b * BLOCK, BLOCK)
        row_gap = cell_row - rc_ref[0:1, pl.ds(at, BLOCK)]
        col_gap = cell_col - rc_ref[1:2, pl.ds(at, BLOCK)]
        near = jnp.maximum(1.0 - row_gap * row_gap - col_gap * col_gap, 0.0)
        cov = jnp.zeros((width, BLOCK), F32)
        for l in range(levels):
            cov_l = jnp.dot(cells, w_ref[l, :, pl.ds(at, BLOCK)], preferred_element_type=F32)
            cov = jnp.where(cell_lev == float(l), cov_l, cov)
        high, low = split(cov * (near * near))
        s = s_ref[pl.ds(at, BLOCK), :]
        acc_ref[...] += jnp.dot(high, s, preferred_element_type=F32)
        acc_ref[:, 0:LANE] += jnp.dot(low, s[:, 0:LANE], preferred_element_type=F32)
        return 0

    lax.fori_loop(0, (off + BLOCK - 1) // BLOCK, body, 0)
    out = x + (acc_ref[:, 0:LANE] + acc_ref[:, LANE : 2 * LANE]).T[0 : groups * share]
    for g in range(groups):
        out_ref[g, 0:share, :] = out[g * share : (g + 1) * share]

        def put(rows, g=g):
            out_ref[g, share : share + SPARE, :] = rows

        counts = att_ref[5:6, 0:width]
        fill_spare(put, jnp.concatenate([att[0:5], counts, att[6:8]], axis=0), g % 2 == 1)


def update_points(geometry, ids, att, seen, priors):
    groups, padded, slots = seen.shape
    return pl.pallas_call(
        functools.partial(points_kernel, geometry, len(priors)),
        out_shape=jax.ShapeDtypeStruct((groups, padded, slots // 2), F32),
        in_specs=[SMEM] + [VMEM] * (2 + len(priors)),
        out_specs=VMEM,
        scratch_shapes=scratch(geometry[0], len(priors), slots)
        + [pltpu.VMEM((slots // 2, 2 * LANE), F32)],
        compiler_params=PARAMS,
        name="update_points",
    )(ids, att, seen, *priors)


def grid_kernel(geometry, window, groups, id_ref, *refs):
    levels, rows, share, row_scale, col_scale = geometry
    priors, refs = refs[:window], refs[window:]
    xs, outs, refs = refs[:groups], refs[groups : 2 * groups], refs[2 * groups :]
    w_ref, s_ref, rc_ref, xt_ref, acc_ref, q_ref = refs
    bands = xs[0].shape[0]
    height = levels * rows
    cols = bands * LANE
    members = groups * share
    _, first, last = pack(geometry, id_ref, id_ref[1], priors, w_ref, s_ref, rc_ref)
    q_ref[...] = (
        lax.broadcasted_iota(jnp.int32, (cols, LANE), 0) + id_ref[1] * cols
    ).astype(F32) * col_scale

    def cells(i):
        return jnp.concatenate(
            [
                jnp.concatenate(
                    [x.at[b][pl.ds(i, share, stride=height), :] for x in xs], axis=0
                )
                for b in range(bands)
            ],
            axis=1,
        )

    for i in range(height):
        xt_ref[i] = triple(cells(i))

    for p in range(rows):
        cell_row = (id_ref[0] * rows + p).astype(F32) * row_scale
        acc_ref[...] = jnp.zeros(acc_ref.shape, F32)

        def body(b, _, p=p, cell_row=cell_row):
            at = pl.multiple_of(first[p] + b * BLOCK, LANE)
            row_gap = cell_row - rc_ref[0:1, pl.ds(at, BLOCK)]
            base = 1.0 - row_gap * row_gap
            q = q_ref[...]
            col_gap = jnp.concatenate([q] * (BLOCK // LANE), axis=1) - rc_ref[1:2, pl.ds(at, BLOCK)]
            near = jnp.maximum(base - col_gap * col_gap, 0.0)
            taper = near * near
            s = s_ref[pl.ds(at, BLOCK), :]
            for l in range(levels):
                cov = jnp.dot(
                    xt_ref[l * rows + p], w_ref[l, :, pl.ds(at, BLOCK)], preferred_element_type=F32
                )
                high, low = split(cov * taper)
                acc_ref[l] += jnp.dot(high, s, preferred_element_type=F32)
                acc_ref[l, :, 0:LANE] += jnp.dot(low, s[:, 0:LANE], preferred_element_type=F32)
            return 0

        lax.fori_loop(0, jnp.maximum(last[p] - first[p] + BLOCK - 1, 0) // BLOCK, body, 0)
        for l in range(levels):
            at = pl.ds(l * rows + p, share, stride=height)
            inc = (acc_ref[l, :, 0:LANE] + acc_ref[l, :, LANE : 2 * LANE]).T[0:members]
            for g in range(groups):
                for b in range(bands):
                    outs[g].at[b][at, :] = (
                        xs[g].at[b][at, :]
                        + inc[g * share : (g + 1) * share, b * LANE : (b + 1) * LANE]
                    )


def update_grid(geometry, ids, priors, parts):
    levels, rows = geometry[:2]
    halves, groups, _, width = priors[0].shape
    cols = parts[0].shape[0] * LANE
    return pl.pallas_call(
        functools.partial(grid_kernel, geometry, len(priors), groups),
        out_shape=[jax.ShapeDtypeStruct(parts[0].shape, F32)] * groups,
        in_specs=[SMEM] + [VMEM] * (len(priors) + groups),
        out_specs=[VMEM] * groups,
        scratch_shapes=scratch(levels, len(priors), halves * width)
        + [
            pltpu.VMEM((levels * rows, cols, DEEP), BF16),
            pltpu.VMEM((levels, cols, 2 * LANE), F32),
            pltpu.VMEM((cols, LANE), F32),
        ],
        compiler_params=PARAMS,
        name="update_grid",
    )(ids, *priors, *parts)


def restore_kernel(id_ref, *refs):
    parts, out_ref = refs[:-1], refs[-1]
    members, levels, rows, cols = out_ref.shape
    bands = parts[0].shape[0]
    height = levels * rows

    def body(m, _):
        at = pl.multiple_of(m * height, height)
        for k, part in enumerate(parts):
            for band in range(bands):
                block = part[band, pl.ds(at, height), :]
                first = pl.multiple_of((id_ref[1] ^ k) * (bands * LANE) + band * LANE, LANE)
                for l in range(levels):
                    out_ref[m, l, :, pl.ds(first, LANE)] = block[l * rows : (l + 1) * rows]
        return 0

    lax.fori_loop(0, members, body, 0)


def restore(ids, parts, shape):
    return pl.pallas_call(
        restore_kernel,
        out_shape=jax.ShapeDtypeStruct(shape, F32),
        in_specs=[SMEM] + [VMEM] * len(parts),
        out_specs=VMEM,
        compiler_params=PARAMS,
        name="restore",
    )(ids, *parts)


def shifted(value, steps):
    count = lax.axis_size("tile")
    pairs = [(i, i + steps) for i in range(count) if 0 <= i + steps < count]
    return lax.ppermute(value, "tile", pairs)


def window_of(value):
    far = {d: shifted(value, -d) for n in range(REACH, 0, -1) for d in (n, -n)}
    far[0] = value
    return [far[d] for d in range(-REACH, REACH + 1)]


def crossed(value, step):
    count = lax.axis_size("ens")
    return lax.ppermute(value, "ens", [(i, i ^ step) for i in range(count)])


def exchanged(parts):
    return [parts[0]] + [crossed(parts[k], k) for k in range(1, len(parts))]


def on_device(initial_sample_set, flow_velocity, obs_loc, obs_count, obs_value, obs_error):
    x = initial_sample_set
    share, levels, rows, col_total = x.shape
    ens = lax.axis_size("ens")
    ids = jnp.stack([lax.axis_index("tile"), lax.axis_index("ens")]).astype(jnp.int32)
    geometry = (levels, rows, share, 1.0 / (REACH * rows), 1.0 / (col_total // 2))

    top = shifted(x[:, :, rows - 1, :], 1)
    bottom = shifted(x[:, :, 0, :], -1)
    att = order(ids, obs_loc, obs_value, obs_error, obs_count, rows)
    parts = forecast(ids, x, top, bottom, flow_velocity, ens)
    seen = observe(ids, att, parts, levels * rows, share)
    seen = lax.all_gather(seen, "ens", axis=0)
    priors = window_of(seen[:, 0][None])
    parts, _ = lax.optimization_barrier((parts, seen))
    parts = exchanged(parts)
    later = update_points(geometry, ids, att[1], seen[:, 1], priors)
    later = window_of(jnp.stack([later, crossed(later, 1)]))
    parts = update_grid(geometry, ids, priors, parts)
    parts = update_grid(geometry, ids, later, parts)
    return restore(ids, exchanged(parts), x.shape)


def solution(mesh):
    in_specs = (
        P("ens", None, "tile", None),
        P(None, None, "tile", None),
        P(None, None, "tile"),
        P(None, "tile"),
        P(None, "tile"),
        P(None, "tile"),
    )
    out_specs = P("ens", None, "tile", None)
    return jax.shard_map(
        on_device, mesh=mesh, in_specs=in_specs, out_specs=out_specs, check_vma=False
    )
```

profile of v0, /device:TPU:19, one launch (start us, length us, event | category | flops | bytes accessed | tf_op | source)
XLA Modules:
  0.0 177.4 jit_solution(13484065566751755950)
XLA Ops:
  0.0 2.5 %fusion = (f32[20,2,1,2048]{3,2,1,0:T(1,128)S(1)}, f32[20,2,1,2048]{3,2,1,0:T(1,128)S(1)}) fusion(f32[20,2,4,2048]{3,2,1,0:T(4,128)} %x_ref.1), kind=kLoop, calls=%fused_computation.7 | loop fusion | bytes 1310720 | tf_op jit(solution)/shard_map/slice | solution.py:479
  2.8 3.2 %collective-permute-start = (f32[20,2,2048]{2,1,0:T(2,128)S(1)}, f32[20,2,2048]{2,1,0:T(2,128)S(1)}, u32[]{:S(2)}, u32[]{:S(2)}) collective-permute-start(f32[20,2,2048]{2,1,0:T(2,128)S(1)} %bitcast.23), channel_id=1, source_target_pairs={{0,4},{4,8},{8,12},{12,16},{16,20},{20,24},{24,28},{1,5},{5,9},{9,... | collective-permute-start | bytes 983048 | tf_op jit(solution)/shard_map/ppermute | solution.py:453
  6.1 2.1 %collective-permute-start.1 = (f32[20,2,2048]{2,1,0:T(2,128)S(1)}, f32[20,2,2048]{2,1,0:T(2,128)S(1)}, u32[]{:S(2)}, u32[]{:S(2)}) collective-permute-start(f32[20,2,2048]{2,1,0:T(2,128)S(1)} %bitcast.24), channel_id=1, source_target_pairs={{4,0},{8,4},{12,8},{16,12},{20,16},{24,20},{28,24},{5,1},{9,5},{13... | collective-permute-start | bytes 983048 | tf_op jit(solution)/shard_map/ppermute | solution.py:453
  8.4 2.2 %order.1.att_ref = f32[2,8,1024]{2,1,0:T(8,128)S(1)} custom-call(s32[2]{0:T(128)S(1)} %pad_add_fusion.id_ref, s32[3,2,1024]{2,1,0:T(2,128)S(1)} %copy-done.2, f32[2,1024]{1,0:T(2,128)S(1)} %copy-done.3, f32[2,1024]{1,0:T(2,128)S(1)} %copy-done.4, s32[2,1]{1,0:T(2,128)S(1)} %copy.15.count_ref), custom_call_target="tpu_custom_call" | custom-call | tf_op jit(solution)/shard_map/order/pallas_call | solution.py:79
  10.7 9.6 %collective-permute-done.top_ref = f32[20,2,2048]{2,1,0:T(2,128)S(1)} collective-permute-done((f32[20,2,2048]{2,1,0:T(2,128)S(1)}, f32[20,2,2048]{2,1,0:T(2,128)S(1)}, u32[]{:S(2)}, u32[]{:S(2)}) %collective-permute-start) | collective-permute-done | bytes 327712 | tf_op jit(solution)/shard_map/ppermute | solution.py:453
  20.3 3.1 %forecast.1 = (f32[4,160,128]{2,1,0:T(8,128)S(1)}, f32[4,160,128]{2,1,0:T(8,128)S(1)}, f32[4,160,128]{2,1,0:T(8,128)S(1)}, f32[4,160,128]{2,1,0:T(8,128)S(1)}) custom-call(s32[2]{0:T(128)S(1)} %pad_add_fusion.id_ref, f32[20,2,4,2048]{3,2,1,0:T(4,128)S(1)} %copy-done, f32[20,2,2048]{2,1,0:T(2,128)S(1)} %collective-permute-done.top_ref, ...), custom_call_target="tpu_custom_call" | custom-call | tf_op jit(solution)/shard_map/forecast/pallas_call | solution.py:130
  23.4 7.4 %observe.1 = f32[2,24,1024]{2,1,0:T(8,128)S(1)} custom-call(s32[2]{0:T(128)S(1)} %pad_add_fusion.id_ref, f32[2,8,1024]{2,1,0:T(8,128)S(1)} %order.1.att_ref, f32[4,160,128]{2,1,0:T(8,128)S(1)} %get-tuple-element.25.refs_0_.refs_5_, f32[4,160,128]{2,1,0:T(8,128)S(1)} %get-tuple-element.26.refs_1_, f32[4,160,128]{2,1,0:T(8,128)S(1)} %get-tuple-element.27.refs_2_, ...), custom_call_target="tpu_custom_call" | custom-call | tf_op jit(solution)/shard_map/observe/pallas_call | solution.py:189
  30.8 10.1 %all-gather = f32[8,24,1024]{2,1,0:T(8,128)S(1)} all-gather(f32[2,24,1024]{2,1,0:T(8,128)S(1)} %observe.1), channel_id=2, replica_groups=mesh['tile'=8,'ens'=4] {'ens'}, dimensions={0}, use_global_device_ids=true | all-gather | bytes 983040 | tf_op jit(solution)/shard_map/all_gather | solution.py:483
  40.9 2.1 %collective-permute-start.5 = (f32[1,4,24,1024]{3,2,1,0:T(8,128)S(1)}, f32[1,4,24,1024]{3,2,1,0:T(8,128)S(1)}, u32[]{:S(2)}, u32[]{:S(2)}) collective-permute-start(f32[1,4,24,1024]{3,2,1,0:T(8,128)S(1)} %get-tuple-element.39.refs_2_), channel_id=1, source_target_pairs={{8,0},{12,4},{16,8},{20,12},{24,16},{28,20},{9,1},{13,5},{17,9},{2... | collective-permute-start | bytes 1179656 | tf_op jit(solution)/shard_map/ppermute | solution.py:453
  43.0 3.1 %collective-permute-start.4 = (f32[1,4,24,1024]{3,2,1,0:T(8,128)S(1)}, f32[1,4,24,1024]{3,2,1,0:T(8,128)S(1)}, u32[]{:S(2)}, u32[]{:S(2)}) collective-permute-start(f32[1,4,24,1024]{3,2,1,0:T(8,128)S(1)} %get-tuple-element.39.refs_2_), channel_id=1, source_target_pairs={{4,0},{8,4},{12,8},{16,12},{20,16},{24,20},{28,24},{5,1},{9,5},{13... | collective-permute-start | bytes 1179656 | tf_op jit(solution)/shard_map/ppermute | solution.py:453
  46.0 3.1 %collective-permute-start.3 = (f32[1,4,24,1024]{3,2,1,0:T(8,128)S(1)}, f32[1,4,24,1024]{3,2,1,0:T(8,128)S(1)}, u32[]{:S(2)}, u32[]{:S(2)}) collective-permute-start(f32[1,4,24,1024]{3,2,1,0:T(8,128)S(1)} %get-tuple-element.39.refs_2_), channel_id=1, source_target_pairs={{0,4},{4,8},{8,12},{12,16},{16,20},{20,24},{24,28},{1,5},{5,9},{9,... | collective-permute-start | bytes 1179656 | tf_op jit(solution)/shard_map/ppermute | solution.py:453
  49.2 1.9 %collective-permute-start.2 = (f32[1,4,24,1024]{3,2,1,0:T(8,128)S(1)}, f32[1,4,24,1024]{3,2,1,0:T(8,128)S(1)}, u32[]{:S(2)}, u32[]{:S(2)}) collective-permute-start(f32[1,4,24,1024]{3,2,1,0:T(8,128)S(1)} %get-tuple-element.39.refs_2_), channel_id=1, source_target_pairs={{0,8},{4,12},{8,16},{12,20},{16,24},{20,28},{1,9},{5,13},{9,17},{1... | collective-permute-start | bytes 1179656 | tf_op jit(solution)/shard_map/ppermute | solution.py:453
  53.4 9.3 %collective-permute-done.4.refs_3_ = f32[1,4,24,1024]{3,2,1,0:T(8,128)S(1)} collective-permute-done((f32[1,4,24,1024]{3,2,1,0:T(8,128)S(1)}, f32[1,4,24,1024]{3,2,1,0:T(8,128)S(1)}, u32[]{:S(2)}, u32[]{:S(2)}) %collective-permute-start.4) | collective-permute-done | bytes 393248 | tf_op jit(solution)/shard_map/ppermute | solution.py:453
  62.7 3.6 %collective-permute-done.3.refs_1_ = f32[1,4,24,1024]{3,2,1,0:T(8,128)S(1)} collective-permute-done((f32[1,4,24,1024]{3,2,1,0:T(8,128)S(1)}, f32[1,4,24,1024]{3,2,1,0:T(8,128)S(1)}, u32[]{:S(2)}, u32[]{:S(2)}) %collective-permute-start.3) | collective-permute-done | bytes 393248 | tf_op jit(solution)/shard_map/ppermute | solution.py:453
  66.3 11.2 %update_points.1 = f32[4,24,512]{2,1,0:T(8,128)S(1)} custom-call(s32[2]{0:T(128)S(1)} %pad_add_fusion.id_ref, f32[8,1024]{1,0:T(8,128)S(1)} %slice_bitcast_fusion.2.att_ref, f32[4,24,1024]{2,1,0:T(8,128)S(1)} %get-tuple-element.40.seen_ref, f32[1,4,24,1024]{3,2,1,0:T(8,128)S(1)} %collective-permute-done.2.refs_0_, ...), custom_call_target="tpu_custom_call" | custom-call | tf_op jit(solution)/shard_map/update_points/pallas_call | solution.py:326
  80.3 1.9 %collective-permute-start.10 = (f32[2,4,24,512]{3,2,1,0:T(8,128)S(1)}, f32[2,4,24,512]{3,2,1,0:T(8,128)S(1)}, u32[]{:S(2)}, u32[]{:S(2)}) collective-permute-start(f32[2,4,24,512]{3,2,1,0:T(8,128)S(1)} %pad_maximum_fusion.refs_2_), channel_id=1, source_target_pairs={{8,0},{12,4},{16,8},{20,12},{24,16},{28,20},{9,1},{13,5},{17,9},{2... | collective-permute-start | bytes 1179656 | tf_op jit(solution)/shard_map/ppermute | solution.py:453
  82.2 1.9 %collective-permute-start.9 = (f32[2,4,24,512]{3,2,1,0:T(8,128)S(1)}, f32[2,4,24,512]{3,2,1,0:T(8,128)S(1)}, u32[]{:S(2)}, u32[]{:S(2)}) collective-permute-start(f32[2,4,24,512]{3,2,1,0:T(8,128)S(1)} %pad_maximum_fusion.refs_2_), channel_id=1, source_target_pairs={{4,0},{8,4},{12,8},{16,12},{20,16},{24,20},{28,24},{5,1},{9,5},{13... | collective-permute-start | bytes 1179656 | tf_op jit(solution)/shard_map/ppermute | solution.py:453
  84.1 4.3 %collective-permute-start.8 = (f32[2,4,24,512]{3,2,1,0:T(8,128)S(1)}, f32[2,4,24,512]{3,2,1,0:T(8,128)S(1)}, u32[]{:S(2)}, u32[]{:S(2)}) collective-permute-start(f32[2,4,24,512]{3,2,1,0:T(8,128)S(1)} %pad_maximum_fusion.refs_2_), channel_id=1, source_target_pairs={{0,4},{4,8},{8,12},{12,16},{16,20},{20,24},{24,28},{1,5},{5,9},{9,... | collective-permute-start | bytes 1179656 | tf_op jit(solution)/shard_map/ppermute | solution.py:453
  92.3 8.4 %collective-permute-done.13.refs_8_ = f32[4,160,128]{2,1,0:T(8,128)S(1)} collective-permute-done((f32[4,160,128]{2,1,0:T(8,128)S(1)}, f32[4,160,128]{2,1,0:T(8,128)S(1)}, u32[]{:S(2)}, u32[]{:S(2)}) %collective-permute-start.13) | collective-permute-done | bytes 327712 | tf_op jit(solution)/shard_map/ppermute | solution.py:464
  100.7 30.6 %update_grid.2 = (f32[4,160,128]{2,1,0:T(8,128)S(1)}, f32[4,160,128]{2,1,0:T(8,128)S(1)}, f32[4,160,128]{2,1,0:T(8,128)S(1)}, f32[4,160,128]{2,1,0:T(8,128)S(1)}) custom-call(s32[2]{0:T(128)S(1)} %pad_add_fusion.id_ref, f32[1,4,24,1024]{3,2,1,0:T(8,128)S(1)} %collective-permute-done.2.refs_0_, f32[1,4,24,1024]{3,2,1,0:T(8,128)S(1)} %collective-permute-done.3.refs_1_, ...), custom_call_target="tpu_custom_call" | custom-call | tf_op jit(solution)/shard_map/update_grid/pallas_call | solution.py:404
  131.3 26.8 %update_grid.3 = (f32[4,160,128]{2,1,0:T(8,128)S(1)}, f32[4,160,128]{2,1,0:T(8,128)S(1)}, f32[4,160,128]{2,1,0:T(8,128)S(1)}, f32[4,160,128]{2,1,0:T(8,128)S(1)}) custom-call(s32[2]{0:T(128)S(1)} %pad_add_fusion.id_ref, f32[2,4,24,512]{3,2,1,0:T(8,128)S(1)} %collective-permute-done.7.refs_0_, f32[2,4,24,512]{3,2,1,0:T(8,128)S(1)} %collective-permute-done.8.refs_1_, ...), custom_call_target="tpu_custom_call" | custom-call | tf_op jit(solution)/shard_map/update_grid/pallas_call | solution.py:404
  160.4 7.6 %collective-permute-done.15.refs_2_ = f32[4,160,128]{2,1,0:T(8,128)S(1)} collective-permute-done((f32[4,160,128]{2,1,0:T(8,128)S(1)}, f32[4,160,128]{2,1,0:T(8,128)S(1)}, u32[]{:S(2)}, u32[]{:S(2)}) %collective-permute-start.15) | collective-permute-done | bytes 327712 | tf_op jit(solution)/shard_map/ppermute | solution.py:464
  168.0 7.2 %collective-permute-done.16.refs_3_ = f32[4,160,128]{2,1,0:T(8,128)S(1)} collective-permute-done((f32[4,160,128]{2,1,0:T(8,128)S(1)}, f32[4,160,128]{2,1,0:T(8,128)S(1)}, u32[]{:S(2)}, u32[]{:S(2)}) %collective-permute-start.16) | collective-permute-done | bytes 327712 | tf_op jit(solution)/shard_map/ppermute | solution.py:464
  175.2 2.2 %restore.1 = f32[20,2,4,2048]{3,2,1,0:T(4,128)} custom-call(s32[2]{0:T(128)S(1)} %pad_add_fusion.id_ref, f32[4,160,128]{2,1,0:T(8,128)S(1)} %get-tuple-element.33.refs_0_, f32[4,160,128]{2,1,0:T(8,128)S(1)} %collective-permute-done.14.refs_1_, f32[4,160,128]{2,1,0:T(8,128)S(1)} %collective-permute-done.15.refs_2_, ...), custom_call_target="tpu_custom_call" | custom-call | tf_op jit(solution)/shard_map/restore/pallas_call | solution.py:440
  (38 shorter events, 11.8 us)
Async XLA Ops:
  0.0 20.3 %copy-start = (f32[20,2,4,2048]{3,2,1,0:T(4,128)S(1)}, f32[20,2,4,2048]{3,2,1,0:T(4,128)}, u32[]{:S(2)}) copy-start(f32[20,2,4,2048]{3,2,1,0:T(4,128)} %x_ref.1) | copy-start | bytes 3932164
  0.0 8.3 %copy-start.5 = (s32[2,1]{0,1:T(1,128)S(1)}, s32[2,1]{0,1:T(1,128)}, u32[]{:S(2)}) copy-start(s32[2,1]{0,1:T(1,128)} %param.9) | copy-start | bytes 28
  0.0 8.4 %copy-start.4 = (f32[2,1024]{1,0:T(2,128)S(1)}, f32[2,1024]{1,0:T(2,128)}, u32[]{:S(2)}) copy-start(f32[2,1024]{1,0:T(2,128)} %error_ref.1) | copy-start | bytes 24580
  0.0 8.4 %copy-start.3 = (f32[2,1024]{1,0:T(2,128)S(1)}, f32[2,1024]{1,0:T(2,128)}, u32[]{:S(2)}) copy-start(f32[2,1024]{1,0:T(2,128)} %value_ref.1) | copy-start | bytes 24580
  0.0 8.4 %copy-start.2 = (s32[3,2,1024]{2,1,0:T(2,128)S(1)}, s32[3,2,1024]{2,1,0:T(2,128)}, u32[]{:S(2)}) copy-start(s32[3,2,1024]{2,1,0:T(2,128)} %loc_ref.1) | copy-start | bytes 73732
  0.0 20.3 %copy-start.1 = (f32[2,2,4,2048]{3,2,1,0:T(4,128)S(1)}, f32[2,2,4,2048]{3,2,1,0:T(4,128)}, u32[]{:S(2)}) copy-start(f32[2,2,4,2048]{3,2,1,0:T(4,128)} %flow_ref.1) | copy-start | bytes 393220
  2.8 17.5 %collective-permute-start = (f32[20,2,2048]{2,1,0:T(2,128)S(1)}, f32[20,2,2048]{2,1,0:T(2,128)S(1)}, u32[]{:S(2)}, u32[]{:S(2)}) collective-permute-start(f32[20,2,2048]{2,1,0:T(2,128)S(1)} %bitcast.23), channel_id=1, source_target_pairs={{0,4},{4,8},{8,12},{12,16},{16,20},{20,24},{24,28},{1,5},{5,9},{9,... | collective-permute-start | bytes 983048 | tf_op jit(solution)/shard_map/ppermute | solution.py:453
  6.1 14.1 %collective-permute-start.1 = (f32[20,2,2048]{2,1,0:T(2,128)S(1)}, f32[20,2,2048]{2,1,0:T(2,128)S(1)}, u32[]{:S(2)}, u32[]{:S(2)}) collective-permute-start(f32[20,2,2048]{2,1,0:T(2,128)S(1)} %bitcast.24), channel_id=1, source_target_pairs={{4,0},{8,4},{12,8},{16,12},{20,16},{24,20},{28,24},{5,1},{9,5},{13... | collective-permute-start | bytes 983048 | tf_op jit(solution)/shard_map/ppermute | solution.py:453
  40.9 12.5 %collective-permute-start.5 = (f32[1,4,24,1024]{3,2,1,0:T(8,128)S(1)}, f32[1,4,24,1024]{3,2,1,0:T(8,128)S(1)}, u32[]{:S(2)}, u32[]{:S(2)}) collective-permute-start(f32[1,4,24,1024]{3,2,1,0:T(8,128)S(1)} %get-tuple-element.39.refs_2_), channel_id=1, source_target_pairs={{8,0},{12,4},{16,8},{20,12},{24,16},{28,20},{9,1},{13,5},{17,9},{2... | collective-permute-start | bytes 1179656 | tf_op jit(solution)/shard_map/ppermute | solution.py:453
  43.0 19.7 %collective-permute-start.4 = (f32[1,4,24,1024]{3,2,1,0:T(8,128)S(1)}, f32[1,4,24,1024]{3,2,1,0:T(8,128)S(1)}, u32[]{:S(2)}, u32[]{:S(2)}) collective-permute-start(f32[1,4,24,1024]{3,2,1,0:T(8,128)S(1)} %get-tuple-element.39.refs_2_), channel_id=1, source_target_pairs={{4,0},{8,4},{12,8},{16,12},{20,16},{24,20},{28,24},{5,1},{9,5},{13... | collective-permute-start | bytes 1179656 | tf_op jit(solution)/shard_map/ppermute | solution.py:453
  46.0 20.2 %collective-permute-start.3 = (f32[1,4,24,1024]{3,2,1,0:T(8,128)S(1)}, f32[1,4,24,1024]{3,2,1,0:T(8,128)S(1)}, u32[]{:S(2)}, u32[]{:S(2)}) collective-permute-start(f32[1,4,24,1024]{3,2,1,0:T(8,128)S(1)} %get-tuple-element.39.refs_2_), channel_id=1, source_target_pairs={{0,4},{4,8},{8,12},{12,16},{16,20},{20,24},{24,28},{1,5},{5,9},{9,... | collective-permute-start | bytes 1179656 | tf_op jit(solution)/shard_map/ppermute | solution.py:453
  49.2 17.1 %collective-permute-start.2 = (f32[1,4,24,1024]{3,2,1,0:T(8,128)S(1)}, f32[1,4,24,1024]{3,2,1,0:T(8,128)S(1)}, u32[]{:S(2)}, u32[]{:S(2)}) collective-permute-start(f32[1,4,24,1024]{3,2,1,0:T(8,128)S(1)} %get-tuple-element.39.refs_2_), channel_id=1, source_target_pairs={{0,8},{4,12},{8,16},{12,20},{16,24},{20,28},{1,9},{5,13},{9,17},{1... | collective-permute-start | bytes 1179656 | tf_op jit(solution)/shard_map/ppermute | solution.py:453
  51.1 37.3 %collective-permute-start.11 = (f32[4,160,128]{2,1,0:T(8,128)S(1)}, f32[4,160,128]{2,1,0:T(8,128)S(1)}, u32[]{:S(2)}, u32[]{:S(2)}) collective-permute-start(f32[4,160,128]{2,1,0:T(8,128)S(1)} %get-tuple-element.26.refs_1_), channel_id=1, source_target_pairs={{0,1},{1,0},{2,3},{3,2},{4,5},{5,4},{6,7},{7,6},{8,9},{9,8},{10,11... | collective-permute-start | bytes 983048 | tf_op jit(solution)/shard_map/ppermute | solution.py:464
  77.5 2.7 %collective-permute-start.6 = (f32[4,24,512]{2,1,0:T(8,128)S(1)}, f32[4,24,512]{2,1,0:T(8,128)S(1)}, u32[]{:S(2)}, u32[]{:S(2)}) collective-permute-start(f32[4,24,512]{2,1,0:T(8,128)S(1)} %update_points.1), channel_id=1, source_target_pairs={{0,1},{1,0},{2,3},{3,2},{4,5},{5,4},{6,7},{7,6},{8,9},{9,8},{10,11... | collective-permute-start | bytes 589832 | tf_op jit(solution)/shard_map/ppermute | solution.py:464
  79.2 11.2 %collective-permute-start.12 = (f32[4,160,128]{2,1,0:T(8,128)S(1)}, f32[4,160,128]{2,1,0:T(8,128)S(1)}, u32[]{:S(2)}, u32[]{:S(2)}) collective-permute-start(f32[4,160,128]{2,1,0:T(8,128)S(1)} %get-tuple-element.27.refs_2_), channel_id=1, source_target_pairs={{0,2},{1,3},{2,0},{3,1},{4,6},{5,7},{6,4},{7,5},{8,10},{9,11},{10,... | collective-permute-start | bytes 983048 | tf_op jit(solution)/shard_map/ppermute | solution.py:464
  80.3 51.0 %collective-permute-start.10 = (f32[2,4,24,512]{3,2,1,0:T(8,128)S(1)}, f32[2,4,24,512]{3,2,1,0:T(8,128)S(1)}, u32[]{:S(2)}, u32[]{:S(2)}) collective-permute-start(f32[2,4,24,512]{3,2,1,0:T(8,128)S(1)} %pad_maximum_fusion.refs_2_), channel_id=1, source_target_pairs={{8,0},{12,4},{16,8},{20,12},{24,16},{28,20},{9,1},{13,5},{17,9},{2... | collective-permute-start | bytes 1179656 | tf_op jit(solution)/shard_map/ppermute | solution.py:453
  82.2 49.1 %collective-permute-start.9 = (f32[2,4,24,512]{3,2,1,0:T(8,128)S(1)}, f32[2,4,24,512]{3,2,1,0:T(8,128)S(1)}, u32[]{:S(2)}, u32[]{:S(2)}) collective-permute-start(f32[2,4,24,512]{3,2,1,0:T(8,128)S(1)} %pad_maximum_fusion.refs_2_), channel_id=1, source_target_pairs={{4,0},{8,4},{12,8},{16,12},{20,16},{24,20},{28,24},{5,1},{9,5},{13... | collective-permute-start | bytes 1179656 | tf_op jit(solution)/shard_map/ppermute | solution.py:453
  84.1 47.2 %collective-permute-start.8 = (f32[2,4,24,512]{3,2,1,0:T(8,128)S(1)}, f32[2,4,24,512]{3,2,1,0:T(8,128)S(1)}, u32[]{:S(2)}, u32[]{:S(2)}) collective-permute-start(f32[2,4,24,512]{3,2,1,0:T(8,128)S(1)} %pad_maximum_fusion.refs_2_), channel_id=1, source_target_pairs={{0,4},{4,8},{8,12},{12,16},{16,20},{20,24},{24,28},{1,5},{5,9},{9,... | collective-permute-start | bytes 1179656 | tf_op jit(solution)/shard_map/ppermute | solution.py:453
  88.4 42.9 %collective-permute-start.7 = (f32[2,4,24,512]{3,2,1,0:T(8,128)S(1)}, f32[2,4,24,512]{3,2,1,0:T(8,128)S(1)}, u32[]{:S(2)}, u32[]{:S(2)}) collective-permute-start(f32[2,4,24,512]{3,2,1,0:T(8,128)S(1)} %pad_maximum_fusion.refs_2_), channel_id=1, source_target_pairs={{0,8},{4,12},{8,16},{12,20},{16,24},{20,28},{1,9},{5,13},{9,17},{1... | collective-permute-start | bytes 1179656 | tf_op jit(solution)/shard_map/ppermute | solution.py:453
  90.4 10.4 %collective-permute-start.13 = (f32[4,160,128]{2,1,0:T(8,128)S(1)}, f32[4,160,128]{2,1,0:T(8,128)S(1)}, u32[]{:S(2)}, u32[]{:S(2)}) collective-permute-start(f32[4,160,128]{2,1,0:T(8,128)S(1)} %get-tuple-element.28.refs_3_), channel_id=1, source_target_pairs={{0,3},{1,2},{2,1},{3,0},{4,7},{5,6},{6,5},{7,4},{8,11},{9,10},{10,... | collective-permute-start | bytes 983048 | tf_op jit(solution)/shard_map/ppermute | solution.py:464
  158.1 2.3 %collective-permute-start.14 = (f32[4,160,128]{2,1,0:T(8,128)S(1)}, f32[4,160,128]{2,1,0:T(8,128)S(1)}, u32[]{:S(2)}, u32[]{:S(2)}) collective-permute-start(f32[4,160,128]{2,1,0:T(8,128)S(1)} %get-tuple-element.34), channel_id=1, source_target_pairs={{0,1},{1,0},{2,3},{3,2},{4,5},{5,4},{6,7},{7,6},{8,9},{9,8},{10,11... | collective-permute-start | bytes 983048 | tf_op jit(solution)/shard_map/ppermute | solution.py:464
  158.7 9.3 %collective-permute-start.15 = (f32[4,160,128]{2,1,0:T(8,128)S(1)}, f32[4,160,128]{2,1,0:T(8,128)S(1)}, u32[]{:S(2)}, u32[]{:S(2)}) collective-permute-start(f32[4,160,128]{2,1,0:T(8,128)S(1)} %get-tuple-element.35), channel_id=1, source_target_pairs={{0,2},{1,3},{2,0},{3,1},{4,6},{5,7},{6,4},{7,5},{8,10},{9,11},{10,... | collective-permute-start | bytes 983048 | tf_op jit(solution)/shard_map/ppermute | solution.py:464
  159.7 15.5 %collective-permute-start.16 = (f32[4,160,128]{2,1,0:T(8,128)S(1)}, f32[4,160,128]{2,1,0:T(8,128)S(1)}, u32[]{:S(2)}, u32[]{:S(2)}) collective-permute-start(f32[4,160,128]{2,1,0:T(8,128)S(1)} %get-tuple-element.36), channel_id=1, source_target_pairs={{0,3},{1,2},{2,1},{3,0},{4,7},{5,6},{6,5},{7,4},{8,11},{9,10},{10,... | collective-permute-start | bytes 983048 | tf_op jit(solution)/shard_map/ppermute | solution.py:464
where the time goes:
time: 180 us; the launch traced here: 177 us
  Pallas kernels  83.5 us (46%)
  waiting for transfers between devices  47 us (26%)
  starting transfers between devices  33.5 us (19%)
  blocking collectives  10.1 us (6%)
  local copies, waits for them, and re-layouts  3.08 us (2%)
    pallas_call x2, Pallas kernels, update_grid(): pl.pallas_call(functools.partial(grid_kernel, geometry, len(priors), grou...  57.4 us
    ppermute x10, starting transfers between devices, shifted(): return lax.ppermute(value, 'tile', pairs)  25.5 us
    ppermute x10, waiting for transfers between devices, shifted(): return lax.ppermute(value, 'tile', pairs)  23.7 us
    ppermute x7, waiting for transfers between devices, crossed(): return lax.ppermute(value, 'ens', [(i, i ^ step) for i in range(count)])  23.2 us
    pallas_call x1, Pallas kernels, update_points(): pl.pallas_call(functools.partial(points_kernel, geometry, len(priors)), o...  11.2 us
    all_gather x1, blocking collectives, on_device(): seen = lax.all_gather(seen, 'ens', axis=0)  10.1 us
    ppermute x7, starting transfers between devices, crossed(): return lax.ppermute(value, 'ens', [(i, i ^ step) for i in range(count)])  7.98 us
    pallas_call x1, Pallas kernels, observe(): pl.pallas_call(functools.partial(observe_kernel, height, share), out_shap...  7.36 us
  transfers between devices with their start and end apart: 17, of which 7 were waited for; matrix products, arithmetic and copies ran while one was open for 0% of the time, Pallas kernels for 25%

commit v1 on v0

v1 whole, which is shorter than its diff:
```python
import functools

import jax
import jax.numpy as jnp
from jax import lax
from jax.experimental import pallas as pl
from jax.experimental.pallas import tpu as pltpu
from jax.sharding import PartitionSpec as P

BATCHES = 2
REACH = 2
SPARE = 4
SPREAD_RATE = 0.05
EPSILON = 1e-06
LANE = 128
DEEP = 256
BLOCK = 512
F32 = jnp.float32
BF16 = jnp.bfloat16
VMEM = pl.BlockSpec(memory_space=pltpu.VMEM)
SMEM = pl.BlockSpec(memory_space=pltpu.SMEM)
PARAMS = pltpu.CompilerParams(vmem_limit_bytes=32 << 20)


def cost(micros):
    return pl.CostEstimate(flops=int(micros * 1e9), bytes_accessed=0, transcendentals=0)


def split(value):
    high = value.astype(BF16)
    return high, (value - high.astype(F32)).astype(BF16)


def order_kernel(rows, id_ref, loc_ref, value_ref, error_ref, count_ref, att_ref):
    batches, slots = value_ref.shape
    earlier = (
        lax.broadcasted_iota(jnp.int32, (slots, slots), 0)
        < lax.broadcasted_iota(jnp.int32, (slots, slots), 1)
    ).astype(BF16)
    slot = lax.broadcasted_iota(jnp.int32, (1, slots), 1)
    key_of = lax.broadcasted_iota(jnp.int32, (8, slots), 0)
    for b in range(batches):
        count = count_ref[b, 0]
        local_row = loc_ref[0, b : b + 1, :] - id_ref[0] * rows
        key = jnp.where(slot < count, local_row, rows)
        mine = key_of == jnp.broadcast_to(key, (8, slots))
        ones = mine.astype(F32)
        before = jnp.dot(ones.astype(BF16), earlier, preferred_element_type=F32)
        totals = jnp.sum(ones, axis=1, keepdims=True)
        start = jnp.zeros((1, slots), F32)
        place = jnp.zeros((1, slots), F32)
        cumulative = jnp.where(slot == 0, count.astype(F32), 0.0)
        for r in range(rows + 1):
            place = place + ones[r : r + 1] * (before[r : r + 1] + start)
            start = start + totals[r : r + 1]
            cumulative = jnp.where(slot == r + 1, start, cumulative)
        level = loc_ref[2, b : b + 1, :]
        fields = [
            loc_ref[0, b : b + 1, :].astype(F32),
            loc_ref[1, b : b + 1, :].astype(F32),
            level.astype(F32),
            value_ref[b : b + 1, :],
            error_ref[b : b + 1, :],
            (level * rows + local_row).astype(F32),
        ]
        table = jnp.concatenate(fields + [jnp.zeros((2, slots), F32)], axis=0)
        high, low = split(table)
        rest = (table - high.astype(F32) - low.astype(F32)).astype(BF16)
        target = lax.broadcasted_iota(jnp.int32, (slots, slots), 0)
        moved = (target == jnp.broadcast_to(place.astype(jnp.int32), (slots, slots))).astype(BF16)
        out = lax.dot_general(
            jnp.concatenate([high.astype(F32), low.astype(F32), rest.astype(F32)], axis=0).astype(BF16),
            moved,
            (((1,), (1,)), ((), ())),
            preferred_element_type=F32,
        )
        out = (out[0:8] + out[8:16]) + out[16:24]
        att_ref[b] = jnp.concatenate([out[0:5], cumulative, out[5:6], jnp.zeros((1, slots), F32)], axis=0)


def order(ids, obs_loc, obs_value, obs_error, obs_count, rows):
    batches, slots = obs_value.shape
    return pl.pallas_call(
        functools.partial(order_kernel, rows),
        out_shape=jax.ShapeDtypeStruct((batches, 8, slots), F32),
        in_specs=[SMEM, VMEM, VMEM, VMEM, SMEM],
        out_specs=VMEM,
        compiler_params=PARAMS,
        cost_estimate=cost(2),
        name="order",
    )(ids, obs_loc, obs_value, obs_error, obs_count)


def forecast_kernel(id_ref, x_ref, top_ref, bottom_ref, flow_ref, *refs):
    outs, row_ref = refs[:-1], refs[-1]
    members, levels, rows, cols = x_ref.shape
    height = levels * rows
    parts, bands = len(outs), outs[0].shape[0]
    row = lax.broadcasted_iota(jnp.int32, (height, cols), 0)
    col = lax.broadcasted_iota(jnp.int32, (height, cols), 1)
    winds = [
        jnp.concatenate([flow_ref[d, l] for l in range(levels)], axis=0) for d in range(2)
    ]

    def body(m, _):
        x = jnp.concatenate([x_ref[m, l] for l in range(levels)], axis=0)
        above = pltpu.roll(x, 1, 0)
        below = pltpu.roll(x, height - 1, 0)
        for l in range(levels):
            above = jnp.where(row == l * rows, top_ref[m, l : l + 1, :], above)
            below = jnp.where(row == (l + 1) * rows - 1, bottom_ref[m, l : l + 1, :], below)
        left = jnp.where(col == 0, 0.0, pltpu.roll(x, 1, 1))
        right = jnp.where(col == cols - 1, 0.0, pltpu.roll(x, cols - 1, 1))
        tendency = (
            jnp.maximum(winds[0], 0.0) * (x - above)
            + jnp.minimum(winds[0], 0.0) * (below - x)
            + jnp.maximum(winds[1], 0.0) * (x - left)
            + jnp.minimum(winds[1], 0.0) * (right - x)
        )
        row_ref[...] = x - tendency + SPREAD_RATE * (above + below + left + right - 4.0 * x)
        at = pl.multiple_of(m * height, height)
        for k in range(parts):
            first = (id_ref[1] ^ k) * (bands * LANE)
            for band in range(bands):
                source = pl.multiple_of(first + band * LANE, LANE)
                outs[k][band, pl.ds(at, height), :] = row_ref[:, pl.ds(source, LANE)]
        return 0

    lax.fori_loop(0, members, body, 0)


def forecast(ids, x, top, bottom, flow, parts):
    members, levels, rows, cols = x.shape
    out = jax.ShapeDtypeStruct((cols // parts // LANE, members * levels * rows, LANE), F32)
    return pl.pallas_call(
        forecast_kernel,
        out_shape=[out] * parts,
        in_specs=[SMEM] + [VMEM] * 4,
        out_specs=[VMEM] * parts,
        scratch_shapes=[pltpu.VMEM((levels * rows, cols), F32)],
        compiler_params=PARAMS,
        cost_estimate=cost(3),
        name="forecast",
    )(ids, x, top, bottom, flow)


def fill_spare(put, att, odd):
    even_rows = jnp.concatenate([att[0:3], att[5:6]], axis=0)
    odd_rows = jnp.concatenate([att[3:5], att[3:5]], axis=0)
    put(jnp.where(odd, odd_rows, even_rows))


def number(row, at):
    lane = lax.broadcasted_iota(jnp.int32, (1, LANE), 1)
    return jnp.sum(jnp.where(lane == at, row, 0.0)).astype(jnp.int32)


def observe_kernel(levels, share, id_ref, att_ref, *refs):
    parts, out_ref = refs[:-1], refs[-1]
    bands = parts[0].shape[0]
    batches, _, slots = att_ref.shape
    height = parts[0].shape[1] // share
    rows = height // levels
    for b in range(batches):
        att = att_ref[b]
        counts = att[5:6, 0:LANE]
        odd = (id_ref[1] & 1) == 1

        def put(rows, b=b):
            out_ref[b, share : share + SPARE, :] = rows

        fill_spare(put, att, odd)

        count = number(counts, 0)
        ends = [number(counts, r + 1) for r in range(rows)]

        def body(n, _, b=b, count=count, ends=ends):
            at = pl.multiple_of(n * LANE, LANE)
            begin, end = n * LANE, jnp.minimum(n * LANE + LANE, count) - 1
            low = sum((e <= begin).astype(jnp.int32) for e in ends)
            high = sum((e <= end).astype(jnp.int32) for e in ends)
            column = att_ref[b, 1:2, pl.ds(at, LANE)].astype(jnp.int32)
            flat_row = jnp.broadcast_to(att_ref[b, 6:7, pl.ds(at, LANE)].astype(jnp.int32), (8, LANE))
            band_of = jnp.broadcast_to(column >> 7, (8, LANE))
            lane_of = jnp.broadcast_to(column & (LANE - 1), (8, LANE))
            here = [
                band_of == (id_ref[1] ^ k) * bands + band
                for k in range(len(parts))
                for band in range(bands)
            ]

            def one_row(r, found):
                found = list(found)
                for l in range(levels):
                    i = l * rows + r
                    mine = flat_row == i
                    for c, m in enumerate(range(0, share, 8)):
                        size = min(8, share - m)
                        value = jnp.zeros((8, LANE), F32)
                        for j in range(len(parts) * bands):
                            block = parts[j // bands].at[j % bands][
                                pl.ds(m * height + i, size, stride=height), :
                            ]
                            if size < 8:
                                block = jnp.concatenate(
                                    [block, jnp.zeros((8 - size, LANE), F32)], axis=0
                                )
                            picked = jnp.take_along_axis(block, lane_of, axis=1)
                            value = jnp.where(here[j], picked, value)
                        found[c] = jnp.where(mine, value, found[c])
                return tuple(found)

            found = lax.fori_loop(
                low, high + 1, one_row, (jnp.zeros((8, LANE), F32),) * ((share + 7) // 8)
            )
            for c, m in enumerate(range(0, share, 8)):
                size = min(8, share - m)
                out_ref[b, m : m + size, pl.ds(at, LANE)] = found[c][0:size]
            return 0

        out_ref[b, 0:share, :] = jnp.zeros((share, slots), F32)
        lax.fori_loop(0, (count + LANE - 1) // LANE, body, 0)


def observe(ids, att, parts, levels, share):
    batches, _, slots = att.shape
    padded = (share + SPARE + 7) // 8 * 8
    return pl.pallas_call(
        functools.partial(observe_kernel, levels, share),
        out_shape=jax.ShapeDtypeStruct((batches, padded, slots), F32),
        in_specs=[SMEM] + [VMEM] * (1 + len(parts)),
        out_specs=VMEM,
        compiler_params=PARAMS,
        cost_estimate=cost(5),
        name="observe",
    )(ids, att, *parts)


def weigh(prior, value, error, live):
    members = prior.shape[0]
    average = jnp.sum(prior, axis=0, keepdims=True) / members
    deviation = prior - average
    var_prior = jnp.sum(deviation * deviation, axis=0, keepdims=True) / (members - 1) + EPSILON
    combined = var_prior + error
    shrink = jnp.sqrt(error / combined)
    post = (error * average + var_prior * value) / combined
    shift = live * ((shrink - 1.0) * deviation + (post - average))
    weight = (live / ((members - 1) * var_prior)) * deviation
    return weight, shift


def pack_kernel(geometry, window, id_ref, *refs):
    priors, (w_ref, s_ref, rc_ref, span_ref) = refs[:window], refs[window:]
    levels, rows, share, row_scale, col_scale = geometry
    halves, groups, _, width = priors[0].shape
    chunk = min(2 * LANE, width)
    counts = [ref[0, 0, share + 3 : share + 4, 0:LANE] for ref in priors]

    totals = [number(row, 0) for row in counts]
    for p in range(rows):
        span_ref[p] = number(counts[0], p + 1) // LANE * LANE
        span_ref[rows + p] = number(counts[-1], p) if p else jnp.int32(0)
    off = jnp.int32(0)
    starts = []
    for t, ref in enumerate(priors):
        count = totals[t]
        starts.append(off)

        def body(k, _, ref=ref, off=off, count=count):
            src = k * chunk
            half = (k ^ id_ref[1]) & (halves - 1)
            at = pl.multiple_of((k // halves) * chunk, chunk)
            dst = pl.multiple_of(off + src, LANE)
            slot = lax.broadcasted_iota(jnp.int32, (1, chunk), 1) + src
            live = (slot < count).astype(F32)
            prior = jnp.concatenate(
                [ref[half, id_ref[1] ^ g, 0:share, pl.ds(at, chunk)] for g in range(groups)], axis=0
            )
            place = ref[half, 0, share : share + SPARE, pl.ds(at, chunk)]
            seen = ref[half, 1, share : share + SPARE, pl.ds(at, chunk)]
            members = prior.shape[0]
            weight, shift = weigh(prior, seen[0:1], seen[1:2], live)
            pad = jnp.zeros((DEEP - 3 * members, chunk), BF16)
            for l in range(levels):
                high, low = split(weight * (1.0 / (1.0 + jnp.abs(place[2:3] - float(l)))))
                w_ref[l, :, pl.ds(dst, chunk)] = jnp.concatenate([high, low, high, pad], axis=0)
            turned = jnp.concatenate([shift, jnp.zeros((LANE - members, chunk), F32)], axis=0).T
            high, low = split(turned)
            s_ref[pl.ds(dst, chunk), 0:LANE] = high
            s_ref[pl.ds(dst, chunk), LANE : 2 * LANE] = low
            rc_ref[0:1, pl.ds(dst, chunk)] = place[0:1] * row_scale
            rc_ref[1:2, pl.ds(dst, chunk)] = place[1:2] * col_scale
            rc_ref[2:3, pl.ds(dst, chunk)] = place[2:3]
            return 0

        lax.fori_loop(0, (count + chunk - 1) // chunk, body, 0)
        off = off + (count + LANE - 1) // LANE * LANE
    dst = pl.multiple_of(off, LANE)
    for l in range(levels):
        w_ref[l, :, pl.ds(dst, 2 * BLOCK)] = jnp.zeros((DEEP, 2 * BLOCK), BF16)
    s_ref[pl.ds(dst, 2 * BLOCK), :] = jnp.zeros((2 * BLOCK, 2 * LANE), BF16)
    rc_ref[:, pl.ds(dst, 2 * BLOCK)] = jnp.zeros((8, 2 * BLOCK), F32)
    for p in range(rows):
        span_ref[rows + p] = starts[-1] + span_ref[rows + p]
    span_ref[2 * rows] = off


def pack(geometry, ids, priors):
    levels, rows = geometry[:2]
    halves, _, _, width = priors[0].shape
    room = len(priors) * halves * width + 2 * BLOCK + 2 * LANE
    return pl.pallas_call(
        functools.partial(pack_kernel, geometry, len(priors)),
        out_shape=[
            jax.ShapeDtypeStruct((levels, DEEP, room), BF16),
            jax.ShapeDtypeStruct((room, 2 * LANE), BF16),
            jax.ShapeDtypeStruct((8, room), F32),
            jax.ShapeDtypeStruct((2 * rows + 1,), jnp.int32),
        ],
        in_specs=[SMEM] + [VMEM] * len(priors),
        out_specs=[VMEM, VMEM, VMEM, SMEM],
        compiler_params=PARAMS,
        cost_estimate=cost(5),
        name="pack",
    )(ids, *priors)


def triple(x):
    high, low = split(x)
    members, width = x.shape
    pad = jnp.zeros((DEEP - 3 * members, width), BF16)
    return jnp.concatenate([high, high, low, pad], axis=0).T


def points_kernel(
    geometry, id_ref, span_ref, att_ref, seen_ref, w_ref, s_ref, rc_ref, out_ref, acc_ref
):
    levels, rows, share, row_scale, col_scale = geometry
    groups, _, width = out_ref.shape
    chunk = min(2 * LANE, width)
    off = span_ref[2 * rows]
    counts = att_ref[5:6, 0:LANE]
    live = number(counts, 0)
    for c in range(width // chunk):
        lanes = slice(c * chunk, (c + 1) * chunk)
        begin = (2 * c + (id_ref[1] & 1)) * chunk
        at = pl.multiple_of(begin, chunk)
        att = att_ref[:, pl.ds(at, chunk)]
        for g in range(groups):

            def put(rows, g=g):
                out_ref[g, share : share + SPARE, lanes] = rows

            rest = jnp.zeros((1, chunk - LANE), F32)
            head = jnp.concatenate([counts, rest], axis=1) if chunk > LANE else counts
            fill_spare(put, jnp.concatenate([att[0:5], head, att[6:8]], axis=0), g % 2 == 1)

        @pl.when(begin >= live)
        def _():
            for g in range(groups):
                out_ref[g, 0:share, lanes] = jnp.zeros((share, chunk), F32)

        @pl.when(begin < live)
        def _():
            x = jnp.concatenate(
                [seen_ref[id_ref[1] ^ g, 0:share, pl.ds(at, chunk)] for g in range(groups)],
                axis=0,
            )
            cells = triple(x)
            place = jnp.concatenate([att, jnp.zeros((LANE - 8, chunk), F32)], axis=0).T
            cell_row = place[:, 0:1] * row_scale
            cell_col = place[:, 1:2] * col_scale
            cell_lev = place[:, 2:3]
            acc_ref[...] = jnp.zeros(acc_ref.shape, F32)

            def body(b, _):
                at = pl.multiple_of(b * BLOCK, BLOCK)
                row_gap = cell_row - rc_ref[0:1, pl.ds(at, BLOCK)]
                col_gap = cell_col - rc_ref[1:2, pl.ds(at, BLOCK)]
                near = jnp.maximum(1.0 - row_gap * row_gap - col_gap * col_gap, 0.0)
                level = rc_ref[2:3, pl.ds(at, BLOCK)]
                ratio = jnp.ones((chunk, BLOCK), F32)
                for l in range(1, levels):
                    other = (1.0 + level) / (1.0 + jnp.abs(level - float(l)))
                    ratio = jnp.where(cell_lev == float(l), other, ratio)
                cov = jnp.dot(cells, w_ref[0, :, pl.ds(at, BLOCK)], preferred_element_type=F32)
                high, low = split(cov * (near * near) * ratio)
                s = s_ref[pl.ds(at, BLOCK), :]
                acc_ref[...] += jnp.dot(high, s, preferred_element_type=F32)
                acc_ref[:, 0:LANE] += jnp.dot(low, s[:, 0:LANE], preferred_element_type=F32)
                return 0

            def pair(b, _):
                body(2 * b, 0)
                body(2 * b + 1, 0)
                return 0

            lax.fori_loop(0, (off + 2 * BLOCK - 1) // (2 * BLOCK), pair, 0)
            out = x + (acc_ref[:, 0:LANE] + acc_ref[:, LANE : 2 * LANE]).T[0 : groups * share]
            for g in range(groups):
                out_ref[id_ref[1] ^ g, 0:share, lanes] = out[g * share : (g + 1) * share]


def update_points(geometry, ids, att, seen, packed):
    w, s, rc, span = packed
    groups, padded, slots = seen.shape
    return pl.pallas_call(
        functools.partial(points_kernel, geometry),
        out_shape=jax.ShapeDtypeStruct((groups, padded, slots // 2), F32),
        in_specs=[SMEM] * 2 + [VMEM] * 5,
        out_specs=VMEM,
        scratch_shapes=[pltpu.VMEM((min(2 * LANE, slots // 2), 2 * LANE), F32)],
        compiler_params=PARAMS,
        cost_estimate=cost(8),
        name="update_points",
    )(ids, span, att, seen, w, s, rc)


def grid_kernel(geometry, begin, groups, id_ref, span_ref, w_ref, s_ref, rc_ref, *refs):
    levels, all_rows, share, row_scale, col_scale = geometry
    xs, outs, refs = refs[:groups], refs[groups : 2 * groups], refs[2 * groups :]
    xt_ref, acc_ref, q_ref, high_ref, low_ref = refs
    bands = xs[0].shape[0]
    height = levels * all_rows
    rows = outs[0].shape[1] // (share * levels)
    first = [span_ref[begin + p] for p in range(rows)]
    last = [span_ref[all_rows + begin + p] for p in range(rows)]
    cols = bands * LANE
    members = groups * share
    q_ref[...] = (
        lax.broadcasted_iota(jnp.int32, (cols, LANE), 0) + id_ref[1] * cols
    ).astype(F32) * col_scale

    def cells(i):
        return jnp.concatenate(
            [
                jnp.concatenate(
                    [x.at[b][pl.ds(i, share, stride=height), :] for x in xs], axis=0
                )
                for b in range(bands)
            ],
            axis=1,
        )

    for l in range(levels):
        for p in range(rows):
            xt_ref[l * rows + p] = triple(cells(l * all_rows + begin + p))

    steps = [jnp.maximum(last[p] - first[p] + BLOCK - 1, 0) // BLOCK for p in range(rows)]
    ends = [steps[0]]
    for n in steps[1:]:
        ends.append(ends[-1] + n)
    acc_ref[...] = jnp.zeros(acc_ref.shape, F32)

    def locate(i):
        p = jnp.int32(0)
        at = first[0] + i * BLOCK
        for j in range(1, rows):
            past = i >= ends[j - 1]
            p = jnp.where(past, j, p)
            at = jnp.where(past, first[j] + (i - ends[j - 1]) * BLOCK, at)
        return p, pl.multiple_of(at, LANE)

    def spread(i, l):
        p, at = locate(i)
        s = s_ref[pl.ds(at, BLOCK), :]
        acc_ref[p, l] += jnp.dot(high_ref[l], s, preferred_element_type=F32)
        acc_ref[p, l, :, 0:LANE] += jnp.dot(low_ref[l], s[:, 0:LANE], preferred_element_type=F32)

    def step(i, _):
        p, at = locate(i)
        row_gap = (id_ref[0] * all_rows + begin + p).astype(F32) * row_scale - rc_ref[0:1, pl.ds(at, BLOCK)]
        base = 1.0 - row_gap * row_gap
        q = q_ref[...]
        col_gap = jnp.concatenate([q] * (BLOCK // LANE), axis=1) - rc_ref[1:2, pl.ds(at, BLOCK)]
        near = jnp.maximum(base - col_gap * col_gap, 0.0)
        taper = near * near
        for l in range(levels):
            cov = jnp.dot(
                xt_ref[l * rows + p], w_ref[l, :, pl.ds(at, BLOCK)], preferred_element_type=F32
            )
            high, low = split(cov * taper)
            if l == 0:
                spread(jnp.maximum(i - 1, 0), levels - 1)
            else:
                spread(i, l - 1)
            high_ref[l], low_ref[l] = high, low
        return 0

    high_ref[levels - 1] = jnp.zeros(high_ref.shape[1:], BF16)
    low_ref[levels - 1] = jnp.zeros(low_ref.shape[1:], BF16)
    def pair(i, _):
        step(2 * i, 0)
        step(2 * i + 1, 0)
        return 0

    pairs = (ends[-1] + 1) // 2
    lax.fori_loop(0, pairs, pair, 0)
    spread(jnp.maximum(2 * pairs - 1, 0), levels - 1)

    def store(p, _):
        for l in range(levels):
            at = pl.ds(l * all_rows + begin + p, share, stride=height)
            to = pl.ds(l * rows + p, share, stride=levels * rows)
            inc = (acc_ref[p, l, :, 0:LANE] + acc_ref[p, l, :, LANE : 2 * LANE]).T[0:members]
            for g in range(groups):
                for b in range(bands):
                    outs[g].at[b][to, :] = (
                        xs[g].at[b][at, :]
                        + inc[g * share : (g + 1) * share, b * LANE : (b + 1) * LANE]
                    )
        return 0

    lax.fori_loop(0, rows, store, 0)


def update_grid(geometry, ids, packed, parts, begin, rows):
    w, s, rc, span = packed
    levels, all_rows = geometry[:2]
    groups = len(parts)
    bands, depth, _ = parts[0].shape
    cols = bands * LANE
    out = jax.ShapeDtypeStruct((bands, depth // all_rows * rows, LANE), F32)
    return pl.pallas_call(
        functools.partial(grid_kernel, geometry, begin, groups),
        out_shape=[out] * groups,
        in_specs=[SMEM] * 2 + [VMEM] * (3 + groups),
        out_specs=[VMEM] * groups,
        scratch_shapes=[
            pltpu.VMEM((levels * rows, cols, DEEP), BF16),
            pltpu.VMEM((rows, levels, cols, 2 * LANE), F32),
            pltpu.VMEM((cols, LANE), F32),
            pltpu.VMEM((levels, cols, BLOCK), BF16),
            pltpu.VMEM((levels, cols, BLOCK), BF16),
        ],
        compiler_params=PARAMS,
        cost_estimate=cost(7 * rows),
        name="update_grid",
    )(ids, span, w, s, rc, *parts)


def restore_kernel(groups, id_ref, *refs):
    pieces, befores, out_ref = refs[:groups], refs[groups:-1], refs[-1]
    members, levels, all_rows, _ = out_ref.shape
    bands = pieces[0].shape[0]
    height = pieces[0].shape[1] // members
    rows = height // levels
    begin = all_rows - rows

    def body(m, _):
        at = pl.multiple_of(m * height, height)
        for before in befores:
            for l in range(levels):
                out_ref[m, l, 0:begin, :] = before[m, l]
        for k in range(groups):
            for band in range(bands):
                block = pieces[k][band, pl.ds(at, height), :]
                first = pl.multiple_of((id_ref[1] ^ k) * (bands * LANE) + band * LANE, LANE)
                for l in range(levels):
                    out_ref[m, l, begin:all_rows, pl.ds(first, LANE)] = block[
                        l * rows : (l + 1) * rows
                    ]
        return 0

    lax.fori_loop(0, members, body, 0)


def restore(ids, pieces, befores, shape):
    return pl.pallas_call(
        functools.partial(restore_kernel, len(pieces)),
        out_shape=jax.ShapeDtypeStruct(shape, F32),
        in_specs=[SMEM] + [VMEM] * (len(pieces) + len(befores)),
        out_specs=VMEM,
        compiler_params=PARAMS,
        cost_estimate=cost(2),
        name="restore",
    )(ids, *pieces, *befores)


def shifted(value, steps):
    count = lax.axis_size("tile")
    pairs = [(i, i + steps) for i in range(count) if 0 <= i + steps < count]
    return lax.ppermute(value, "tile", pairs)


def paired(value, odd):
    count = lax.axis_size("tile")
    firsts = range(odd, count - 1, 2)
    pairs = [(i, i + 1) for i in firsts] + [(i + 1, i) for i in firsts]
    return lax.ppermute(value, "tile", pairs)


def window_of(value):
    return [
        shifted(value, 2),
        paired(value, 0),
        value,
        paired(value, 1),
        shifted(value, -2),
    ]


def crossed(value, step):
    count = lax.axis_size("ens")
    return lax.ppermute(value, "ens", [(i, i ^ step) for i in range(count)])


def exchanged(parts):
    return [parts[0]] + [crossed(parts[k], k) for k in range(1, len(parts))]


def on_device(initial_sample_set, flow_velocity, obs_loc, obs_count, obs_value, obs_error):
    x = initial_sample_set
    share, levels, rows, col_total = x.shape
    ens = lax.axis_size("ens")
    ids = jnp.stack([lax.axis_index("tile"), lax.axis_index("ens")]).astype(jnp.int32)
    geometry = (levels, rows, share, 1.0 / (REACH * rows), 1.0 / (col_total // 2))

    top = shifted(x[:, :, rows - 1, :], 1)
    bottom = shifted(lax.optimization_barrier(x)[:, :, 0, :], -1)
    att = order(ids, obs_loc, obs_value, obs_error, obs_count, rows)
    parts = forecast(ids, x, top, bottom, flow_velocity, ens)
    seen = observe(ids, att, parts, levels, share)
    seen = lax.all_gather(seen, "ens", axis=0)
    priors = window_of(seen[:, 0][None])
    parts, _ = lax.optimization_barrier((parts, seen))
    parts = exchanged(parts)
    priors, parts = lax.optimization_barrier((priors, parts))
    packed = pack(geometry, ids, priors)
    later = update_points(geometry, ids, att[1], seen[:, 1], packed)
    later = window_of(jnp.stack([later, crossed(later, 1)]))
    parts = update_grid(geometry, ids, packed, parts, 0, rows)
    packed = pack(geometry, ids, later)
    half = rows // 2
    upper = update_grid(geometry, ids, packed, parts, 0, half)
    parts, upper = lax.optimization_barrier((parts, upper))
    lower = update_grid(geometry, ids, packed, parts, half, rows - half)
    done = restore(ids, exchanged(upper), (), (share, levels, half, col_total))
    return restore(ids, exchanged(lower), (done,), x.shape)


def solution(mesh):
    in_specs = (
        P("ens", None, "tile", None),
        P(None, None, "tile", None),
        P(None, None, "tile"),
        P(None, "tile"),
        P(None, "tile"),
        P(None, "tile"),
    )
    out_specs = P("ens", None, "tile", None)
    return jax.shard_map(
        on_device, mesh=mesh, in_specs=in_specs, out_specs=out_specs, check_vma=False
    )
```

time: 180 us -> 159 us (0.88)
  the two profiles are of different devices: /device:TPU:19 before, /device:TPU:11 now
where the time goes in v1:
time: 159 us; the launch traced here: 157 us
  Pallas kernels  81.5 us (51%)
  starting transfers between devices  32.6 us (21%)
  waiting for transfers between devices  25.6 us (16%)
  blocking collectives  10.1 us (6%)
  local copies, waits for them, and re-layouts  6.5 us (4%)
    pallas_call x3, Pallas kernels, update_grid(): pl.pallas_call(functools.partial(grid_kernel, geometry, begin, groups), o...  53.4 us
    ppermute x6, starting transfers between devices, shifted(): return lax.ppermute(value, 'tile', pairs)  15.9 us
    ppermute x10, waiting for transfers between devices, crossed(): return lax.ppermute(value, 'ens', [(i, i ^ step) for i in range(count)])  15.2 us
    all_gather x1, blocking collectives, on_device(): seen = lax.all_gather(seen, 'ens', axis=0)  10.1 us
    ppermute x10, starting transfers between devices, crossed(): return lax.ppermute(value, 'ens', [(i, i ^ step) for i in range(count)])  9.56 us
    pallas_call x2, Pallas kernels, pack(): pl.pallas_call(functools.partial(pack_kernel, geometry, len(priors)), out...  8.32 us
    ppermute x4, starting transfers between devices, paired(): return lax.ppermute(value, 'tile', pairs)  7.19 us
    pallas_call x1, Pallas kernels, update_points(): pl.pallas_call(functools.partial(points_kernel, geometry), out_shape=jax....  6.38 us
  transfers between devices with their start and end apart: 20, of which 7 were waited for; matrix products, arithmetic and copies ran while one was open for 2% of the time, Pallas kernels for 28%

profile of v1, /device:TPU:11, one launch (start us, length us, event | category | flops | bytes accessed | tf_op | source)
XLA Modules:
  0.0 156.6 jit_solution(732787455907369080)
XLA Ops:
  1.8 3.2 %collective-permute-start = (f32[20,2,2048]{2,1,0:T(2,128)S(1)}, f32[20,2,2048]{2,1,0:T(2,128)S(1)}, u32[]{:S(2)}, u32[]{:S(2)}) collective-permute-start(f32[20,2,2048]{2,1,0:T(2,128)S(1)} %bitcast.23), channel_id=1, source_target_pairs={{0,4},{4,8},{8,12},{12,16},{16,20},{20,24},{24,28},{1,5},{5,9},{9,... | collective-permute-start | bytes 983048 | tf_op jit(solution)/shard_map/ppermute | solution.py:583
  6.8 2.1 %collective-permute-start.1 = (f32[20,2,2048]{2,1,0:T(2,128)S(1)}, f32[20,2,2048]{2,1,0:T(2,128)S(1)}, u32[]{:S(2)}, u32[]{:S(2)}) collective-permute-start(f32[20,2,2048]{2,1,0:T(2,128)S(1)} %bitcast.24), channel_id=1, source_target_pairs={{4,0},{8,4},{12,8},{16,12},{20,16},{24,20},{28,24},{5,1},{9,5},{13... | collective-permute-start | bytes 983048 | tf_op jit(solution)/shard_map/ppermute | solution.py:583
  11.9 2.2 %order.1.att_ref = f32[2,8,1024]{2,1,0:T(8,128)S(1)} custom-call(s32[2]{0:T(128)S(1)} %pad_add_fusion.id_ref, s32[3,2,1024]{2,1,0:T(2,128)S(1)} %copy-done.2, f32[2,1024]{1,0:T(2,128)S(1)} %copy-done.3, f32[2,1024]{1,0:T(2,128)S(1)} %copy-done.4, s32[2,1]{1,0:T(2,128)S(1)} %copy.15.count_ref), custom_call_target="tpu_custom_call" | custom-call | flops 2000000000 | tf_op jit(solution)/shard_map/order/pallas_call | solution.py:83
  14.1 5.3 %collective-permute-done.1.bottom_ref = f32[20,2,2048]{2,1,0:T(2,128)S(1)} collective-permute-done((f32[20,2,2048]{2,1,0:T(2,128)S(1)}, f32[20,2,2048]{2,1,0:T(2,128)S(1)}, u32[]{:S(2)}, u32[]{:S(2)}) %collective-permute-start.1) | collective-permute-done | bytes 327712 | tf_op jit(solution)/shard_map/ppermute | solution.py:583
  19.4 3.1 %forecast.1 = (f32[4,160,128]{2,1,0:T(8,128)S(1)}, f32[4,160,128]{2,1,0:T(8,128)S(1)}, f32[4,160,128]{2,1,0:T(8,128)S(1)}, f32[4,160,128]{2,1,0:T(8,128)S(1)}) custom-call(s32[2]{0:T(128)S(1)} %pad_add_fusion.id_ref, f32[20,2,4,2048]{3,2,1,0:T(4,128)S(1)} %copy-done, f32[20,2,2048]{2,1,0:T(2,128)S(1)} %collective-permute-done.top_ref, ...), custom_call_target="tpu_custom_call" | custom-call | flops 3000000000 | tf_op jit(solution)/shard_map/forecast/pallas_call | solution.py:135
  22.5 4.7 %observe.1 = f32[2,24,1024]{2,1,0:T(8,128)S(1)} custom-call(s32[2]{0:T(128)S(1)} %pad_add_fusion.id_ref, f32[2,8,1024]{2,1,0:T(8,128)S(1)} %order.1.att_ref, f32[4,160,128]{2,1,0:T(8,128)S(1)} %get-tuple-element.71.refs_0_, f32[4,160,128]{2,1,0:T(8,128)S(1)} %get-tuple-element.55.refs_1_, f32[4,160,128]{2,1,0:T(8,128)S(1)} %get-tuple-element.56.refs_2_, ...), custom_call_target="tpu_custom_call" | custom-call | flops 5000000000 | tf_op jit(solution)/shard_map/observe/pallas_call | solution.py:228
  27.2 10.1 %all-gather = f32[8,24,1024]{2,1,0:T(8,128)S(1)} all-gather(f32[2,24,1024]{2,1,0:T(8,128)S(1)} %observe.1), channel_id=2, replica_groups=mesh['tile'=8,'ens'=4] {'ens'}, dimensions={0}, use_global_device_ids=true | all-gather | bytes 983040 | tf_op jit(solution)/shard_map/all_gather | solution.py:624
  39.6 4.3 %collective-permute-start.4 = (f32[1,4,24,1024]{3,2,1,0:T(8,128)S(1)}, f32[1,4,24,1024]{3,2,1,0:T(8,128)S(1)}, u32[]{:S(2)}, u32[]{:S(2)}) collective-permute-start(f32[1,4,24,1024]{3,2,1,0:T(8,128)S(1)} %get-tuple-element.60.refs_2_), channel_id=1, source_target_pairs={{4,8},{12,16},{20,24},{8,4},{16,12},{24,20},{5,9},{13,17},{21,25},... | collective-permute-start | bytes 1179656 | tf_op jit(solution)/shard_map/ppermute | solution.py:590
  44.0 3.0 %collective-permute-start.2 = (f32[1,4,24,1024]{3,2,1,0:T(8,128)S(1)}, f32[1,4,24,1024]{3,2,1,0:T(8,128)S(1)}, u32[]{:S(2)}, u32[]{:S(2)}) collective-permute-start(f32[1,4,24,1024]{3,2,1,0:T(8,128)S(1)} %get-tuple-element.60.refs_2_), channel_id=1, source_target_pairs={{0,8},{4,12},{8,16},{12,20},{16,24},{20,28},{1,9},{5,13},{9,17},{1... | collective-permute-start | bytes 1179656 | tf_op jit(solution)/shard_map/ppermute | solution.py:583
  48.9 7.9 %collective-permute-done.8.refs_3_ = f32[4,160,128]{2,1,0:T(8,128)S(1)} collective-permute-done((f32[4,160,128]{2,1,0:T(8,128)S(1)}, f32[4,160,128]{2,1,0:T(8,128)S(1)}, u32[]{:S(2)}, u32[]{:S(2)}) %collective-permute-start.8) | collective-permute-done | bytes 327712 | tf_op jit(solution)/shard_map/ppermute | solution.py:605
  56.7 2.3 %collective-permute-done.4.refs_3_ = f32[1,4,24,1024]{3,2,1,0:T(8,128)S(1)} collective-permute-done((f32[1,4,24,1024]{3,2,1,0:T(8,128)S(1)}, f32[1,4,24,1024]{3,2,1,0:T(8,128)S(1)}, u32[]{:S(2)}, u32[]{:S(2)}) %collective-permute-start.4) | collective-permute-done | bytes 393248 | tf_op jit(solution)/shard_map/ppermute | solution.py:590
  59.0 2.8 %collective-permute-done.3.refs_1_ = f32[1,4,24,1024]{3,2,1,0:T(8,128)S(1)} collective-permute-done((f32[1,4,24,1024]{3,2,1,0:T(8,128)S(1)}, f32[1,4,24,1024]{3,2,1,0:T(8,128)S(1)}, u32[]{:S(2)}, u32[]{:S(2)}) %collective-permute-start.3) | collective-permute-done | bytes 393248 | tf_op jit(solution)/shard_map/ppermute | solution.py:590
  61.8 4.0 %pack.2 = (bf16[2,256,6400]{2,1,0:T(8,128)(2,1)S(1)}, bf16[6400,256]{1,0:T(8,128)(2,1)S(1)}, f32[8,6400]{1,0:T(8,128)S(1)}, s32[9]{0:T(128)S(1)}) custom-call(s32[2]{0:T(128)S(1)} %pad_add_fusion.id_ref, f32[1,4,24,1024]{3,2,1,0:T(8,128)S(1)} %collective-permute-done.2.refs_0_, f32[1,4,24,1024]{3,2,1,0:T(8,128)S(1)} %collective-permute-done.3.refs_1_, ...), custom_call_target="tpu_custom_call" | custom-call | flops 5000000000 | tf_op jit(solution)/shard_map/pack/pallas_call | solution.py:312
  65.8 6.4 %update_points.1 = f32[4,24,512]{2,1,0:T(8,128)S(1)} custom-call(s32[2]{0:T(128)S(1)} %pad_add_fusion.id_ref, s32[9]{0:T(128)S(1)} %get-tuple-element.63.span_ref, f32[8,1024]{1,0:T(8,128)S(1)} %slice_bitcast_fusion.2.att_ref, f32[4,24,1024]{2,1,0:T(8,128)S(1)} %get-tuple-element.95.seen_ref, bf16[2,256,6400]{2,1,0:T(8,128)(2,1)S(1)} %get-tuple-element.64.w_ref, ...), custom_call_target="tpu_custom_call" | custom-call | flops 8000000000 | tf_op jit(solution)/shard_map/update_points/pallas_call | solution.py:407
  72.2 2.2 %collective-permute-start.9 = (f32[4,24,512]{2,1,0:T(8,128)S(1)}, f32[4,24,512]{2,1,0:T(8,128)S(1)}, u32[]{:S(2)}, u32[]{:S(2)}) collective-permute-start(f32[4,24,512]{2,1,0:T(8,128)S(1)} %update_points.1), channel_id=1, source_target_pairs={{0,1},{1,0},{2,3},{3,2},{4,5},{5,4},{6,7},{7,6},{8,9},{9,8},{10,11... | collective-permute-start | bytes 589832 | tf_op jit(solution)/shard_map/ppermute | solution.py:605
  77.4 2.7 %collective-permute-start.12 = (f32[2,4,24,512]{3,2,1,0:T(8,128)S(1)}, f32[2,4,24,512]{3,2,1,0:T(8,128)S(1)}, u32[]{:S(2)}, u32[]{:S(2)}) collective-permute-start(f32[2,4,24,512]{3,2,1,0:T(8,128)S(1)} %pad_maximum_fusion.refs_2_), channel_id=1, source_target_pairs={{4,8},{12,16},{20,24},{8,4},{16,12},{24,20},{5,9},{13,17},{21,25},... | collective-permute-start | bytes 1179656 | tf_op jit(solution)/shard_map/ppermute | solution.py:590
  80.2 3.7 %collective-permute-start.10 = (f32[2,4,24,512]{3,2,1,0:T(8,128)S(1)}, f32[2,4,24,512]{3,2,1,0:T(8,128)S(1)}, u32[]{:S(2)}, u32[]{:S(2)}) collective-permute-start(f32[2,4,24,512]{3,2,1,0:T(8,128)S(1)} %pad_maximum_fusion.refs_2_), channel_id=1, source_target_pairs={{0,8},{4,12},{8,16},{12,20},{16,24},{20,28},{1,9},{5,13},{9,17},{1... | collective-permute-start | bytes 1179656 | tf_op jit(solution)/shard_map/ppermute | solution.py:583
  84.0 26.3 %update_grid.3 = (f32[4,160,128]{2,1,0:T(8,128)S(1)}, f32[4,160,128]{2,1,0:T(8,128)S(1)}, f32[4,160,128]{2,1,0:T(8,128)S(1)}, f32[4,160,128]{2,1,0:T(8,128)S(1)}) custom-call(s32[2]{0:T(128)S(1)} %pad_add_fusion.id_ref, s32[9]{0:T(128)S(1)} %get-tuple-element.63.span_ref, bf16[2,256,6400]{2,1,0:T(8,128)(2,1)S(1)} %get-tuple-element.64.w_ref, ...), custom_call_target="tpu_custom_call" | custom-call | flops 28000000000 | tf_op jit(solution)/shard_map/update_grid/pallas_call | solution.py:524
  110.4 4.3 %pack.3 = (bf16[2,256,6400]{2,1,0:T(8,128)(2,1)S(1)}, bf16[6400,256]{1,0:T(8,128)(2,1)S(1)}, f32[8,6400]{1,0:T(8,128)S(1)}, s32[9]{0:T(128)S(1)}) custom-call(s32[2]{0:T(128)S(1)} %pad_add_fusion.id_ref, f32[2,4,24,512]{3,2,1,0:T(8,128)S(1)} %collective-permute-done.10.refs_0_, f32[2,4,24,512]{3,2,1,0:T(8,128)S(1)} %collective-permute-done.11.refs_1_, ...), custom_call_target="tpu_custom_call" | custom-call | flops 5000000000 | tf_op jit(solution)/shard_map/pack/pallas_call | solution.py:312
  114.7 13.5 %update_grid.4 = (f32[4,80,128]{2,1,0:T(8,128)S(1)}, f32[4,80,128]{2,1,0:T(8,128)S(1)}, f32[4,80,128]{2,1,0:T(8,128)S(1)}, f32[4,80,128]{2,1,0:T(8,128)S(1)}) custom-call(s32[2]{0:T(128)S(1)} %pad_add_fusion.id_ref, s32[9]{0:T(128)S(1)} %get-tuple-element.67.span_ref, bf16[2,256,6400]{2,1,0:T(8,128)(2,1)S(1)} %get-tuple-element.68.w_ref, ...), custom_call_target="tpu_custom_call" | custom-call | flops 14000000000 | tf_op jit(solution)/shard_map/update_grid/pallas_call | solution.py:524
  131.2 13.5 %update_grid.5 = (f32[4,80,128]{2,1,0:T(8,128)S(1)}, f32[4,80,128]{2,1,0:T(8,128)S(1)}, f32[4,80,128]{2,1,0:T(8,128)S(1)}, f32[4,80,128]{2,1,0:T(8,128)S(1)}) custom-call(s32[2]{0:T(128)S(1)} %pad_add_fusion.id_ref, s32[9]{0:T(128)S(1)} %get-tuple-element.67.span_ref, bf16[2,256,6400]{2,1,0:T(8,128)(2,1)S(1)} %get-tuple-element.68.w_ref, ...), custom_call_target="tpu_custom_call" | custom-call | flops 14000000000 | tf_op jit(solution)/shard_map/update_grid/pallas_call | solution.py:524
  148.1 2.3 %collective-permute-done.15.refs_2_ = f32[4,80,128]{2,1,0:T(8,128)S(1)} collective-permute-done((f32[4,80,128]{2,1,0:T(8,128)S(1)}, f32[4,80,128]{2,1,0:T(8,128)S(1)}, u32[]{:S(2)}, u32[]{:S(2)}) %collective-permute-start.15) | collective-permute-done | bytes 163872 | tf_op jit(solution)/shard_map/ppermute | solution.py:605
  150.4 4.0 %collective-permute-done.16.refs_3_ = f32[4,80,128]{2,1,0:T(8,128)S(1)} collective-permute-done((f32[4,80,128]{2,1,0:T(8,128)S(1)}, f32[4,80,128]{2,1,0:T(8,128)S(1)}, u32[]{:S(2)}, u32[]{:S(2)}) %collective-permute-start.16) | collective-permute-done | bytes 163872 | tf_op jit(solution)/shard_map/ppermute | solution.py:605
  154.4 2.2 %restore.3 = f32[20,2,4,2048]{3,2,1,0:T(4,128)} custom-call(s32[2]{0:T(128)S(1)} %pad_add_fusion.id_ref, f32[4,80,128]{2,1,0:T(8,128)S(1)} %get-tuple-element.87.refs_0_, f32[4,80,128]{2,1,0:T(8,128)S(1)} %collective-permute-done.14.refs_1_, f32[4,80,128]{2,1,0:T(8,128)S(1)} %collective-permute-done.15.refs_2_, ...), custom_call_target="tpu_custom_call" | custom-call | flops 2000000000 | tf_op jit(solution)/shard_map/restore/pallas_call | solution.py:569
  (47 shorter events, 20.2 us)
Async XLA Ops:
  1.8 12.2 %collective-permute-start = (f32[20,2,2048]{2,1,0:T(2,128)S(1)}, f32[20,2,2048]{2,1,0:T(2,128)S(1)}, u32[]{:S(2)}, u32[]{:S(2)}) collective-permute-start(f32[20,2,2048]{2,1,0:T(2,128)S(1)} %bitcast.23), channel_id=1, source_target_pairs={{0,4},{4,8},{8,12},{12,16},{16,20},{20,24},{24,28},{1,5},{5,9},{9,... | collective-permute-start | bytes 983048 | tf_op jit(solution)/shard_map/ppermute | solution.py:583
  6.8 12.6 %collective-permute-start.1 = (f32[20,2,2048]{2,1,0:T(2,128)S(1)}, f32[20,2,2048]{2,1,0:T(2,128)S(1)}, u32[]{:S(2)}, u32[]{:S(2)}) collective-permute-start(f32[20,2,2048]{2,1,0:T(2,128)S(1)} %bitcast.24), channel_id=1, source_target_pairs={{4,0},{8,4},{12,8},{16,12},{20,16},{24,20},{28,24},{5,1},{9,5},{13... | collective-permute-start | bytes 983048 | tf_op jit(solution)/shard_map/ppermute | solution.py:583
  9.7 0.7 copy-start.2
  10.5 0.7 copy-start.3
  11.9 7.5 %copy-start = (f32[20,2,4,2048]{3,2,1,0:T(4,128)S(1)}, f32[20,2,4,2048]{3,2,1,0:T(4,128)}, u32[]{:S(2)}) copy-start(f32[20,2,4,2048]{3,2,1,0:T(4,128)} %x_ref.1) | copy-start | bytes 3932164
  11.9 7.5 %copy-start.1 = (f32[2,2,4,2048]{3,2,1,0:T(4,128)S(1)}, f32[2,2,4,2048]{3,2,1,0:T(4,128)}, u32[]{:S(2)}) copy-start(f32[2,2,4,2048]{3,2,1,0:T(4,128)} %flow_ref.1) | copy-start | bytes 393220
  37.2 6.7 %collective-permute-start.6 = (f32[4,160,128]{2,1,0:T(8,128)S(1)}, f32[4,160,128]{2,1,0:T(8,128)S(1)}, u32[]{:S(2)}, u32[]{:S(2)}) collective-permute-start(f32[4,160,128]{2,1,0:T(8,128)S(1)} %get-tuple-element.55.refs_1_), channel_id=1, source_target_pairs={{0,1},{1,0},{2,3},{3,2},{4,5},{5,4},{6,7},{7,6},{8,9},{9,8},{10,11... | collective-permute-start | bytes 983048 | tf_op jit(solution)/shard_map/ppermute | solution.py:605
  37.4 9.6 %collective-permute-start.7 = (f32[4,160,128]{2,1,0:T(8,128)S(1)}, f32[4,160,128]{2,1,0:T(8,128)S(1)}, u32[]{:S(2)}, u32[]{:S(2)}) collective-permute-start(f32[4,160,128]{2,1,0:T(8,128)S(1)} %get-tuple-element.56.refs_2_), channel_id=1, source_target_pairs={{0,2},{1,3},{2,0},{3,1},{4,6},{5,7},{6,4},{7,5},{8,10},{9,11},{10,... | collective-permute-start | bytes 983048 | tf_op jit(solution)/shard_map/ppermute | solution.py:605
  37.6 19.1 %collective-permute-start.5 = (f32[1,4,24,1024]{3,2,1,0:T(8,128)S(1)}, f32[1,4,24,1024]{3,2,1,0:T(8,128)S(1)}, u32[]{:S(2)}, u32[]{:S(2)}) collective-permute-start(f32[1,4,24,1024]{3,2,1,0:T(8,128)S(1)} %get-tuple-element.60.refs_2_), channel_id=1, source_target_pairs={{8,0},{12,4},{16,8},{20,12},{24,16},{28,20},{9,1},{13,5},{17,9},{2... | collective-permute-start | bytes 1179656 | tf_op jit(solution)/shard_map/ppermute | solution.py:583
  39.6 19.4 %collective-permute-start.4 = (f32[1,4,24,1024]{3,2,1,0:T(8,128)S(1)}, f32[1,4,24,1024]{3,2,1,0:T(8,128)S(1)}, u32[]{:S(2)}, u32[]{:S(2)}) collective-permute-start(f32[1,4,24,1024]{3,2,1,0:T(8,128)S(1)} %get-tuple-element.60.refs_2_), channel_id=1, source_target_pairs={{4,8},{12,16},{20,24},{8,4},{16,12},{24,20},{5,9},{13,17},{21,25},... | collective-permute-start | bytes 1179656 | tf_op jit(solution)/shard_map/ppermute | solution.py:590
  43.9 17.9 %collective-permute-start.3 = (f32[1,4,24,1024]{3,2,1,0:T(8,128)S(1)}, f32[1,4,24,1024]{3,2,1,0:T(8,128)S(1)}, u32[]{:S(2)}, u32[]{:S(2)}) collective-permute-start(f32[1,4,24,1024]{3,2,1,0:T(8,128)S(1)} %get-tuple-element.60.refs_2_), channel_id=1, source_target_pairs={{0,4},{8,12},{16,20},{24,28},{4,0},{12,8},{20,16},{28,24},{1,5},{9... | collective-permute-start | bytes 1179656 | tf_op jit(solution)/shard_map/ppermute | solution.py:590
  44.0 17.8 %collective-permute-start.2 = (f32[1,4,24,1024]{3,2,1,0:T(8,128)S(1)}, f32[1,4,24,1024]{3,2,1,0:T(8,128)S(1)}, u32[]{:S(2)}, u32[]{:S(2)}) collective-permute-start(f32[1,4,24,1024]{3,2,1,0:T(8,128)S(1)} %get-tuple-element.60.refs_2_), channel_id=1, source_target_pairs={{0,8},{4,12},{8,16},{12,20},{16,24},{20,28},{1,9},{5,13},{9,17},{1... | collective-permute-start | bytes 1179656 | tf_op jit(solution)/shard_map/ppermute | solution.py:583
  47.0 9.7 %collective-permute-start.8 = (f32[4,160,128]{2,1,0:T(8,128)S(1)}, f32[4,160,128]{2,1,0:T(8,128)S(1)}, u32[]{:S(2)}, u32[]{:S(2)}) collective-permute-start(f32[4,160,128]{2,1,0:T(8,128)S(1)} %get-tuple-element.57.refs_3_), channel_id=1, source_target_pairs={{0,3},{1,2},{2,1},{3,0},{4,7},{5,6},{6,5},{7,4},{8,11},{9,10},{10,... | collective-permute-start | bytes 983048 | tf_op jit(solution)/shard_map/ppermute | solution.py:605
  72.2 3.2 %collective-permute-start.9 = (f32[4,24,512]{2,1,0:T(8,128)S(1)}, f32[4,24,512]{2,1,0:T(8,128)S(1)}, u32[]{:S(2)}, u32[]{:S(2)}) collective-permute-start(f32[4,24,512]{2,1,0:T(8,128)S(1)} %update_points.1), channel_id=1, source_target_pairs={{0,1},{1,0},{2,3},{3,2},{4,5},{5,4},{6,7},{7,6},{8,9},{9,8},{10,11... | collective-permute-start | bytes 589832 | tf_op jit(solution)/shard_map/ppermute | solution.py:605
  75.5 34.8 %collective-permute-start.13 = (f32[2,4,24,512]{3,2,1,0:T(8,128)S(1)}, f32[2,4,24,512]{3,2,1,0:T(8,128)S(1)}, u32[]{:S(2)}, u32[]{:S(2)}) collective-permute-start(f32[2,4,24,512]{3,2,1,0:T(8,128)S(1)} %pad_maximum_fusion.refs_2_), channel_id=1, source_target_pairs={{8,0},{12,4},{16,8},{20,12},{24,16},{28,20},{9,1},{13,5},{17,9},{2... | collective-permute-start | bytes 1179656 | tf_op jit(solution)/shard_map/ppermute | solution.py:583
  77.4 32.9 %collective-permute-start.12 = (f32[2,4,24,512]{3,2,1,0:T(8,128)S(1)}, f32[2,4,24,512]{3,2,1,0:T(8,128)S(1)}, u32[]{:S(2)}, u32[]{:S(2)}) collective-permute-start(f32[2,4,24,512]{3,2,1,0:T(8,128)S(1)} %pad_maximum_fusion.refs_2_), channel_id=1, source_target_pairs={{4,8},{12,16},{20,24},{8,4},{16,12},{24,20},{5,9},{13,17},{21,25},... | collective-permute-start | bytes 1179656 | tf_op jit(solution)/shard_map/ppermute | solution.py:590
  80.2 30.2 %collective-permute-start.11 = (f32[2,4,24,512]{3,2,1,0:T(8,128)S(1)}, f32[2,4,24,512]{3,2,1,0:T(8,128)S(1)}, u32[]{:S(2)}, u32[]{:S(2)}) collective-permute-start(f32[2,4,24,512]{3,2,1,0:T(8,128)S(1)} %pad_maximum_fusion.refs_2_), channel_id=1, source_target_pairs={{0,4},{8,12},{16,20},{24,28},{4,0},{12,8},{20,16},{28,24},{1,5},{9... | collective-permute-start | bytes 1179656 | tf_op jit(solution)/shard_map/ppermute | solution.py:590
  80.2 30.1 %collective-permute-start.10 = (f32[2,4,24,512]{3,2,1,0:T(8,128)S(1)}, f32[2,4,24,512]{3,2,1,0:T(8,128)S(1)}, u32[]{:S(2)}, u32[]{:S(2)}) collective-permute-start(f32[2,4,24,512]{3,2,1,0:T(8,128)S(1)} %pad_maximum_fusion.refs_2_), channel_id=1, source_target_pairs={{0,8},{4,12},{8,16},{12,20},{16,24},{20,28},{1,9},{5,13},{9,17},{1... | collective-permute-start | bytes 1179656 | tf_op jit(solution)/shard_map/ppermute | solution.py:583
  128.2 17.2 %collective-permute-start.17 = (f32[4,80,128]{2,1,0:T(8,128)S(1)}, f32[4,80,128]{2,1,0:T(8,128)S(1)}, u32[]{:S(2)}, u32[]{:S(2)}) collective-permute-start(f32[4,80,128]{2,1,0:T(8,128)S(1)} %get-tuple-element.92), channel_id=1, source_target_pairs={{0,1},{1,0},{2,3},{3,2},{4,5},{5,4},{6,7},{7,6},{8,9},{9,8},{10,11... | collective-permute-start | bytes 491528 | tf_op jit(solution)/shard_map/ppermute | solution.py:605
  129.5 17.5 %collective-permute-start.18 = (f32[4,80,128]{2,1,0:T(8,128)S(1)}, f32[4,80,128]{2,1,0:T(8,128)S(1)}, u32[]{:S(2)}, u32[]{:S(2)}) collective-permute-start(f32[4,80,128]{2,1,0:T(8,128)S(1)} %get-tuple-element.93), channel_id=1, source_target_pairs={{0,2},{1,3},{2,0},{3,1},{4,6},{5,7},{6,4},{7,5},{8,10},{9,11},{10,... | collective-permute-start | bytes 491528 | tf_op jit(solution)/shard_map/ppermute | solution.py:605
  129.9 17.0 %collective-permute-start.19 = (f32[4,80,128]{2,1,0:T(8,128)S(1)}, f32[4,80,128]{2,1,0:T(8,128)S(1)}, u32[]{:S(2)}, u32[]{:S(2)}) collective-permute-start(f32[4,80,128]{2,1,0:T(8,128)S(1)} %get-tuple-element.94), channel_id=1, source_target_pairs={{0,3},{1,2},{2,1},{3,0},{4,7},{5,6},{6,5},{7,4},{8,11},{9,10},{10,... | collective-permute-start | bytes 491528 | tf_op jit(solution)/shard_map/ppermute | solution.py:605
  144.7 3.3 %collective-permute-start.14 = (f32[4,80,128]{2,1,0:T(8,128)S(1)}, f32[4,80,128]{2,1,0:T(8,128)S(1)}, u32[]{:S(2)}, u32[]{:S(2)}) collective-permute-start(f32[4,80,128]{2,1,0:T(8,128)S(1)} %get-tuple-element.88), channel_id=1, source_target_pairs={{0,1},{1,0},{2,3},{3,2},{4,5},{5,4},{6,7},{7,6},{8,9},{9,8},{10,11... | collective-permute-start | bytes 491528 | tf_op jit(solution)/shard_map/ppermute | solution.py:605
  145.0 5.4 %collective-permute-start.15 = (f32[4,80,128]{2,1,0:T(8,128)S(1)}, f32[4,80,128]{2,1,0:T(8,128)S(1)}, u32[]{:S(2)}, u32[]{:S(2)}) collective-permute-start(f32[4,80,128]{2,1,0:T(8,128)S(1)} %get-tuple-element.89), channel_id=1, source_target_pairs={{0,2},{1,3},{2,0},{3,1},{4,6},{5,7},{6,4},{7,5},{8,10},{9,11},{10,... | collective-permute-start | bytes 491528 | tf_op jit(solution)/shard_map/ppermute | solution.py:605
  145.4 9.0 %collective-permute-start.16 = (f32[4,80,128]{2,1,0:T(8,128)S(1)}, f32[4,80,128]{2,1,0:T(8,128)S(1)}, u32[]{:S(2)}, u32[]{:S(2)}) collective-permute-start(f32[4,80,128]{2,1,0:T(8,128)S(1)} %get-tuple-element.90), channel_id=1, source_target_pairs={{0,3},{1,2},{2,1},{3,0},{4,7},{5,6},{6,5},{7,4},{8,11},{9,10},{10,... | collective-permute-start | bytes 491528 | tf_op jit(solution)/shard_map/ppermute | solution.py:605
  (1 other events, 0.7 us)

commit v2 on v1

--- a/solution.py
+++ b/solution.py
@@ -91,7 +91,7 @@
     )(ids, obs_loc, obs_value, obs_error, obs_count)
 
 
-def forecast_kernel(id_ref, x_ref, top_ref, bottom_ref, flow_ref, *refs):
+def forecast_kernel(id_ref, x_ref, flow_ref, *refs):
     outs, row_ref = refs[:-1], refs[-1]
     members, levels, rows, cols = x_ref.shape
     height = levels * rows
@@ -104,11 +104,8 @@
 
     def body(m, _):
         x = jnp.concatenate([x_ref[m, l] for l in range(levels)], axis=0)
-        above = pltpu.roll(x, 1, 0)
-        below = pltpu.roll(x, height - 1, 0)
-        for l in range(levels):
-            above = jnp.where(row == l * rows, top_ref[m, l : l + 1, :], above)
-            below = jnp.where(row == (l + 1) * rows - 1, bottom_ref[m, l : l + 1, :], below)
+        above = jnp.where(row % rows == 0, 0.0, pltpu.roll(x, 1, 0))
+        below = jnp.where(row % rows == rows - 1, 0.0, pltpu.roll(x, height - 1, 0))
         left = jnp.where(col == 0, 0.0, pltpu.roll(x, 1, 1))
         right = jnp.where(col == cols - 1, 0.0, pltpu.roll(x, cols - 1, 1))
         tendency = (
@@ -129,19 +126,66 @@
     lax.fori_loop(0, members, body, 0)
 
 
-def forecast(ids, x, top, bottom, flow, parts):
+def forecast(ids, x, flow, parts):
     members, levels, rows, cols = x.shape
     out = jax.ShapeDtypeStruct((cols // parts // LANE, members * levels * rows, LANE), F32)
     return pl.pallas_call(
         forecast_kernel,
         out_shape=[out] * parts,
-        in_specs=[SMEM] + [VMEM] * 4,
+        in_specs=[SMEM] + [VMEM] * 2,
         out_specs=[VMEM] * parts,
         scratch_shapes=[pltpu.VMEM((levels * rows, cols), F32)],
         compiler_params=PARAMS,
         cost_estimate=cost(3),
         name="forecast",
-    )(ids, x, top, bottom, flow)
+    )(ids, x, flow)
+
+
+def mend_kernel(id_ref, top_ref, bottom_ref, flow_ref, *refs):
+    groups = (len(refs) - 1) // 2
+    parts, outs, rate_ref = refs[:groups], refs[groups : 2 * groups], refs[-1]
+    members, levels, cols = top_ref.shape
+    rows = flow_ref.shape[2]
+    height = levels * rows
+    bands = parts[0].shape[0]
+    row = lax.broadcasted_iota(jnp.int32, (height, cols), 0)
+    wind = jnp.concatenate([flow_ref[0, l] for l in range(levels)], axis=0)
+    rate_ref[0] = jnp.where(row % rows == 0, jnp.maximum(wind, 0.0) + SPREAD_RATE, 0.0)
+    rate_ref[1] = jnp.where(row % rows == rows - 1, SPREAD_RATE - jnp.minimum(wind, 0.0), 0.0)
+
+    def spread_rows(value):
+        return jnp.concatenate(
+            [jnp.broadcast_to(value[l : l + 1], (rows, LANE)) for l in range(levels)], axis=0
+        )
+
+    def body(m, _):
+        at = pl.multiple_of(m * height, height)
+        for k in range(groups):
+            for band in range(bands):
+                source = pl.multiple_of((id_ref[1] ^ k) * (bands * LANE) + band * LANE, LANE)
+                there = pl.ds(source, LANE)
+                outs[k][band, pl.ds(at, height), :] = (
+                    parts[k][band, pl.ds(at, height), :]
+                    + rate_ref[0, :, there] * spread_rows(top_ref[m, :, there])
+                    + rate_ref[1, :, there] * spread_rows(bottom_ref[m, :, there])
+                )
+        return 0
+
+    lax.fori_loop(0, members, body, 0)
+
+
+def mend(ids, top, bottom, flow, parts):
+    _, levels, cols = top.shape
+    return pl.pallas_call(
+        mend_kernel,
+        out_shape=[jax.ShapeDtypeStruct(parts[0].shape, F32)] * len(parts),
+        in_specs=[SMEM] + [VMEM] * (3 + len(parts)),
+        out_specs=[VMEM] * len(parts),
+        scratch_shapes=[pltpu.VMEM((2, levels * flow.shape[2], cols), F32)],
+        compiler_params=PARAMS,
+        cost_estimate=cost(1),
+        name="mend",
+    )(ids, top, bottom, flow, *parts)
 
 
 def fill_spare(put, att, odd):
@@ -155,85 +199,95 @@
     return jnp.sum(jnp.where(lane == at, row, 0.0)).astype(jnp.int32)
 
 
-def observe_kernel(levels, share, id_ref, att_ref, *refs):
-    parts, out_ref = refs[:-1], refs[-1]
+def observe_kernel(levels, share, groups, ranges, id_ref, att_ref, *refs):
+    parts, befores, out_ref = refs[:groups], refs[groups:-1], refs[-1]
     bands = parts[0].shape[0]
-    batches, _, slots = att_ref.shape
+    slots = att_ref.shape[1]
     height = parts[0].shape[1] // share
     rows = height // levels
-    for b in range(batches):
-        att = att_ref[b]
-        counts = att[5:6, 0:LANE]
-        odd = (id_ref[1] & 1) == 1
-
-        def put(rows, b=b):
-            out_ref[b, share : share + SPARE, :] = rows
-
-        fill_spare(put, att, odd)
-
-        count = number(counts, 0)
-        ends = [number(counts, r + 1) for r in range(rows)]
-
-        def body(n, _, b=b, count=count, ends=ends):
-            at = pl.multiple_of(n * LANE, LANE)
-            begin, end = n * LANE, jnp.minimum(n * LANE + LANE, count) - 1
-            low = sum((e <= begin).astype(jnp.int32) for e in ends)
-            high = sum((e <= end).astype(jnp.int32) for e in ends)
-            column = att_ref[b, 1:2, pl.ds(at, LANE)].astype(jnp.int32)
-            flat_row = jnp.broadcast_to(att_ref[b, 6:7, pl.ds(at, LANE)].astype(jnp.int32), (8, LANE))
-            band_of = jnp.broadcast_to(column >> 7, (8, LANE))
-            lane_of = jnp.broadcast_to(column & (LANE - 1), (8, LANE))
-            here = [
-                band_of == (id_ref[1] ^ k) * bands + band
-                for k in range(len(parts))
-                for band in range(bands)
-            ]
-
-            def one_row(r, found):
-                found = list(found)
-                for l in range(levels):
-                    i = l * rows + r
-                    mine = flat_row == i
-                    for c, m in enumerate(range(0, share, 8)):
-                        size = min(8, share - m)
-                        value = jnp.zeros((8, LANE), F32)
-                        for j in range(len(parts) * bands):
-                            block = parts[j // bands].at[j % bands][
-                                pl.ds(m * height + i, size, stride=height), :
-                            ]
-                            if size < 8:
-                                block = jnp.concatenate(
-                                    [block, jnp.zeros((8 - size, LANE), F32)], axis=0
-                                )
-                            picked = jnp.take_along_axis(block, lane_of, axis=1)
-                            value = jnp.where(here[j], picked, value)
-                        found[c] = jnp.where(mine, value, found[c])
-                return tuple(found)
-
+    att = att_ref[...]
+    counts = att[5:6, 0:LANE]
+    odd = (id_ref[1] & 1) == 1
+
+    def put(rows):
+        out_ref[share : share + SPARE, :] = rows
+
+    fill_spare(put, att, odd)
+
+    count = number(counts, 0)
+    ends = [number(counts, r + 1) for r in range(rows)]
+
+    def body(n, _, count=count, ends=ends):
+        at = pl.multiple_of(n * LANE, LANE)
+        begin, end = n * LANE, jnp.minimum(n * LANE + LANE, count) - 1
+        low = sum((e <= begin).astype(jnp.int32) for e in ends)
+        high = sum((e <= end).astype(jnp.int32) for e in ends)
+        column = att_ref[1:2, pl.ds(at, LANE)].astype(jnp.int32)
+        flat_row = jnp.broadcast_to(att_ref[6:7, pl.ds(at, LANE)].astype(jnp.int32), (8, LANE))
+        band_of = jnp.broadcast_to(column >> 7, (8, LANE))
+        lane_of = jnp.broadcast_to(column & (LANE - 1), (8, LANE))
+        here = [
+            band_of == (id_ref[1] ^ k) * bands + band
+            for k in range(len(parts))
+            for band in range(bands)
+        ]
+
+        def one_row(r, found):
+            found = list(found)
+            for l in range(levels):
+                i = l * rows + r
+                mine = flat_row == i
+                for c, m in enumerate(range(0, share, 8)):
+                    size = min(8, share - m)
+                    value = jnp.zeros((8, LANE), F32)
+                    for j in range(len(parts) * bands):
+                        block = parts[j // bands].at[j % bands][
+                            pl.ds(m * height + i, size, stride=height), :
+                        ]
+                        if size < 8:
+                            block = jnp.concatenate(
+                                [block, jnp.zeros((8 - size, LANE), F32)], axis=0
+                            )
+                        picked = jnp.take_along_axis(block, lane_of, axis=1)
+                        value = jnp.where(here[j], picked, value)
+                    found[c] = jnp.where(mine, value, found[c])
+            return tuple(found)
+
+        found = []
+        for m in range(0, share, 8):
+            size = min(8, share - m)
+            value = jnp.zeros((8, LANE), F32)
+            for before in befores:
+                value = before[m : m + size, pl.ds(at, LANE)]
+                if size < 8:
+                    value = jnp.concatenate([value, jnp.zeros((8 - size, LANE), F32)], axis=0)
+            found.append(value)
+        found = tuple(found)
+        for begin_row, end_row in ranges:
             found = lax.fori_loop(
-                low, high + 1, one_row, (jnp.zeros((8, LANE), F32),) * ((share + 7) // 8)
+                jnp.maximum(low, begin_row), jnp.minimum(high, end_row) + 1, one_row, found
             )
-            for c, m in enumerate(range(0, share, 8)):
-                size = min(8, share - m)
-                out_ref[b, m : m + size, pl.ds(at, LANE)] = found[c][0:size]
-            return 0
-
-        out_ref[b, 0:share, :] = jnp.zeros((share, slots), F32)
-        lax.fori_loop(0, (count + LANE - 1) // LANE, body, 0)
-
-
-def observe(ids, att, parts, levels, share):
-    batches, _, slots = att.shape
+        for c, m in enumerate(range(0, share, 8)):
+            size = min(8, share - m)
+            out_ref[m : m + size, pl.ds(at, LANE)] = found[c][0:size]
+        return 0
+
+    out_ref[0:share, :] = jnp.zeros((share, slots), F32)
+    lax.fori_loop(0, (count + LANE - 1) // LANE, body, 0)
+
+
+def observe(ids, att, parts, levels, share, ranges, befores=()):
+    slots = att.shape[1]
     padded = (share + SPARE + 7) // 8 * 8
     return pl.pallas_call(
-        functools.partial(observe_kernel, levels, share),
-        out_shape=jax.ShapeDtypeStruct((batches, padded, slots), F32),
-        in_specs=[SMEM] + [VMEM] * (1 + len(parts)),
+        functools.partial(observe_kernel, levels, share, len(parts), ranges),
+        out_shape=jax.ShapeDtypeStruct((padded, slots), F32),
+        in_specs=[SMEM] + [VMEM] * (1 + len(parts) + len(befores)),
         out_specs=VMEM,
         compiler_params=PARAMS,
-        cost_estimate=cost(5),
+        cost_estimate=cost(3),
         name="observe",
-    )(ids, att, *parts)
+    )(ids, att, *parts, *befores)
 
 
 def weigh(prior, value, error, live):
@@ -253,7 +307,9 @@
     priors, (w_ref, s_ref, rc_ref, span_ref) = refs[:window], refs[window:]
     levels, rows, share, row_scale, col_scale = geometry
     halves, groups, _, width = priors[0].shape
-    chunk = min(2 * LANE, width)
+    piece = width if halves == 1 else min(2 * LANE, width)
+    piece = min(piece, BLOCK)
+    chunk = piece * halves
     counts = [ref[0, 0, share + 3 : share + 4, 0:LANE] for ref in priors]
 
     totals = [number(row, 0) for row in counts]
@@ -268,16 +324,22 @@
 
         def body(k, _, ref=ref, off=off, count=count):
             src = k * chunk
-            half = (k ^ id_ref[1]) & (halves - 1)
-            at = pl.multiple_of((k // halves) * chunk, chunk)
+            at = pl.multiple_of(k * piece, piece)
+            half = [(h ^ id_ref[1]) & (halves - 1) for h in range(halves)]
+
+            def taken(g, begin, size):
+                return jnp.concatenate(
+                    [ref[h, g, begin : begin + size, pl.ds(at, piece)] for h in half], axis=1
+                )
+
             dst = pl.multiple_of(off + src, LANE)
             slot = lax.broadcasted_iota(jnp.int32, (1, chunk), 1) + src
             live = (slot < count).astype(F32)
             prior = jnp.concatenate(
-                [ref[half, id_ref[1] ^ g, 0:share, pl.ds(at, chunk)] for g in range(groups)], axis=0
+                [taken(id_ref[1] ^ g, 0, share) for g in range(groups)], axis=0
             )
-            place = ref[half, 0, share : share + SPARE, pl.ds(at, chunk)]
-            seen = ref[half, 1, share : share + SPARE, pl.ds(at, chunk)]
+            place = taken(0, share, SPARE)
+            seen = taken(1, share, SPARE)
             members = prior.shape[0]
             weight, shift = weigh(prior, seen[0:1], seen[1:2], live)
             pad = jnp.zeros((DEEP - 3 * members, chunk), BF16)
@@ -308,7 +370,7 @@
 def pack(geometry, ids, priors):
     levels, rows = geometry[:2]
     halves, _, _, width = priors[0].shape
-    room = len(priors) * halves * width + 2 * BLOCK + 2 * LANE
+    room = len(priors) * halves * width + 2 * BLOCK + LANE
     return pl.pallas_call(
         functools.partial(pack_kernel, geometry, len(priors)),
         out_shape=[
@@ -619,15 +681,20 @@
     top = shifted(x[:, :, rows - 1, :], 1)
     bottom = shifted(lax.optimization_barrier(x)[:, :, 0, :], -1)
     att = order(ids, obs_loc, obs_value, obs_error, obs_count, rows)
-    parts = forecast(ids, x, top, bottom, flow_velocity, ens)
-    seen = observe(ids, att, parts, levels, share)
+    parts = forecast(ids, x, flow_velocity, ens)
+    inner, edges = [(1, rows - 2)], [(0, 0), (rows - 1, rows - 1)]
+    seen = observe(ids, att[0], parts, levels, share, inner)
+    parts = mend(ids, top, bottom, flow_velocity, parts)
+    seen = observe(ids, att[0], parts, levels, share, edges, (seen,))
     seen = lax.all_gather(seen, "ens", axis=0)
-    priors = window_of(seen[:, 0][None])
-    parts, _ = lax.optimization_barrier((parts, seen))
+    parts, seen = lax.optimization_barrier((parts, seen))
+    priors = window_of(seen[None])
+    ahead = observe(ids, att[1], parts, levels, share, [(0, rows - 1)])
+    ahead = lax.all_gather(ahead, "ens", axis=0)
     parts = exchanged(parts)
-    priors, parts = lax.optimization_barrier((priors, parts))
+    priors, parts, ahead = lax.optimization_barrier((priors, parts, ahead))
     packed = pack(geometry, ids, priors)
-    later = update_points(geometry, ids, att[1], seen[:, 1], packed)
+    later = update_points(geometry, ids, att[1], ahead, packed)
     later = window_of(jnp.stack([later, crossed(later, 1)]))
     parts = update_grid(geometry, ids, packed, parts, 0, rows)
     packed = pack(geometry, ids, later)

time: 159 us -> 147 us (0.925)
  the two profiles are of different devices: /device:TPU:11 before, /device:TPU:19 now
where the time goes in v2:
time: 147 us; the launch traced here: 145 us
  Pallas kernels  76.4 us (52%)
  starting transfers between devices  34 us (23%)
  blocking collectives  17.6 us (12%)
  waiting for transfers between devices  10.2 us (7%)
  local copies, waits for them, and re-layouts  6.55 us (4%)
    pallas_call x3, Pallas kernels, update_grid(): pl.pallas_call(functools.partial(grid_kernel, geometry, begin, groups), o...  51.9 us
    ppermute x6, starting transfers between devices, shifted(): return lax.ppermute(value, 'tile', pairs)  13.6 us
    ppermute x10, starting transfers between devices, crossed(): return lax.ppermute(value, 'ens', [(i, i ^ step) for i in range(count)])  10.5 us
    ppermute x4, starting transfers between devices, paired(): return lax.ppermute(value, 'tile', pairs)  9.93 us
    all_gather x1, blocking collectives, on_device(): ahead = lax.all_gather(ahead, 'ens', axis=0)  9.75 us
    all_gather x1, blocking collectives, on_device(): seen = lax.all_gather(seen, 'ens', axis=0)  7.87 us
    ppermute x10, waiting for transfers between devices, crossed(): return lax.ppermute(value, 'ens', [(i, i ^ step) for i in range(count)])  7.4 us
    pallas_call x2, Pallas kernels, pack(): pl.pallas_call(functools.partial(pack_kernel, geometry, len(priors)), out...  6.46 us
  transfers between devices with their start and end apart: 20, of which 5 were waited for; matrix products, arithmetic and copies ran while one was open for 2% of the time, Pallas kernels for 33%

profile of v2, /device:TPU:19, one launch (start us, length us, event | category | flops | bytes accessed | tf_op | source)
XLA Modules:
  0.0 145.3 jit_solution(7922321623171632831)
XLA Ops:
  1.8 3.2 %collective-permute-start = (f32[20,2,2048]{2,1,0:T(2,128)S(1)}, f32[20,2,2048]{2,1,0:T(2,128)S(1)}, u32[]{:S(2)}, u32[]{:S(2)}) collective-permute-start(f32[20,2,2048]{2,1,0:T(2,128)S(1)} %bitcast.24), channel_id=1, source_target_pairs={{0,4},{4,8},{8,12},{12,16},{16,20},{20,24},{24,28},{1,5},{5,9},{9,... | collective-permute-start | bytes 983048 | tf_op jit(solution)/shard_map/ppermute | solution.py:645
  6.8 2.1 %collective-permute-start.1 = (f32[20,2,2048]{2,1,0:T(2,128)S(1)}, f32[20,2,2048]{2,1,0:T(2,128)S(1)}, u32[]{:S(2)}, u32[]{:S(2)}) collective-permute-start(f32[20,2,2048]{2,1,0:T(2,128)S(1)} %bitcast.25), channel_id=1, source_target_pairs={{4,0},{8,4},{12,8},{16,12},{20,16},{24,20},{28,24},{5,1},{9,5},{13... | collective-permute-start | bytes 983048 | tf_op jit(solution)/shard_map/ppermute | solution.py:645
  11.9 3.1 %forecast.1 = (f32[4,160,128]{2,1,0:T(8,128)S(1)}, f32[4,160,128]{2,1,0:T(8,128)S(1)}, f32[4,160,128]{2,1,0:T(8,128)S(1)}, f32[4,160,128]{2,1,0:T(8,128)S(1)}) custom-call(s32[2]{0:T(128)S(1)} %pad_add_fusion.id_ref, f32[20,2,4,2048]{3,2,1,0:T(4,128)S(1)} %copy-done, f32[2,2,4,2048]{3,2,1,0:T(4,128)S(1)} %copy-done.1), custom_call_target="tpu_custom_call" | custom-call | flops 3000000000 | tf_op jit(solution)/shard_map/forecast/pallas_call | solution.py:132
  15.1 2.2 %order.1 = f32[2,8,1024]{2,1,0:T(8,128)S(1)} custom-call(s32[2]{0:T(128)S(1)} %pad_add_fusion.id_ref, s32[3,2,1024]{2,1,0:T(2,128)S(1)} %copy-done.3, f32[2,1024]{1,0:T(2,128)S(1)} %copy-done.4, f32[2,1024]{1,0:T(2,128)S(1)} %copy-done.5, s32[2,1]{1,0:T(2,128)S(1)} %copy.9.count_ref), custom_call_target="tpu_custom_call" | custom-call | flops 2000000000 | tf_op jit(solution)/shard_map/order/pallas_call | solution.py:83
  22.2 7.9 %all-gather = f32[96,1024]{1,0:T(8,128)S(1)} all-gather(f32[24,1024]{1,0:T(8,128)S(1)} %observe.4), channel_id=2, replica_groups=mesh['tile'=8,'ens'=4] {'ens'}, dimensions={0}, use_global_device_ids=true | all-gather | bytes 491520 | tf_op jit(solution)/shard_map/all_gather | solution.py:689
  31.1 2.1 %collective-permute-start.5 = (f32[1,4,24,1024]{3,2,1,0:T(8,128)S(1)}, f32[1,4,24,1024]{3,2,1,0:T(8,128)S(1)}, u32[]{:S(2)}, u32[]{:S(2)}) collective-permute-start(f32[1,4,24,1024]{3,2,1,0:T(8,128)S(1)} %bitcast.17), channel_id=1, source_target_pairs={{8,0},{12,4},{16,8},{20,12},{24,16},{28,20},{9,1},{13,5},{17,9},{2... | collective-permute-start | bytes 1179656 | tf_op jit(solution)/shard_map/ppermute | solution.py:645
  33.2 4.5 %collective-permute-start.4 = (f32[1,4,24,1024]{3,2,1,0:T(8,128)S(1)}, f32[1,4,24,1024]{3,2,1,0:T(8,128)S(1)}, u32[]{:S(2)}, u32[]{:S(2)}) collective-permute-start(f32[1,4,24,1024]{3,2,1,0:T(8,128)S(1)} %bitcast.18), channel_id=1, source_target_pairs={{4,8},{12,16},{20,24},{8,4},{16,12},{24,20},{5,9},{13,17},{21,25},... | collective-permute-start | bytes 1179656 | tf_op jit(solution)/shard_map/ppermute | solution.py:652
  37.7 2.2 %collective-permute-start.2 = (f32[1,4,24,1024]{3,2,1,0:T(8,128)S(1)}, f32[1,4,24,1024]{3,2,1,0:T(8,128)S(1)}, u32[]{:S(2)}, u32[]{:S(2)}) collective-permute-start(f32[1,4,24,1024]{3,2,1,0:T(8,128)S(1)} %bitcast.20), channel_id=1, source_target_pairs={{0,8},{4,12},{8,16},{12,20},{16,24},{20,28},{1,9},{5,13},{9,17},{1... | collective-permute-start | bytes 1179656 | tf_op jit(solution)/shard_map/ppermute | solution.py:645
  39.9 2.1 %collective-permute-start.8 = (f32[4,160,128]{2,1,0:T(8,128)S(1)}, f32[4,160,128]{2,1,0:T(8,128)S(1)}, u32[]{:S(2)}, u32[]{:S(2)}) collective-permute-start(f32[4,160,128]{2,1,0:T(8,128)S(1)} %get-tuple-element.68.refs_3_), channel_id=1, source_target_pairs={{0,3},{1,2},{2,1},{3,0},{4,7},{5,6},{6,5},{7,4},{8,11},{9,10},{10,... | collective-permute-start | bytes 983048 | tf_op jit(solution)/shard_map/ppermute | solution.py:667
  43.8 9.7 %all-gather.1 = f32[96,1024]{1,0:T(8,128)S(1)} all-gather(f32[24,1024]{1,0:T(8,128)S(1)} %observe.5), channel_id=3, replica_groups=mesh['tile'=8,'ens'=4] {'ens'}, dimensions={0}, use_global_device_ids=true | all-gather | bytes 491520 | tf_op jit(solution)/shard_map/all_gather | solution.py:693
  53.5 2.0 %collective-permute-done.3.refs_1_ = f32[1,4,24,1024]{3,2,1,0:T(8,128)S(1)} collective-permute-done((f32[1,4,24,1024]{3,2,1,0:T(8,128)S(1)}, f32[1,4,24,1024]{3,2,1,0:T(8,128)S(1)}, u32[]{:S(2)}, u32[]{:S(2)}) %collective-permute-start.3) | collective-permute-done | bytes 393248 | tf_op jit(solution)/shard_map/ppermute | solution.py:652
  55.6 3.1 %pack.2 = (bf16[2,256,6272]{2,1,0:T(8,128)(2,1)S(1)}, bf16[6272,256]{1,0:T(8,128)(2,1)S(1)}, f32[8,6272]{1,0:T(8,128)S(1)}, s32[9]{0:T(128)S(1)}) custom-call(s32[2]{0:T(128)S(1)} %pad_add_fusion.id_ref, f32[1,4,24,1024]{3,2,1,0:T(8,128)S(1)} %collective-permute-done.2.refs_0_, f32[1,4,24,1024]{3,2,1,0:T(8,128)S(1)} %collective-permute-done.3.refs_1_, ...), custom_call_target="tpu_custom_call" | custom-call | flops 5000000000 | tf_op jit(solution)/shard_map/pack/pallas_call | solution.py:374
  58.7 3.6 %update_points.1 = f32[4,24,512]{2,1,0:T(8,128)S(1)} custom-call(s32[2]{0:T(128)S(1)} %pad_add_fusion.id_ref, s32[9]{0:T(128)S(1)} %get-tuple-element.74.span_ref, f32[8,1024]{1,0:T(8,128)S(1)} %get-tuple-element.107.att_ref, f32[4,24,1024]{2,1,0:T(8,128)S(1)} %bitcast.22, bf16[2,256,6272]{2,1,0:T(8,128)(2,1)S(1)} %get-tuple-element.76.w_ref, ...), custom_call_target="tpu_custom_call" | custom-call | flops 8000000000 | tf_op jit(solution)/shard_map/update_points/pallas_call | solution.py:469
  62.2 2.2 %collective-permute-start.9 = (f32[4,24,512]{2,1,0:T(8,128)S(1)}, f32[4,24,512]{2,1,0:T(8,128)S(1)}, u32[]{:S(2)}, u32[]{:S(2)}) collective-permute-start(f32[4,24,512]{2,1,0:T(8,128)S(1)} %update_points.1), channel_id=1, source_target_pairs={{0,1},{1,0},{2,3},{3,2},{4,5},{5,4},{6,7},{7,6},{8,9},{9,8},{10,11... | collective-permute-start | bytes 589832 | tf_op jit(solution)/shard_map/ppermute | solution.py:667
  65.5 1.9 %collective-permute-start.13 = (f32[2,4,24,512]{3,2,1,0:T(8,128)S(1)}, f32[2,4,24,512]{3,2,1,0:T(8,128)S(1)}, u32[]{:S(2)}, u32[]{:S(2)}) collective-permute-start(f32[2,4,24,512]{3,2,1,0:T(8,128)S(1)} %pad_maximum_fusion.refs_2_), channel_id=1, source_target_pairs={{8,0},{12,4},{16,8},{20,12},{24,16},{28,20},{9,1},{13,5},{17,9},{2... | collective-permute-start | bytes 1179656 | tf_op jit(solution)/shard_map/ppermute | solution.py:645
  67.4 5.3 %collective-permute-start.12 = (f32[2,4,24,512]{3,2,1,0:T(8,128)S(1)}, f32[2,4,24,512]{3,2,1,0:T(8,128)S(1)}, u32[]{:S(2)}, u32[]{:S(2)}) collective-permute-start(f32[2,4,24,512]{3,2,1,0:T(8,128)S(1)} %pad_maximum_fusion.refs_2_), channel_id=1, source_target_pairs={{4,8},{12,16},{20,24},{8,4},{16,12},{24,20},{5,9},{13,17},{21,25},... | collective-permute-start | bytes 1179656 | tf_op jit(solution)/shard_map/ppermute | solution.py:652
  72.8 2.2 %collective-permute-start.10 = (f32[2,4,24,512]{3,2,1,0:T(8,128)S(1)}, f32[2,4,24,512]{3,2,1,0:T(8,128)S(1)}, u32[]{:S(2)}, u32[]{:S(2)}) collective-permute-start(f32[2,4,24,512]{3,2,1,0:T(8,128)S(1)} %pad_maximum_fusion.refs_2_), channel_id=1, source_target_pairs={{0,8},{4,12},{8,16},{12,20},{16,24},{20,28},{1,9},{5,13},{9,17},{1... | collective-permute-start | bytes 1179656 | tf_op jit(solution)/shard_map/ppermute | solution.py:645
  75.0 22.7 %update_grid.3 = (f32[4,160,128]{2,1,0:T(8,128)S(1)}, f32[4,160,128]{2,1,0:T(8,128)S(1)}, f32[4,160,128]{2,1,0:T(8,128)S(1)}, f32[4,160,128]{2,1,0:T(8,128)S(1)}) custom-call(s32[2]{0:T(128)S(1)} %pad_add_fusion.id_ref, s32[9]{0:T(128)S(1)} %get-tuple-element.74.span_ref, bf16[2,256,6272]{2,1,0:T(8,128)(2,1)S(1)} %get-tuple-element.76.w_ref, ...), custom_call_target="tpu_custom_call" | custom-call | flops 28000000000 | tf_op jit(solution)/shard_map/update_grid/pallas_call | solution.py:586
  97.8 3.4 %pack.3 = (bf16[2,256,6272]{2,1,0:T(8,128)(2,1)S(1)}, bf16[6272,256]{1,0:T(8,128)(2,1)S(1)}, f32[8,6272]{1,0:T(8,128)S(1)}, s32[9]{0:T(128)S(1)}) custom-call(s32[2]{0:T(128)S(1)} %pad_add_fusion.id_ref, f32[2,4,24,512]{3,2,1,0:T(8,128)S(1)} %collective-permute-done.10.refs_0_, f32[2,4,24,512]{3,2,1,0:T(8,128)S(1)} %collective-permute-done.11.refs_1_, ...), custom_call_target="tpu_custom_call" | custom-call | flops 5000000000 | tf_op jit(solution)/shard_map/pack/pallas_call | solution.py:374
  101.2 13.6 %update_grid.4 = (f32[4,80,128]{2,1,0:T(8,128)S(1)}, f32[4,80,128]{2,1,0:T(8,128)S(1)}, f32[4,80,128]{2,1,0:T(8,128)S(1)}, f32[4,80,128]{2,1,0:T(8,128)S(1)}) custom-call(s32[2]{0:T(128)S(1)} %pad_add_fusion.id_ref, s32[9]{0:T(128)S(1)} %get-tuple-element.79.span_ref, bf16[2,256,6272]{2,1,0:T(8,128)(2,1)S(1)} %get-tuple-element.80.w_ref, ...), custom_call_target="tpu_custom_call" | custom-call | flops 14000000000 | tf_op jit(solution)/shard_map/update_grid/pallas_call | solution.py:586
  117.7 15.6 %update_grid.5 = (f32[4,80,128]{2,1,0:T(8,128)S(1)}, f32[4,80,128]{2,1,0:T(8,128)S(1)}, f32[4,80,128]{2,1,0:T(8,128)S(1)}, f32[4,80,128]{2,1,0:T(8,128)S(1)}) custom-call(s32[2]{0:T(128)S(1)} %pad_add_fusion.id_ref, s32[9]{0:T(128)S(1)} %get-tuple-element.79.span_ref, bf16[2,256,6272]{2,1,0:T(8,128)(2,1)S(1)} %get-tuple-element.80.w_ref, ...), custom_call_target="tpu_custom_call" | custom-call | flops 14000000000 | tf_op jit(solution)/shard_map/update_grid/pallas_call | solution.py:586
  136.7 2.3 %collective-permute-done.15.refs_2_ = f32[4,80,128]{2,1,0:T(8,128)S(1)} collective-permute-done((f32[4,80,128]{2,1,0:T(8,128)S(1)}, f32[4,80,128]{2,1,0:T(8,128)S(1)}, u32[]{:S(2)}, u32[]{:S(2)}) %collective-permute-start.15) | collective-permute-done | bytes 163872 | tf_op jit(solution)/shard_map/ppermute | solution.py:667
  139.0 4.0 %collective-permute-done.16.refs_3_ = f32[4,80,128]{2,1,0:T(8,128)S(1)} collective-permute-done((f32[4,80,128]{2,1,0:T(8,128)S(1)}, f32[4,80,128]{2,1,0:T(8,128)S(1)}, u32[]{:S(2)}, u32[]{:S(2)}) %collective-permute-start.16) | collective-permute-done | bytes 163872 | tf_op jit(solution)/shard_map/ppermute | solution.py:667
  143.0 2.2 %restore.3 = f32[20,2,4,2048]{3,2,1,0:T(4,128)} custom-call(s32[2]{0:T(128)S(1)} %pad_add_fusion.id_ref, f32[4,80,128]{2,1,0:T(8,128)S(1)} %get-tuple-element.99.refs_0_, f32[4,80,128]{2,1,0:T(8,128)S(1)} %collective-permute-done.14.refs_1_, f32[4,80,128]{2,1,0:T(8,128)S(1)} %collective-permute-done.15.refs_2_, ...), custom_call_target="tpu_custom_call" | custom-call | flops 2000000000 | tf_op jit(solution)/shard_map/restore/pallas_call | solution.py:631
  (52 shorter events, 21.8 us)
Async XLA Ops:
  1.8 16.8 %collective-permute-start = (f32[20,2,2048]{2,1,0:T(2,128)S(1)}, f32[20,2,2048]{2,1,0:T(2,128)S(1)}, u32[]{:S(2)}, u32[]{:S(2)}) collective-permute-start(f32[20,2,2048]{2,1,0:T(2,128)S(1)} %bitcast.24), channel_id=1, source_target_pairs={{0,4},{4,8},{8,12},{12,16},{16,20},{20,24},{24,28},{1,5},{5,9},{9,... | collective-permute-start | bytes 983048 | tf_op jit(solution)/shard_map/ppermute | solution.py:645
  6.8 12.6 %collective-permute-start.1 = (f32[20,2,2048]{2,1,0:T(2,128)S(1)}, f32[20,2,2048]{2,1,0:T(2,128)S(1)}, u32[]{:S(2)}, u32[]{:S(2)}) collective-permute-start(f32[20,2,2048]{2,1,0:T(2,128)S(1)} %bitcast.25), channel_id=1, source_target_pairs={{4,0},{8,4},{12,8},{16,12},{20,16},{24,20},{28,24},{5,1},{9,5},{13... | collective-permute-start | bytes 983048 | tf_op jit(solution)/shard_map/ppermute | solution.py:645
  11.9 3.1 %copy-start.3 = (s32[3,2,1024]{2,1,0:T(2,128)S(1)}, s32[3,2,1024]{2,1,0:T(2,128)}, u32[]{:S(2)}) copy-start(s32[3,2,1024]{2,1,0:T(2,128)} %loc_ref.1) | copy-start | bytes 73732
  11.9 3.1 %copy-start.4 = (f32[2,1024]{1,0:T(2,128)S(1)}, f32[2,1024]{1,0:T(2,128)}, u32[]{:S(2)}) copy-start(f32[2,1024]{1,0:T(2,128)} %value_ref.1) | copy-start | bytes 24580
  11.9 3.1 %copy-start.5 = (f32[2,1024]{1,0:T(2,128)S(1)}, f32[2,1024]{1,0:T(2,128)}, u32[]{:S(2)}) copy-start(f32[2,1024]{1,0:T(2,128)} %error_ref.1) | copy-start | bytes 24580
  17.3 2.0 %copy-start.2 = (f32[2,2,4,2048]{3,2,1,0:T(4,128)S(1)}, f32[2,2,4,2048]{3,2,1,0:T(4,128)}, u32[]{:S(2)}) copy-start(f32[2,2,4,2048]{3,2,1,0:T(4,128)} %flow_ref.3) | copy-start | bytes 393220
  30.0 7.7 %collective-permute-start.6 = (f32[4,160,128]{2,1,0:T(8,128)S(1)}, f32[4,160,128]{2,1,0:T(8,128)S(1)}, u32[]{:S(2)}, u32[]{:S(2)}) collective-permute-start(f32[4,160,128]{2,1,0:T(8,128)S(1)} %get-tuple-element.66.refs_1_), channel_id=1, source_target_pairs={{0,1},{1,0},{2,3},{3,2},{4,5},{5,4},{6,7},{7,6},{8,9},{9,8},{10,11... | collective-permute-start | bytes 983048 | tf_op jit(solution)/shard_map/ppermute | solution.py:667
  30.2 9.7 %collective-permute-start.7 = (f32[4,160,128]{2,1,0:T(8,128)S(1)}, f32[4,160,128]{2,1,0:T(8,128)S(1)}, u32[]{:S(2)}, u32[]{:S(2)}) collective-permute-start(f32[4,160,128]{2,1,0:T(8,128)S(1)} %get-tuple-element.67.refs_2_), channel_id=1, source_target_pairs={{0,2},{1,3},{2,0},{3,1},{4,6},{5,7},{6,4},{7,5},{8,10},{9,11},{10,... | collective-permute-start | bytes 983048 | tf_op jit(solution)/shard_map/ppermute | solution.py:667
  31.1 22.4 %collective-permute-start.5 = (f32[1,4,24,1024]{3,2,1,0:T(8,128)S(1)}, f32[1,4,24,1024]{3,2,1,0:T(8,128)S(1)}, u32[]{:S(2)}, u32[]{:S(2)}) collective-permute-start(f32[1,4,24,1024]{3,2,1,0:T(8,128)S(1)} %bitcast.17), channel_id=1, source_target_pairs={{8,0},{12,4},{16,8},{20,12},{24,16},{28,20},{9,1},{13,5},{17,9},{2... | collective-permute-start | bytes 1179656 | tf_op jit(solution)/shard_map/ppermute | solution.py:645
  33.2 20.3 %collective-permute-start.4 = (f32[1,4,24,1024]{3,2,1,0:T(8,128)S(1)}, f32[1,4,24,1024]{3,2,1,0:T(8,128)S(1)}, u32[]{:S(2)}, u32[]{:S(2)}) collective-permute-start(f32[1,4,24,1024]{3,2,1,0:T(8,128)S(1)} %bitcast.18), channel_id=1, source_target_pairs={{4,8},{12,16},{20,24},{8,4},{16,12},{24,20},{5,9},{13,17},{21,25},... | collective-permute-start | bytes 1179656 | tf_op jit(solution)/shard_map/ppermute | solution.py:652
  37.7 17.9 %collective-permute-start.3 = (f32[1,4,24,1024]{3,2,1,0:T(8,128)S(1)}, f32[1,4,24,1024]{3,2,1,0:T(8,128)S(1)}, u32[]{:S(2)}, u32[]{:S(2)}) collective-permute-start(f32[1,4,24,1024]{3,2,1,0:T(8,128)S(1)} %bitcast.19), channel_id=1, source_target_pairs={{0,4},{8,12},{16,20},{24,28},{4,0},{12,8},{20,16},{28,24},{1,5},{9... | collective-permute-start | bytes 1179656 | tf_op jit(solution)/shard_map/ppermute | solution.py:652
  37.7 17.8 %collective-permute-start.2 = (f32[1,4,24,1024]{3,2,1,0:T(8,128)S(1)}, f32[1,4,24,1024]{3,2,1,0:T(8,128)S(1)}, u32[]{:S(2)}, u32[]{:S(2)}) collective-permute-start(f32[1,4,24,1024]{3,2,1,0:T(8,128)S(1)} %bitcast.20), channel_id=1, source_target_pairs={{0,8},{4,12},{8,16},{12,20},{16,24},{20,28},{1,9},{5,13},{9,17},{1... | collective-permute-start | bytes 1179656 | tf_op jit(solution)/shard_map/ppermute | solution.py:645
  39.9 13.6 %collective-permute-start.8 = (f32[4,160,128]{2,1,0:T(8,128)S(1)}, f32[4,160,128]{2,1,0:T(8,128)S(1)}, u32[]{:S(2)}, u32[]{:S(2)}) collective-permute-start(f32[4,160,128]{2,1,0:T(8,128)S(1)} %get-tuple-element.68.refs_3_), channel_id=1, source_target_pairs={{0,3},{1,2},{2,1},{3,0},{4,7},{5,6},{6,5},{7,4},{8,11},{9,10},{10,... | collective-permute-start | bytes 983048 | tf_op jit(solution)/shard_map/ppermute | solution.py:667
  62.2 3.2 %collective-permute-start.9 = (f32[4,24,512]{2,1,0:T(8,128)S(1)}, f32[4,24,512]{2,1,0:T(8,128)S(1)}, u32[]{:S(2)}, u32[]{:S(2)}) collective-permute-start(f32[4,24,512]{2,1,0:T(8,128)S(1)} %update_points.1), channel_id=1, source_target_pairs={{0,1},{1,0},{2,3},{3,2},{4,5},{5,4},{6,7},{7,6},{8,9},{9,8},{10,11... | collective-permute-start | bytes 589832 | tf_op jit(solution)/shard_map/ppermute | solution.py:667
  65.5 32.2 %collective-permute-start.13 = (f32[2,4,24,512]{3,2,1,0:T(8,128)S(1)}, f32[2,4,24,512]{3,2,1,0:T(8,128)S(1)}, u32[]{:S(2)}, u32[]{:S(2)}) collective-permute-start(f32[2,4,24,512]{3,2,1,0:T(8,128)S(1)} %pad_maximum_fusion.refs_2_), channel_id=1, source_target_pairs={{8,0},{12,4},{16,8},{20,12},{24,16},{28,20},{9,1},{13,5},{17,9},{2... | collective-permute-start | bytes 1179656 | tf_op jit(solution)/shard_map/ppermute | solution.py:645
  67.4 30.3 %collective-permute-start.12 = (f32[2,4,24,512]{3,2,1,0:T(8,128)S(1)}, f32[2,4,24,512]{3,2,1,0:T(8,128)S(1)}, u32[]{:S(2)}, u32[]{:S(2)}) collective-permute-start(f32[2,4,24,512]{3,2,1,0:T(8,128)S(1)} %pad_maximum_fusion.refs_2_), channel_id=1, source_target_pairs={{4,8},{12,16},{20,24},{8,4},{16,12},{24,20},{5,9},{13,17},{21,25},... | collective-permute-start | bytes 1179656 | tf_op jit(solution)/shard_map/ppermute | solution.py:652
  72.8 25.0 %collective-permute-start.11 = (f32[2,4,24,512]{3,2,1,0:T(8,128)S(1)}, f32[2,4,24,512]{3,2,1,0:T(8,128)S(1)}, u32[]{:S(2)}, u32[]{:S(2)}) collective-permute-start(f32[2,4,24,512]{3,2,1,0:T(8,128)S(1)} %pad_maximum_fusion.refs_2_), channel_id=1, source_target_pairs={{0,4},{8,12},{16,20},{24,28},{4,0},{12,8},{20,16},{28,24},{1,5},{9... | collective-permute-start | bytes 1179656 | tf_op jit(solution)/shard_map/ppermute | solution.py:652
  72.8 24.9 %collective-permute-start.10 = (f32[2,4,24,512]{3,2,1,0:T(8,128)S(1)}, f32[2,4,24,512]{3,2,1,0:T(8,128)S(1)}, u32[]{:S(2)}, u32[]{:S(2)}) collective-permute-start(f32[2,4,24,512]{3,2,1,0:T(8,128)S(1)} %pad_maximum_fusion.refs_2_), channel_id=1, source_target_pairs={{0,8},{4,12},{8,16},{12,20},{16,24},{20,28},{1,9},{5,13},{9,17},{1... | collective-permute-start | bytes 1179656 | tf_op jit(solution)/shard_map/ppermute | solution.py:645
  114.8 19.3 %collective-permute-start.17 = (f32[4,80,128]{2,1,0:T(8,128)S(1)}, f32[4,80,128]{2,1,0:T(8,128)S(1)}, u32[]{:S(2)}, u32[]{:S(2)}) collective-permute-start(f32[4,80,128]{2,1,0:T(8,128)S(1)} %get-tuple-element.104), channel_id=1, source_target_pairs={{0,1},{1,0},{2,3},{3,2},{4,5},{5,4},{6,7},{7,6},{8,9},{9,8},{10,11... | collective-permute-start | bytes 491528 | tf_op jit(solution)/shard_map/ppermute | solution.py:667
  116.0 19.5 %collective-permute-start.18 = (f32[4,80,128]{2,1,0:T(8,128)S(1)}, f32[4,80,128]{2,1,0:T(8,128)S(1)}, u32[]{:S(2)}, u32[]{:S(2)}) collective-permute-start(f32[4,80,128]{2,1,0:T(8,128)S(1)} %get-tuple-element.105), channel_id=1, source_target_pairs={{0,2},{1,3},{2,0},{3,1},{4,6},{5,7},{6,4},{7,5},{8,10},{9,11},{10,... | collective-permute-start | bytes 491528 | tf_op jit(solution)/shard_map/ppermute | solution.py:667
  116.5 19.1 %collective-permute-start.19 = (f32[4,80,128]{2,1,0:T(8,128)S(1)}, f32[4,80,128]{2,1,0:T(8,128)S(1)}, u32[]{:S(2)}, u32[]{:S(2)}) collective-permute-start(f32[4,80,128]{2,1,0:T(8,128)S(1)} %get-tuple-element.106), channel_id=1, source_target_pairs={{0,3},{1,2},{2,1},{3,0},{4,7},{5,6},{6,5},{7,4},{8,11},{9,10},{10,... | collective-permute-start | bytes 491528 | tf_op jit(solution)/shard_map/ppermute | solution.py:667
  133.4 3.3 %collective-permute-start.14 = (f32[4,80,128]{2,1,0:T(8,128)S(1)}, f32[4,80,128]{2,1,0:T(8,128)S(1)}, u32[]{:S(2)}, u32[]{:S(2)}) collective-permute-start(f32[4,80,128]{2,1,0:T(8,128)S(1)} %get-tuple-element.100), channel_id=1, source_target_pairs={{0,1},{1,0},{2,3},{3,2},{4,5},{5,4},{6,7},{7,6},{8,9},{9,8},{10,11... | collective-permute-start | bytes 491528 | tf_op jit(solution)/shard_map/ppermute | solution.py:667
  133.6 5.4 %collective-permute-start.15 = (f32[4,80,128]{2,1,0:T(8,128)S(1)}, f32[4,80,128]{2,1,0:T(8,128)S(1)}, u32[]{:S(2)}, u32[]{:S(2)}) collective-permute-start(f32[4,80,128]{2,1,0:T(8,128)S(1)} %get-tuple-element.101), channel_id=1, source_target_pairs={{0,2},{1,3},{2,0},{3,1},{4,6},{5,7},{6,4},{7,5},{8,10},{9,11},{10,... | collective-permute-start | bytes 491528 | tf_op jit(solution)/shard_map/ppermute | solution.py:667
  134.1 9.0 %collective-permute-start.16 = (f32[4,80,128]{2,1,0:T(8,128)S(1)}, f32[4,80,128]{2,1,0:T(8,128)S(1)}, u32[]{:S(2)}, u32[]{:S(2)}) collective-permute-start(f32[4,80,128]{2,1,0:T(8,128)S(1)} %get-tuple-element.102), channel_id=1, source_target_pairs={{0,3},{1,2},{2,1},{3,0},{4,7},{5,6},{6,5},{7,4},{8,11},{9,10},{10,... | collective-permute-start | bytes 491528 | tf_op jit(solution)/shard_map/ppermute | solution.py:667
  (2 other events, 2.2 us)

commit v3 on v2

--- a/solution.py
+++ b/solution.py
@@ -307,15 +307,18 @@
     priors, (w_ref, s_ref, rc_ref, span_ref) = refs[:window], refs[window:]
     levels, rows, share, row_scale, col_scale = geometry
     halves, groups, _, width = priors[0].shape
-    piece = width if halves == 1 else min(2 * LANE, width)
-    piece = min(piece, BLOCK)
-    chunk = piece * halves
+    piece = min(width, BLOCK) if halves == 1 else LANE
+    chunk = min(BLOCK, halves * width)
+    lane = lax.broadcasted_iota(jnp.int32, (1, LANE), 1)
     counts = [ref[0, 0, share + 3 : share + 4, 0:LANE] for ref in priors]
 
     totals = [number(row, 0) for row in counts]
     for p in range(rows):
         span_ref[p] = number(counts[0], p + 1) // LANE * LANE
         span_ref[rows + p] = number(counts[-1], p) if p else jnp.int32(0)
+    w_ref[:, :, 0:LANE] = jnp.zeros((levels, DEEP, LANE), BF16)
+    s_ref[0:LANE, :] = jnp.zeros((LANE, 2 * LANE), BF16)
+    rc_ref[:, 0:LANE] = jnp.zeros((8, LANE), F32)
     off = jnp.int32(0)
     starts = []
     for t, ref in enumerate(priors):
@@ -324,40 +327,77 @@
 
         def body(k, _, ref=ref, off=off, count=count):
             src = k * chunk
-            at = pl.multiple_of(k * piece, piece)
+            each = chunk // (piece * halves)
             half = [(h ^ id_ref[1]) & (halves - 1) for h in range(halves)]
 
             def taken(g, begin, size):
                 return jnp.concatenate(
-                    [ref[h, g, begin : begin + size, pl.ds(at, piece)] for h in half], axis=1
+                    [
+                        ref[h, g, begin : begin + size, pl.ds(pl.multiple_of((k * each + n) * piece, piece), piece)]
+                        for n in range(each)
+                        for h in half
+                    ],
+                    axis=1,
                 )
 
-            dst = pl.multiple_of(off + src, LANE)
             slot = lax.broadcasted_iota(jnp.int32, (1, chunk), 1) + src
             live = (slot < count).astype(F32)
             prior = jnp.concatenate(
                 [taken(id_ref[1] ^ g, 0, share) for g in range(groups)], axis=0
             )
-            place = taken(0, share, SPARE)
+            place = taken(0, share, SPARE) * live
             seen = taken(1, share, SPARE)
             members = prior.shape[0]
             weight, shift = weigh(prior, seen[0:1], seen[1:2], live)
-            pad = jnp.zeros((DEEP - 3 * members, chunk), BF16)
+            table = jnp.concatenate(
+                [
+                    weight,
+                    shift,
+                    place[0:1] * row_scale,
+                    place[1:2] * col_scale,
+                    place[2:3],
+                    jnp.zeros((5, chunk), F32),
+                ],
+                axis=0,
+            )
+            filled = off & (LANE - 1)
+            dst = pl.multiple_of(off - filled + src, LANE)
+            turned = [
+                pltpu.roll(table[:, n : n + LANE], filled, 1) for n in range(0, chunk, LANE)
+            ]
+            none = jnp.zeros_like(turned[0])
+            table = jnp.concatenate(
+                [jnp.where(lane < filled, a, b) for a, b in zip([none] + turned, turned + [none])],
+                axis=1,
+            )
+            first, rest = pl.ds(dst, LANE), pl.ds(pl.multiple_of(dst + LANE, LANE), chunk)
+            weight, shift = table[0:members], table[members : 2 * members]
+            level = table[2 * members + 2 : 2 * members + 3]
+            pad = jnp.zeros((DEEP - 3 * members, chunk + LANE), BF16)
+            high, low = split(weight)
+            stacked = jnp.concatenate([high, low, high, pad], axis=0)
             for l in range(levels):
-                high, low = split(weight * (1.0 / (1.0 + jnp.abs(place[2:3] - float(l)))))
-                w_ref[l, :, pl.ds(dst, chunk)] = jnp.concatenate([high, low, high, pad], axis=0)
-            turned = jnp.concatenate([shift, jnp.zeros((LANE - members, chunk), F32)], axis=0).T
-            high, low = split(turned)
-            s_ref[pl.ds(dst, chunk), 0:LANE] = high
-            s_ref[pl.ds(dst, chunk), LANE : 2 * LANE] = low
-            rc_ref[0:1, pl.ds(dst, chunk)] = place[0:1] * row_scale
-            rc_ref[1:2, pl.ds(dst, chunk)] = place[1:2] * col_scale
-            rc_ref[2:3, pl.ds(dst, chunk)] = place[2:3]
+                factor = 1.0 / (1.0 + jnp.abs(level - float(l)))
+                if levels <= 2:
+                    stack = stacked * factor.astype(BF16)
+                else:
+                    high, low = split(weight * factor)
+                    stack = jnp.concatenate([high, low, high, pad], axis=0)
+                w_ref[l, :, first] += stack[:, 0:LANE]
+                w_ref[l, :, rest] = stack[:, LANE:]
+            pad = jnp.zeros((LANE - members, chunk + LANE), F32)
+            high, low = split(jnp.concatenate([shift, pad], axis=0).T)
+            s_ref[first, 0:LANE] += high[0:LANE]
+            s_ref[rest, 0:LANE] = high[LANE:]
+            s_ref[first, LANE : 2 * LANE] += low[0:LANE]
+            s_ref[rest, LANE : 2 * LANE] = low[LANE:]
+            rc_ref[:, first] += table[2 * members :, 0:LANE]
+            rc_ref[:, rest] = table[2 * members :, LANE:]
             return 0
 
         lax.fori_loop(0, (count + chunk - 1) // chunk, body, 0)
-        off = off + (count + LANE - 1) // LANE * LANE
-    dst = pl.multiple_of(off, LANE)
+        off = off + count
+    dst = pl.multiple_of((off + LANE - 1) // LANE * LANE, LANE)
     for l in range(levels):
         w_ref[l, :, pl.ds(dst, 2 * BLOCK)] = jnp.zeros((DEEP, 2 * BLOCK), BF16)
     s_ref[pl.ds(dst, 2 * BLOCK), :] = jnp.zeros((2 * BLOCK, 2 * LANE), BF16)
@@ -370,7 +410,7 @@
 def pack(geometry, ids, priors):
     levels, rows = geometry[:2]
     halves, _, _, width = priors[0].shape
-    room = len(priors) * halves * width + 2 * BLOCK + LANE
+    room = len(priors) * halves * width + 2 * BLOCK + 2 * LANE
     return pl.pallas_call(
         functools.partial(pack_kernel, geometry, len(priors)),
         out_shape=[
@@ -399,68 +439,77 @@
 ):
     levels, rows, share, row_scale, col_scale = geometry
     groups, _, width = out_ref.shape
-    chunk = min(2 * LANE, width)
     off = span_ref[2 * rows]
     counts = att_ref[5:6, 0:LANE]
     live = number(counts, 0)
-    for c in range(width // chunk):
-        lanes = slice(c * chunk, (c + 1) * chunk)
-        begin = (2 * c + (id_ref[1] & 1)) * chunk
-        at = pl.multiple_of(begin, chunk)
-        att = att_ref[:, pl.ds(at, chunk)]
+    core = id_ref[1] & 1
+    pieces = jnp.maximum((live + LANE - 1) // LANE + 1 - core, 0) // 2
+
+    def lanes(ref, n, count, *index):
+        return jnp.concatenate(
+            [
+                ref[(*index, pl.ds(pl.multiple_of((2 * (n + j) + core) * LANE, LANE), LANE))]
+                for j in range(count)
+            ],
+            axis=-1,
+        )
+
+    for n in range(width // LANE):
+        att = lanes(att_ref, n, 1, slice(None))
         for g in range(groups):
 
-            def put(rows, g=g):
-                out_ref[g, share : share + SPARE, lanes] = rows
-
-            rest = jnp.zeros((1, chunk - LANE), F32)
-            head = jnp.concatenate([counts, rest], axis=1) if chunk > LANE else counts
-            fill_spare(put, jnp.concatenate([att[0:5], head, att[6:8]], axis=0), g % 2 == 1)
-
-        @pl.when(begin >= live)
-        def _():
-            for g in range(groups):
-                out_ref[g, 0:share, lanes] = jnp.zeros((share, chunk), F32)
-
-        @pl.when(begin < live)
-        def _():
-            x = jnp.concatenate(
-                [seen_ref[id_ref[1] ^ g, 0:share, pl.ds(at, chunk)] for g in range(groups)],
-                axis=0,
-            )
-            cells = triple(x)
-            place = jnp.concatenate([att, jnp.zeros((LANE - 8, chunk), F32)], axis=0).T
-            cell_row = place[:, 0:1] * row_scale
-            cell_col = place[:, 1:2] * col_scale
-            cell_lev = place[:, 2:3]
-            acc_ref[...] = jnp.zeros(acc_ref.shape, F32)
-
-            def body(b, _):
-                at = pl.multiple_of(b * BLOCK, BLOCK)
-                row_gap = cell_row - rc_ref[0:1, pl.ds(at, BLOCK)]
-                col_gap = cell_col - rc_ref[1:2, pl.ds(at, BLOCK)]
-                near = jnp.maximum(1.0 - row_gap * row_gap - col_gap * col_gap, 0.0)
-                level = rc_ref[2:3, pl.ds(at, BLOCK)]
-                ratio = jnp.ones((chunk, BLOCK), F32)
-                for l in range(1, levels):
-                    other = (1.0 + level) / (1.0 + jnp.abs(level - float(l)))
-                    ratio = jnp.where(cell_lev == float(l), other, ratio)
-                cov = jnp.dot(cells, w_ref[0, :, pl.ds(at, BLOCK)], preferred_element_type=F32)
-                high, low = split(cov * (near * near) * ratio)
-                s = s_ref[pl.ds(at, BLOCK), :]
-                acc_ref[...] += jnp.dot(high, s, preferred_element_type=F32)
-                acc_ref[:, 0:LANE] += jnp.dot(low, s[:, 0:LANE], preferred_element_type=F32)
-                return 0
-
-            def pair(b, _):
-                body(2 * b, 0)
-                body(2 * b + 1, 0)
-                return 0
-
-            lax.fori_loop(0, (off + 2 * BLOCK - 1) // (2 * BLOCK), pair, 0)
-            out = x + (acc_ref[:, 0:LANE] + acc_ref[:, LANE : 2 * LANE]).T[0 : groups * share]
-            for g in range(groups):
-                out_ref[id_ref[1] ^ g, 0:share, lanes] = out[g * share : (g + 1) * share]
+            def put(value, g=g):
+                out_ref[g, share : share + SPARE, n * LANE : (n + 1) * LANE] = value
+
+            fill_spare(put, jnp.concatenate([att[0:5], counts, att[6:8]], axis=0), g % 2 == 1)
+            out_ref[g, 0:share, n * LANE : (n + 1) * LANE] = jnp.zeros((share, LANE), F32)
+
+    def update(n, count):
+        size = count * LANE
+        att = lanes(att_ref, n, count, slice(None))
+        x = jnp.concatenate(
+            [lanes(seen_ref, n, count, id_ref[1] ^ g, slice(0, share)) for g in range(groups)],
+            axis=0,
+        )
+        cells = triple(x)
+        place = jnp.concatenate([att, jnp.zeros((LANE - 8, size), F32)], axis=0).T
+        cell_row = place[:, 0:1] * row_scale
+        cell_col = place[:, 1:2] * col_scale
+        cell_lev = place[:, 2:3]
+        acc_ref[0:size] = jnp.zeros((size, 2 * LANE), F32)
+
+        def body(b):
+            at = pl.multiple_of(b * BLOCK, BLOCK)
+            row_gap = cell_row - rc_ref[0:1, pl.ds(at, BLOCK)]
+            col_gap = cell_col - rc_ref[1:2, pl.ds(at, BLOCK)]
+            near = jnp.maximum(1.0 - row_gap * row_gap - col_gap * col_gap, 0.0)
+            level = rc_ref[2:3, pl.ds(at, BLOCK)]
+            ratio = jnp.ones((size, BLOCK), F32)
+            for l in range(1, levels):
+                other = (1.0 + level) / (1.0 + jnp.abs(level - float(l)))
+                ratio = jnp.where(cell_lev == float(l), other, ratio)
+            cov = jnp.dot(cells, w_ref[0, :, pl.ds(at, BLOCK)], preferred_element_type=F32)
+            high, low = split(cov * (near * near) * ratio)
+            s = s_ref[pl.ds(at, BLOCK), :]
+            acc_ref[0:size] += jnp.dot(high, s, preferred_element_type=F32)
+            acc_ref[0:size, 0:LANE] += jnp.dot(low, s[:, 0:LANE], preferred_element_type=F32)
+
+        def pair(b, _):
+            body(2 * b)
+            body(2 * b + 1)
+            return 0
+
+        lax.fori_loop(0, (off + 2 * BLOCK - 1) // (2 * BLOCK), pair, 0)
+        out = x + (acc_ref[0:size, 0:LANE] + acc_ref[0:size, LANE : 2 * LANE]).T[0 : groups * share]
+        for g in range(groups):
+            out_ref[id_ref[1] ^ g, 0:share, n * LANE : n * LANE + size] = out[
+                g * share : (g + 1) * share
+            ]
+
+    for n in range(0, width // LANE, 2):
+        if n + 2 <= width // LANE:
+            pl.when(pieces >= n + 2)(functools.partial(update, n, 2))
+        pl.when(pieces == n + 1)(functools.partial(update, n, 1))
 
 
 def update_points(geometry, ids, att, seen, packed):
@@ -471,7 +520,7 @@
         out_shape=jax.ShapeDtypeStruct((groups, padded, slots // 2), F32),
         in_specs=[SMEM] * 2 + [VMEM] * 5,
         out_specs=VMEM,
-        scratch_shapes=[pltpu.VMEM((min(2 * LANE, slots // 2), 2 * LANE), F32)],
+        scratch_shapes=[pltpu.VMEM((2 * LANE, 2 * LANE), F32)],
         compiler_params=PARAMS,
         cost_estimate=cost(8),
         name="update_points",
@@ -508,7 +557,9 @@
         for p in range(rows):
             xt_ref[l * rows + p] = triple(cells(l * all_rows + begin + p))
 
-    steps = [jnp.maximum(last[p] - first[p] + BLOCK - 1, 0) // BLOCK for p in range(rows)]
+    half = BLOCK // 2
+    spans = [jnp.maximum(last[p] - first[p], 0) for p in range(rows)]
+    steps = [(n + half - 1) // BLOCK for n in spans]
     ends = [steps[0]]
     for n in steps[1:]:
         ends.append(ends[-1] + n)
@@ -523,42 +574,73 @@
             at = jnp.where(past, first[j] + (i - ends[j - 1]) * BLOCK, at)
         return p, pl.multiple_of(at, LANE)
 
+    def tapered(p, at, width):
+        row_gap = (id_ref[0] * all_rows + begin + p).astype(F32) * row_scale - rc_ref[
+            0:1, pl.ds(at, width)
+        ]
+        base = 1.0 - row_gap * row_gap
+        q = q_ref[...]
+        col_gap = jnp.concatenate([q] * (width // LANE), axis=1) - rc_ref[1:2, pl.ds(at, width)]
+        near = jnp.maximum(base - col_gap * col_gap, 0.0)
+        return near * near
+
+    def gains(p, l, at, width, taper):
+        w = w_ref[l, :, pl.ds(at, width)]
+        return split(jnp.dot(xt_ref[l * rows + p], w, preferred_element_type=F32) * taper)
+
+    def add(p, l, at, high, low):
+        s = s_ref[pl.ds(at, high.shape[1]), :]
+        acc_ref[p, l] += jnp.dot(high, s, preferred_element_type=F32)
+        acc_ref[p, l, :, 0:LANE] += jnp.dot(low, s[:, 0:LANE], preferred_element_type=F32)
+
     def spread(i, l):
         p, at = locate(i)
-        s = s_ref[pl.ds(at, BLOCK), :]
-        acc_ref[p, l] += jnp.dot(high_ref[l], s, preferred_element_type=F32)
-        acc_ref[p, l, :, 0:LANE] += jnp.dot(low_ref[l], s[:, 0:LANE], preferred_element_type=F32)
-
-    def step(i, _):
+        add(p, l, at, high_ref[l], low_ref[l])
+
+    def step(i):
         p, at = locate(i)
-        row_gap = (id_ref[0] * all_rows + begin + p).astype(F32) * row_scale - rc_ref[0:1, pl.ds(at, BLOCK)]
-        base = 1.0 - row_gap * row_gap
-        q = q_ref[...]
-        col_gap = jnp.concatenate([q] * (BLOCK // LANE), axis=1) - rc_ref[1:2, pl.ds(at, BLOCK)]
-        near = jnp.maximum(base - col_gap * col_gap, 0.0)
-        taper = near * near
+        taper = tapered(p, at, BLOCK)
         for l in range(levels):
-            cov = jnp.dot(
-                xt_ref[l * rows + p], w_ref[l, :, pl.ds(at, BLOCK)], preferred_element_type=F32
-            )
-            high, low = split(cov * taper)
+            high, low = gains(p, l, at, BLOCK, taper)
             if l == 0:
                 spread(jnp.maximum(i - 1, 0), levels - 1)
             else:
                 spread(i, l - 1)
             high_ref[l], low_ref[l] = high, low
+
+    def several(i, _):
+        for n in range(4):
+            step(4 * i + n)
+        return 0
+
+    def single(i, _):
+        step(i)
         return 0
 
     high_ref[levels - 1] = jnp.zeros(high_ref.shape[1:], BF16)
     low_ref[levels - 1] = jnp.zeros(low_ref.shape[1:], BF16)
-    def pair(i, _):
-        step(2 * i, 0)
-        step(2 * i + 1, 0)
+    lax.fori_loop(0, ends[-1] // 4, several, 0)
+    lax.fori_loop(ends[-1] // 4 * 4, ends[-1], single, 0)
+    spread(jnp.maximum(ends[-1] - 1, 0), levels - 1)
+
+    def remainder(p, _):
+        def of(values):
+            chosen = values[0]
+            for j in range(1, rows):
+                chosen = jnp.where(p == j, values[j], chosen)
+            return chosen
+
+        at = pl.multiple_of(of([first[j] + steps[j] * BLOCK for j in range(rows)]), LANE)
+
+        @pl.when(of(spans) > of(steps) * BLOCK)
+        def _():
+            taper = tapered(p, at, half)
+            for l in range(levels):
+                add(p, l, at, *gains(p, l, at, half, taper))
+
         return 0
 
-    pairs = (ends[-1] + 1) // 2
-    lax.fori_loop(0, pairs, pair, 0)
-    spread(jnp.maximum(2 * pairs - 1, 0), levels - 1)
+    lax.fori_loop(0, rows, remainder, 0)
 
     def store(p, _):
         for l in range(levels):

time: 147 us -> 139 us (0.946)
  the two profiles are of different devices: /device:TPU:19 before, /device:TPU:9 now
where the time goes in v3:
time: 139 us; the launch traced here: 136 us
  Pallas kernels  64.3 us (46%)
  starting transfers between devices  38.9 us (28%)
  blocking collectives  16.4 us (12%)
  waiting for transfers between devices  9.89 us (7%)
  local copies, waits for them, and re-layouts  6.55 us (5%)
    pallas_call x3, Pallas kernels, update_grid(): pl.pallas_call(functools.partial(grid_kernel, geometry, begin, groups), o...  38.9 us
    ppermute x6, starting transfers between devices, shifted(): return lax.ppermute(value, 'tile', pairs)  16.6 us
    ppermute x4, starting transfers between devices, paired(): return lax.ppermute(value, 'tile', pairs)  13 us
    all_gather x1, blocking collectives, on_device(): ahead = lax.all_gather(ahead, 'ens', axis=0)  9.56 us
    ppermute x10, starting transfers between devices, crossed(): return lax.ppermute(value, 'ens', [(i, i ^ step) for i in range(count)])  9.36 us
    pallas_call x2, Pallas kernels, pack(): pl.pallas_call(functools.partial(pack_kernel, geometry, len(priors)), out...  7.96 us
    ppermute x10, waiting for transfers between devices, crossed(): return lax.ppermute(value, 'ens', [(i, i ^ step) for i in range(count)])  7.4 us
    all_gather x1, blocking collectives, on_device(): seen = lax.all_gather(seen, 'ens', axis=0)  6.82 us
  transfers between devices with their start and end apart: 20, of which 5 were waited for; matrix products, arithmetic and copies ran while one was open for 2% of the time, Pallas kernels for 27%

profile of v3, /device:TPU:9, one launch (start us, length us, event | category | flops | bytes accessed | tf_op | source)
XLA Modules:
  0.0 136.4 jit_solution(8952654200798589282)
XLA Ops:
  1.8 3.1 %collective-permute-start = (f32[20,2,2048]{2,1,0:T(2,128)S(1)}, f32[20,2,2048]{2,1,0:T(2,128)S(1)}, u32[]{:S(2)}, u32[]{:S(2)}) collective-permute-start(f32[20,2,2048]{2,1,0:T(2,128)S(1)} %bitcast.24), channel_id=1, source_target_pairs={{0,4},{4,8},{8,12},{12,16},{16,20},{20,24},{24,28},{1,5},{5,9},{9,... | collective-permute-start | bytes 983048 | tf_op jit(solution)/shard_map/ppermute | solution.py:727
  6.7 3.1 %collective-permute-start.1 = (f32[20,2,2048]{2,1,0:T(2,128)S(1)}, f32[20,2,2048]{2,1,0:T(2,128)S(1)}, u32[]{:S(2)}, u32[]{:S(2)}) collective-permute-start(f32[20,2,2048]{2,1,0:T(2,128)S(1)} %bitcast.25), channel_id=1, source_target_pairs={{4,0},{8,4},{12,8},{16,12},{20,16},{24,20},{28,24},{5,1},{9,5},{13... | collective-permute-start | bytes 983048 | tf_op jit(solution)/shard_map/ppermute | solution.py:727
  12.8 3.1 %forecast.1 = (f32[4,160,128]{2,1,0:T(8,128)S(1)}, f32[4,160,128]{2,1,0:T(8,128)S(1)}, f32[4,160,128]{2,1,0:T(8,128)S(1)}, f32[4,160,128]{2,1,0:T(8,128)S(1)}) custom-call(s32[2]{0:T(128)S(1)} %pad_add_fusion.id_ref, f32[20,2,4,2048]{3,2,1,0:T(4,128)S(1)} %copy-done, f32[2,2,4,2048]{3,2,1,0:T(4,128)S(1)} %copy-done.1), custom_call_target="tpu_custom_call" | custom-call | flops 3000000000 | tf_op jit(solution)/shard_map/forecast/pallas_call | solution.py:132
  16.0 2.2 %order.1 = f32[2,8,1024]{2,1,0:T(8,128)S(1)} custom-call(s32[2]{0:T(128)S(1)} %pad_add_fusion.id_ref, s32[3,2,1024]{2,1,0:T(2,128)S(1)} %copy-done.3, f32[2,1024]{1,0:T(2,128)S(1)} %copy-done.4, f32[2,1024]{1,0:T(2,128)S(1)} %copy-done.5, s32[2,1]{1,0:T(2,128)S(1)} %copy.9.count_ref), custom_call_target="tpu_custom_call" | custom-call | flops 2000000000 | tf_op jit(solution)/shard_map/order/pallas_call | solution.py:83
  24.1 6.8 %all-gather = f32[96,1024]{1,0:T(8,128)S(1)} all-gather(f32[24,1024]{1,0:T(8,128)S(1)} %observe.4), channel_id=2, replica_groups=mesh['tile'=8,'ens'=4] {'ens'}, dimensions={0}, use_global_device_ids=true | all-gather | bytes 491520 | tf_op jit(solution)/shard_map/all_gather | solution.py:771
  34.0 1.9 %collective-permute-start.4 = (f32[1,4,24,1024]{3,2,1,0:T(8,128)S(1)}, f32[1,4,24,1024]{3,2,1,0:T(8,128)S(1)}, u32[]{:S(2)}, u32[]{:S(2)}) collective-permute-start(f32[1,4,24,1024]{3,2,1,0:T(8,128)S(1)} %bitcast.18), channel_id=1, source_target_pairs={{4,8},{12,16},{20,24},{8,4},{16,12},{24,20},{5,9},{13,17},{21,25},... | collective-permute-start | bytes 1179656 | tf_op jit(solution)/shard_map/ppermute | solution.py:734
  36.0 2.7 %collective-permute-start.3 = (f32[1,4,24,1024]{3,2,1,0:T(8,128)S(1)}, f32[1,4,24,1024]{3,2,1,0:T(8,128)S(1)}, u32[]{:S(2)}, u32[]{:S(2)}) collective-permute-start(f32[1,4,24,1024]{3,2,1,0:T(8,128)S(1)} %bitcast.19), channel_id=1, source_target_pairs={{0,4},{8,12},{16,20},{24,28},{4,0},{12,8},{20,16},{28,24},{1,5},{9... | collective-permute-start | bytes 1179656 | tf_op jit(solution)/shard_map/ppermute | solution.py:734
  38.6 3.2 %collective-permute-start.2 = (f32[1,4,24,1024]{3,2,1,0:T(8,128)S(1)}, f32[1,4,24,1024]{3,2,1,0:T(8,128)S(1)}, u32[]{:S(2)}, u32[]{:S(2)}) collective-permute-start(f32[1,4,24,1024]{3,2,1,0:T(8,128)S(1)} %bitcast.20), channel_id=1, source_target_pairs={{0,8},{4,12},{8,16},{12,20},{16,24},{20,28},{1,9},{5,13},{9,17},{1... | collective-permute-start | bytes 1179656 | tf_op jit(solution)/shard_map/ppermute | solution.py:727
  41.9 2.2 %collective-permute-start.8 = (f32[4,160,128]{2,1,0:T(8,128)S(1)}, f32[4,160,128]{2,1,0:T(8,128)S(1)}, u32[]{:S(2)}, u32[]{:S(2)}) collective-permute-start(f32[4,160,128]{2,1,0:T(8,128)S(1)} %get-tuple-element.68.refs_3_), channel_id=1, source_target_pairs={{0,3},{1,2},{2,1},{3,0},{4,7},{5,6},{6,5},{7,4},{8,11},{9,10},{10,... | collective-permute-start | bytes 983048 | tf_op jit(solution)/shard_map/ppermute | solution.py:749
  44.0 2.0 %observe.5 = f32[24,1024]{1,0:T(8,128)S(1)} custom-call(s32[2]{0:T(128)S(1)} %pad_add_fusion.id_ref, f32[8,1024]{1,0:T(8,128)S(1)} %get-tuple-element.107.att_ref, f32[4,160,128]{2,1,0:T(8,128)S(1)} %get-tuple-element.83.refs_0_, f32[4,160,128]{2,1,0:T(8,128)S(1)} %get-tuple-element.66.refs_1_, f32[4,160,128]{2,1,0:T(8,128)S(1)} %get-tuple-element.67.refs_2_, ...), custom_call_target="tpu_custom_call" | custom-call | flops 3000000000 | tf_op jit(solution)/shard_map/observe/pallas_call | solution.py:282
  46.0 9.6 %all-gather.1 = f32[96,1024]{1,0:T(8,128)S(1)} all-gather(f32[24,1024]{1,0:T(8,128)S(1)} %observe.5), channel_id=3, replica_groups=mesh['tile'=8,'ens'=4] {'ens'}, dimensions={0}, use_global_device_ids=true | all-gather | bytes 491520 | tf_op jit(solution)/shard_map/all_gather | solution.py:775
  56.3 3.9 %pack.2 = (bf16[2,256,6400]{2,1,0:T(8,128)(2,1)S(1)}, bf16[6400,256]{1,0:T(8,128)(2,1)S(1)}, f32[8,6400]{1,0:T(8,128)S(1)}, s32[9]{0:T(128)S(1)}) custom-call(s32[2]{0:T(128)S(1)} %pad_add_fusion.id_ref, f32[1,4,24,1024]{3,2,1,0:T(8,128)S(1)} %collective-permute-done.2.refs_0_, f32[1,4,24,1024]{3,2,1,0:T(8,128)S(1)} %collective-permute-done.3.refs_1_, ...), custom_call_target="tpu_custom_call" | custom-call | flops 5000000000 | tf_op jit(solution)/shard_map/pack/pallas_call | solution.py:414
  60.2 2.7 %update_points.1 = f32[4,24,512]{2,1,0:T(8,128)S(1)} custom-call(s32[2]{0:T(128)S(1)} %pad_add_fusion.id_ref, s32[9]{0:T(128)S(1)} %get-tuple-element.74.span_ref, f32[8,1024]{1,0:T(8,128)S(1)} %get-tuple-element.107.att_ref, f32[4,24,1024]{2,1,0:T(8,128)S(1)} %bitcast.22, bf16[2,256,6400]{2,1,0:T(8,128)(2,1)S(1)} %get-tuple-element.76.w_ref, ...), custom_call_target="tpu_custom_call" | custom-call | flops 8000000000 | tf_op jit(solution)/shard_map/update_points/pallas_call | solution.py:518
  64.6 1.9 %collective-permute-start.13 = (f32[2,4,24,512]{3,2,1,0:T(8,128)S(1)}, f32[2,4,24,512]{3,2,1,0:T(8,128)S(1)}, u32[]{:S(2)}, u32[]{:S(2)}) collective-permute-start(f32[2,4,24,512]{3,2,1,0:T(8,128)S(1)} %pad_maximum_fusion.refs_2_), channel_id=1, source_target_pairs={{8,0},{12,4},{16,8},{20,12},{24,16},{28,20},{9,1},{13,5},{17,9},{2... | collective-permute-start | bytes 1179656 | tf_op jit(solution)/shard_map/ppermute | solution.py:727
  66.5 4.5 %collective-permute-start.12 = (f32[2,4,24,512]{3,2,1,0:T(8,128)S(1)}, f32[2,4,24,512]{3,2,1,0:T(8,128)S(1)}, u32[]{:S(2)}, u32[]{:S(2)}) collective-permute-start(f32[2,4,24,512]{3,2,1,0:T(8,128)S(1)} %pad_maximum_fusion.refs_2_), channel_id=1, source_target_pairs={{4,8},{12,16},{20,24},{8,4},{16,12},{24,20},{5,9},{13,17},{21,25},... | collective-permute-start | bytes 1179656 | tf_op jit(solution)/shard_map/ppermute | solution.py:734
  71.0 3.9 %collective-permute-start.11 = (f32[2,4,24,512]{3,2,1,0:T(8,128)S(1)}, f32[2,4,24,512]{3,2,1,0:T(8,128)S(1)}, u32[]{:S(2)}, u32[]{:S(2)}) collective-permute-start(f32[2,4,24,512]{3,2,1,0:T(8,128)S(1)} %pad_maximum_fusion.refs_2_), channel_id=1, source_target_pairs={{0,4},{8,12},{16,20},{24,28},{4,0},{12,8},{20,16},{28,24},{1,5},{9... | collective-permute-start | bytes 1179656 | tf_op jit(solution)/shard_map/ppermute | solution.py:734
  74.8 3.4 %collective-permute-start.10 = (f32[2,4,24,512]{3,2,1,0:T(8,128)S(1)}, f32[2,4,24,512]{3,2,1,0:T(8,128)S(1)}, u32[]{:S(2)}, u32[]{:S(2)}) collective-permute-start(f32[2,4,24,512]{3,2,1,0:T(8,128)S(1)} %pad_maximum_fusion.refs_2_), channel_id=1, source_target_pairs={{0,8},{4,12},{8,16},{12,20},{16,24},{20,28},{1,9},{5,13},{9,17},{1... | collective-permute-start | bytes 1179656 | tf_op jit(solution)/shard_map/ppermute | solution.py:727
  78.2 16.6 %update_grid.3 = (f32[4,160,128]{2,1,0:T(8,128)S(1)}, f32[4,160,128]{2,1,0:T(8,128)S(1)}, f32[4,160,128]{2,1,0:T(8,128)S(1)}, f32[4,160,128]{2,1,0:T(8,128)S(1)}) custom-call(s32[2]{0:T(128)S(1)} %pad_add_fusion.id_ref, s32[9]{0:T(128)S(1)} %get-tuple-element.74.span_ref, bf16[2,256,6400]{2,1,0:T(8,128)(2,1)S(1)} %get-tuple-element.76.w_ref, ...), custom_call_target="tpu_custom_call" | custom-call | flops 28000000000 | tf_op jit(solution)/shard_map/update_grid/pallas_call | solution.py:668
  94.9 4.0 %pack.3 = (bf16[2,256,6400]{2,1,0:T(8,128)(2,1)S(1)}, bf16[6400,256]{1,0:T(8,128)(2,1)S(1)}, f32[8,6400]{1,0:T(8,128)S(1)}, s32[9]{0:T(128)S(1)}) custom-call(s32[2]{0:T(128)S(1)} %pad_add_fusion.id_ref, f32[2,4,24,512]{3,2,1,0:T(8,128)S(1)} %collective-permute-done.10.refs_0_, f32[2,4,24,512]{3,2,1,0:T(8,128)S(1)} %collective-permute-done.11.refs_1_, ...), custom_call_target="tpu_custom_call" | custom-call | flops 5000000000 | tf_op jit(solution)/shard_map/pack/pallas_call | solution.py:414
  98.9 11.1 %update_grid.4 = (f32[4,80,128]{2,1,0:T(8,128)S(1)}, f32[4,80,128]{2,1,0:T(8,128)S(1)}, f32[4,80,128]{2,1,0:T(8,128)S(1)}, f32[4,80,128]{2,1,0:T(8,128)S(1)}) custom-call(s32[2]{0:T(128)S(1)} %pad_add_fusion.id_ref, s32[9]{0:T(128)S(1)} %get-tuple-element.79.span_ref, bf16[2,256,6400]{2,1,0:T(8,128)(2,1)S(1)} %get-tuple-element.80.w_ref, ...), custom_call_target="tpu_custom_call" | custom-call | flops 14000000000 | tf_op jit(solution)/shard_map/update_grid/pallas_call | solution.py:668
  113.3 11.2 %update_grid.5 = (f32[4,80,128]{2,1,0:T(8,128)S(1)}, f32[4,80,128]{2,1,0:T(8,128)S(1)}, f32[4,80,128]{2,1,0:T(8,128)S(1)}, f32[4,80,128]{2,1,0:T(8,128)S(1)}) custom-call(s32[2]{0:T(128)S(1)} %pad_add_fusion.id_ref, s32[9]{0:T(128)S(1)} %get-tuple-element.79.span_ref, bf16[2,256,6400]{2,1,0:T(8,128)(2,1)S(1)} %get-tuple-element.80.w_ref, ...), custom_call_target="tpu_custom_call" | custom-call | flops 14000000000 | tf_op jit(solution)/shard_map/update_grid/pallas_call | solution.py:668
  127.9 2.3 %collective-permute-done.15.refs_2_ = f32[4,80,128]{2,1,0:T(8,128)S(1)} collective-permute-done((f32[4,80,128]{2,1,0:T(8,128)S(1)}, f32[4,80,128]{2,1,0:T(8,128)S(1)}, u32[]{:S(2)}, u32[]{:S(2)}) %collective-permute-start.15) | collective-permute-done | bytes 163872 | tf_op jit(solution)/shard_map/ppermute | solution.py:749
  130.2 4.0 %collective-permute-done.16.refs_3_ = f32[4,80,128]{2,1,0:T(8,128)S(1)} collective-permute-done((f32[4,80,128]{2,1,0:T(8,128)S(1)}, f32[4,80,128]{2,1,0:T(8,128)S(1)}, u32[]{:S(2)}, u32[]{:S(2)}) %collective-permute-start.16) | collective-permute-done | bytes 163872 | tf_op jit(solution)/shard_map/ppermute | solution.py:749
  134.2 2.2 %restore.3 = f32[20,2,4,2048]{3,2,1,0:T(4,128)} custom-call(s32[2]{0:T(128)S(1)} %pad_add_fusion.id_ref, f32[4,80,128]{2,1,0:T(8,128)S(1)} %get-tuple-element.99.refs_0_, f32[4,80,128]{2,1,0:T(8,128)S(1)} %collective-permute-done.14.refs_1_, f32[4,80,128]{2,1,0:T(8,128)S(1)} %collective-permute-done.15.refs_2_, ...), custom_call_target="tpu_custom_call" | custom-call | flops 2000000000 | tf_op jit(solution)/shard_map/restore/pallas_call | solution.py:713
  (52 shorter events, 24.5 us)
Async XLA Ops:
  1.8 17.7 %collective-permute-start = (f32[20,2,2048]{2,1,0:T(2,128)S(1)}, f32[20,2,2048]{2,1,0:T(2,128)S(1)}, u32[]{:S(2)}, u32[]{:S(2)}) collective-permute-start(f32[20,2,2048]{2,1,0:T(2,128)S(1)} %bitcast.24), channel_id=1, source_target_pairs={{0,4},{4,8},{8,12},{12,16},{16,20},{20,24},{24,28},{1,5},{5,9},{9,... | collective-permute-start | bytes 983048 | tf_op jit(solution)/shard_map/ppermute | solution.py:727
  6.7 14.6 %collective-permute-start.1 = (f32[20,2,2048]{2,1,0:T(2,128)S(1)}, f32[20,2,2048]{2,1,0:T(2,128)S(1)}, u32[]{:S(2)}, u32[]{:S(2)}) collective-permute-start(f32[20,2,2048]{2,1,0:T(2,128)S(1)} %bitcast.25), channel_id=1, source_target_pairs={{4,0},{8,4},{12,8},{16,12},{20,16},{24,20},{28,24},{5,1},{9,5},{13... | collective-permute-start | bytes 983048 | tf_op jit(solution)/shard_map/ppermute | solution.py:727
  12.8 3.1 %copy-start.3 = (s32[3,2,1024]{2,1,0:T(2,128)S(1)}, s32[3,2,1024]{2,1,0:T(2,128)}, u32[]{:S(2)}) copy-start(s32[3,2,1024]{2,1,0:T(2,128)} %loc_ref.1) | copy-start | bytes 73732
  12.8 3.1 %copy-start.4 = (f32[2,1024]{1,0:T(2,128)S(1)}, f32[2,1024]{1,0:T(2,128)}, u32[]{:S(2)}) copy-start(f32[2,1024]{1,0:T(2,128)} %value_ref.1) | copy-start | bytes 24580
  12.8 3.1 %copy-start.5 = (f32[2,1024]{1,0:T(2,128)S(1)}, f32[2,1024]{1,0:T(2,128)}, u32[]{:S(2)}) copy-start(f32[2,1024]{1,0:T(2,128)} %error_ref.1) | copy-start | bytes 24580
  18.2 3.1 %copy-start.2 = (f32[2,2,4,2048]{3,2,1,0:T(4,128)S(1)}, f32[2,2,4,2048]{3,2,1,0:T(4,128)}, u32[]{:S(2)}) copy-start(f32[2,2,4,2048]{3,2,1,0:T(4,128)} %flow_ref.3) | copy-start | bytes 393220
  30.9 7.7 %collective-permute-start.6 = (f32[4,160,128]{2,1,0:T(8,128)S(1)}, f32[4,160,128]{2,1,0:T(8,128)S(1)}, u32[]{:S(2)}, u32[]{:S(2)}) collective-permute-start(f32[4,160,128]{2,1,0:T(8,128)S(1)} %get-tuple-element.66.refs_1_), channel_id=1, source_target_pairs={{0,1},{1,0},{2,3},{3,2},{4,5},{5,4},{6,7},{7,6},{8,9},{9,8},{10,11... | collective-permute-start | bytes 983048 | tf_op jit(solution)/shard_map/ppermute | solution.py:749
  31.1 10.8 %collective-permute-start.7 = (f32[4,160,128]{2,1,0:T(8,128)S(1)}, f32[4,160,128]{2,1,0:T(8,128)S(1)}, u32[]{:S(2)}, u32[]{:S(2)}) collective-permute-start(f32[4,160,128]{2,1,0:T(8,128)S(1)} %get-tuple-element.67.refs_2_), channel_id=1, source_target_pairs={{0,2},{1,3},{2,0},{3,1},{4,6},{5,7},{6,4},{7,5},{8,10},{9,11},{10,... | collective-permute-start | bytes 983048 | tf_op jit(solution)/shard_map/ppermute | solution.py:749
  32.1 23.5 %collective-permute-start.5 = (f32[1,4,24,1024]{3,2,1,0:T(8,128)S(1)}, f32[1,4,24,1024]{3,2,1,0:T(8,128)S(1)}, u32[]{:S(2)}, u32[]{:S(2)}) collective-permute-start(f32[1,4,24,1024]{3,2,1,0:T(8,128)S(1)} %bitcast.17), channel_id=1, source_target_pairs={{8,0},{12,4},{16,8},{20,12},{24,16},{28,20},{9,1},{13,5},{17,9},{2... | collective-permute-start | bytes 1179656 | tf_op jit(solution)/shard_map/ppermute | solution.py:727
  34.0 21.5 %collective-permute-start.4 = (f32[1,4,24,1024]{3,2,1,0:T(8,128)S(1)}, f32[1,4,24,1024]{3,2,1,0:T(8,128)S(1)}, u32[]{:S(2)}, u32[]{:S(2)}) collective-permute-start(f32[1,4,24,1024]{3,2,1,0:T(8,128)S(1)} %bitcast.18), channel_id=1, source_target_pairs={{4,8},{12,16},{20,24},{8,4},{16,12},{24,20},{5,9},{13,17},{21,25},... | collective-permute-start | bytes 1179656 | tf_op jit(solution)/shard_map/ppermute | solution.py:734
  36.0 20.3 %collective-permute-start.3 = (f32[1,4,24,1024]{3,2,1,0:T(8,128)S(1)}, f32[1,4,24,1024]{3,2,1,0:T(8,128)S(1)}, u32[]{:S(2)}, u32[]{:S(2)}) collective-permute-start(f32[1,4,24,1024]{3,2,1,0:T(8,128)S(1)} %bitcast.19), channel_id=1, source_target_pairs={{0,4},{8,12},{16,20},{24,28},{4,0},{12,8},{20,16},{28,24},{1,5},{9... | collective-permute-start | bytes 1179656 | tf_op jit(solution)/shard_map/ppermute | solution.py:734
  38.6 17.6 %collective-permute-start.2 = (f32[1,4,24,1024]{3,2,1,0:T(8,128)S(1)}, f32[1,4,24,1024]{3,2,1,0:T(8,128)S(1)}, u32[]{:S(2)}, u32[]{:S(2)}) collective-permute-start(f32[1,4,24,1024]{3,2,1,0:T(8,128)S(1)} %bitcast.20), channel_id=1, source_target_pairs={{0,8},{4,12},{8,16},{12,20},{16,24},{20,28},{1,9},{5,13},{9,17},{1... | collective-permute-start | bytes 1179656 | tf_op jit(solution)/shard_map/ppermute | solution.py:727
  41.9 13.7 %collective-permute-start.8 = (f32[4,160,128]{2,1,0:T(8,128)S(1)}, f32[4,160,128]{2,1,0:T(8,128)S(1)}, u32[]{:S(2)}, u32[]{:S(2)}) collective-permute-start(f32[4,160,128]{2,1,0:T(8,128)S(1)} %get-tuple-element.68.refs_3_), channel_id=1, source_target_pairs={{0,3},{1,2},{2,1},{3,0},{4,7},{5,6},{6,5},{7,4},{8,11},{9,10},{10,... | collective-permute-start | bytes 983048 | tf_op jit(solution)/shard_map/ppermute | solution.py:749
  62.9 1.6 %collective-permute-start.9 = (f32[4,24,512]{2,1,0:T(8,128)S(1)}, f32[4,24,512]{2,1,0:T(8,128)S(1)}, u32[]{:S(2)}, u32[]{:S(2)}) collective-permute-start(f32[4,24,512]{2,1,0:T(8,128)S(1)} %update_points.1), channel_id=1, source_target_pairs={{0,1},{1,0},{2,3},{3,2},{4,5},{5,4},{6,7},{7,6},{8,9},{9,8},{10,11... | collective-permute-start | bytes 589832 | tf_op jit(solution)/shard_map/ppermute | solution.py:749
  64.6 30.3 %collective-permute-start.13 = (f32[2,4,24,512]{3,2,1,0:T(8,128)S(1)}, f32[2,4,24,512]{3,2,1,0:T(8,128)S(1)}, u32[]{:S(2)}, u32[]{:S(2)}) collective-permute-start(f32[2,4,24,512]{3,2,1,0:T(8,128)S(1)} %pad_maximum_fusion.refs_2_), channel_id=1, source_target_pairs={{8,0},{12,4},{16,8},{20,12},{24,16},{28,20},{9,1},{13,5},{17,9},{2... | collective-permute-start | bytes 1179656 | tf_op jit(solution)/shard_map/ppermute | solution.py:727
  66.5 28.4 %collective-permute-start.12 = (f32[2,4,24,512]{3,2,1,0:T(8,128)S(1)}, f32[2,4,24,512]{3,2,1,0:T(8,128)S(1)}, u32[]{:S(2)}, u32[]{:S(2)}) collective-permute-start(f32[2,4,24,512]{3,2,1,0:T(8,128)S(1)} %pad_maximum_fusion.refs_2_), channel_id=1, source_target_pairs={{4,8},{12,16},{20,24},{8,4},{16,12},{24,20},{5,9},{13,17},{21,25},... | collective-permute-start | bytes 1179656 | tf_op jit(solution)/shard_map/ppermute | solution.py:734
  71.0 23.9 %collective-permute-start.11 = (f32[2,4,24,512]{3,2,1,0:T(8,128)S(1)}, f32[2,4,24,512]{3,2,1,0:T(8,128)S(1)}, u32[]{:S(2)}, u32[]{:S(2)}) collective-permute-start(f32[2,4,24,512]{3,2,1,0:T(8,128)S(1)} %pad_maximum_fusion.refs_2_), channel_id=1, source_target_pairs={{0,4},{8,12},{16,20},{24,28},{4,0},{12,8},{20,16},{28,24},{1,5},{9... | collective-permute-start | bytes 1179656 | tf_op jit(solution)/shard_map/ppermute | solution.py:734
  74.8 20.0 %collective-permute-start.10 = (f32[2,4,24,512]{3,2,1,0:T(8,128)S(1)}, f32[2,4,24,512]{3,2,1,0:T(8,128)S(1)}, u32[]{:S(2)}, u32[]{:S(2)}) collective-permute-start(f32[2,4,24,512]{3,2,1,0:T(8,128)S(1)} %pad_maximum_fusion.refs_2_), channel_id=1, source_target_pairs={{0,8},{4,12},{8,16},{12,20},{16,24},{20,28},{1,9},{5,13},{9,17},{1... | collective-permute-start | bytes 1179656 | tf_op jit(solution)/shard_map/ppermute | solution.py:727
  110.1 15.1 %collective-permute-start.17 = (f32[4,80,128]{2,1,0:T(8,128)S(1)}, f32[4,80,128]{2,1,0:T(8,128)S(1)}, u32[]{:S(2)}, u32[]{:S(2)}) collective-permute-start(f32[4,80,128]{2,1,0:T(8,128)S(1)} %get-tuple-element.104), channel_id=1, source_target_pairs={{0,1},{1,0},{2,3},{3,2},{4,5},{5,4},{6,7},{7,6},{8,9},{9,8},{10,11... | collective-permute-start | bytes 491528 | tf_op jit(solution)/shard_map/ppermute | solution.py:749
  111.6 15.1 %collective-permute-start.18 = (f32[4,80,128]{2,1,0:T(8,128)S(1)}, f32[4,80,128]{2,1,0:T(8,128)S(1)}, u32[]{:S(2)}, u32[]{:S(2)}) collective-permute-start(f32[4,80,128]{2,1,0:T(8,128)S(1)} %get-tuple-element.105), channel_id=1, source_target_pairs={{0,2},{1,3},{2,0},{3,1},{4,6},{5,7},{6,4},{7,5},{8,10},{9,11},{10,... | collective-permute-start | bytes 491528 | tf_op jit(solution)/shard_map/ppermute | solution.py:749
  112.1 14.6 %collective-permute-start.19 = (f32[4,80,128]{2,1,0:T(8,128)S(1)}, f32[4,80,128]{2,1,0:T(8,128)S(1)}, u32[]{:S(2)}, u32[]{:S(2)}) collective-permute-start(f32[4,80,128]{2,1,0:T(8,128)S(1)} %get-tuple-element.106), channel_id=1, source_target_pairs={{0,3},{1,2},{2,1},{3,0},{4,7},{5,6},{6,5},{7,4},{8,11},{9,10},{10,... | collective-permute-start | bytes 491528 | tf_op jit(solution)/shard_map/ppermute | solution.py:749
  124.5 3.3 %collective-permute-start.14 = (f32[4,80,128]{2,1,0:T(8,128)S(1)}, f32[4,80,128]{2,1,0:T(8,128)S(1)}, u32[]{:S(2)}, u32[]{:S(2)}) collective-permute-start(f32[4,80,128]{2,1,0:T(8,128)S(1)} %get-tuple-element.100), channel_id=1, source_target_pairs={{0,1},{1,0},{2,3},{3,2},{4,5},{5,4},{6,7},{7,6},{8,9},{9,8},{10,11... | collective-permute-start | bytes 491528 | tf_op jit(solution)/shard_map/ppermute | solution.py:749
  124.7 5.4 %collective-permute-start.15 = (f32[4,80,128]{2,1,0:T(8,128)S(1)}, f32[4,80,128]{2,1,0:T(8,128)S(1)}, u32[]{:S(2)}, u32[]{:S(2)}) collective-permute-start(f32[4,80,128]{2,1,0:T(8,128)S(1)} %get-tuple-element.101), channel_id=1, source_target_pairs={{0,2},{1,3},{2,0},{3,1},{4,6},{5,7},{6,4},{7,5},{8,10},{9,11},{10,... | collective-permute-start | bytes 491528 | tf_op jit(solution)/shard_map/ppermute | solution.py:749
  125.2 9.0 %collective-permute-start.16 = (f32[4,80,128]{2,1,0:T(8,128)S(1)}, f32[4,80,128]{2,1,0:T(8,128)S(1)}, u32[]{:S(2)}, u32[]{:S(2)}) collective-permute-start(f32[4,80,128]{2,1,0:T(8,128)S(1)} %get-tuple-element.102), channel_id=1, source_target_pairs={{0,3},{1,2},{2,1},{3,0},{4,7},{5,6},{6,5},{7,4},{8,11},{9,10},{10,... | collective-permute-start | bytes 491528 | tf_op jit(solution)/shard_map/ppermute | solution.py:749
  (2 other events, 2.2 us)
